TPU v7x, 32 devices: a whole 2x2x4 slice. The times are simulated.
32 devices in a mesh: dp: 4 (over z), tensor: 8 (over y, x, core).
Axes of the slice: x: 2, y: 2, z: 4, core: 2. Of those that a mesh axis runs over, the one named last changes fastest.
Arguments:
- tokens: bfloat16 [8192, 1024], P(('dp', 'tensor')), may hold values from -6 to 6
- out_grad: bfloat16 [8192, 1024], P(('dp', 'tensor')), may hold values from -6 to 6
- doc_lengths: int32 [32, 4], P(('dp', 'tensor')), may hold values from 0 to 256, as said below
- w_qkv: bfloat16 [1024, 3072], P(('dp', 'tensor')), may hold values from -0.1875 to 0.1875
- w_out: bfloat16 [1024, 1024], P(('dp', 'tensor')), may hold values from -0.1875 to 0.1875
- gains: float32 [1024, 3], P(('dp', 'tensor')), may hold values from 0.25 to 1.75
- biases: float32 [1024, 7], P(('dp', 'tensor')), may hold values from -3 to 3
- head_scale: float32 [16], replicated, may hold values from 0.5 to 2
- w_fc1: bfloat16 [1024, 4096], P('dp', 'tensor'), may hold values from -0.1875 to 0.1875
- w_fc2: bfloat16 [4096, 1024], P('tensor', 'dp'), may hold values from -0.09375 to 0.09375
- mid_gain: float32 [4096], P('tensor'), may hold values from 0.25 to 1.75
- ffn_biases: float32 [2, 4096], P(None, 'tensor'), may hold values from -3 to 3
Outputs:
- mixed_out: bfloat16 [8192, 1024], P(('dp', 'tensor'))
- token_grad: float32 [8192, 1024], P(('dp', 'tensor'))
- qkv_grad: float32 [1024, 3072], P(('dp', 'tensor'))
- out_weight_grad: float32 [1024, 1024], P(('dp', 'tensor'))
- gains_grad: float32 [1024, 3], P(('dp', 'tensor'))
- biases_grad: float32 [1024, 7], P(('dp', 'tensor'))
- scale_grad: float32 [16], replicated
- fc1_grad: float32 [1024, 4096], P('dp', 'tensor')
- fc2_grad: float32 [4096, 1024], P('tensor', 'dp')
- mid_gain_grad: float32 [4096], P('tensor')
- ffn_bias_grad: float32 [2, 4096], P(None, 'tensor')
Inputs may be any that keep to these rules, and one draw needn't show every extreme that they name: `doc_lengths`: each row holds, in order, the lengths of the 4 documents packed into one pack's 256 slots; they sum to 256, a zero length is an empty document, and some pack holds one document of 256 tokens.
All inputs are finite; a program needn't handle non-finite values.
Results may differ from a plain program's by a relative error of at most 0.025.
Values may be sent and summed in bfloat16 or wider, within the bound.
A program may use at most 256 MiB of HBM per device.

v0:
```python
import math

import jax
import jax.numpy as jnp
from jax import lax
from jax.sharding import PartitionSpec as P

HEADS = 16
FF = 4096


EPS = 1e-05
NEGATIVE = -1000000000.0


def normalize(values):
    center = jnp.mean(values, axis=-1, keepdims=True)
    spread = jnp.mean(values * values, axis=-1, keepdims=True) - center * center
    inverse = lax.rsqrt(spread + EPS)
    return ((values - center) * inverse, inverse)


def normalize_back(grad_normed, normed, inverse):
    first_mean = jnp.mean(grad_normed, axis=-1, keepdims=True)
    second = jnp.mean(grad_normed * normed, axis=-1, keepdims=True)
    return inverse * (grad_normed - first_mean - normed * second)


def block_scores(query_rows, key_rows, doc_ids, row_first, row_last, factor):
    scores = (
        jnp.einsum("qhd,khd->hqk", query_rows, key_rows, preferred_element_type=jnp.float32)
        * factor
    )
    query_pos = jnp.arange(row_first, row_last)
    key_pos = jnp.arange(row_last)
    same_doc = doc_ids[row_first:row_last, None] == doc_ids[None, :row_last]
    allowed = jnp.logical_and(same_doc, key_pos[None, :] <= query_pos[:, None])
    return (jnp.where(allowed[None], scores, NEGATIVE), allowed)


def attend_forward(query_rows, key_rows, value_rows, doc_ids, factor):
    total_rows = query_rows.shape[0]
    block_rows = min(512, total_rows)
    scores, allowed = block_scores(query_rows, key_rows, doc_ids, 0, block_rows, factor)
    row_peak = jnp.max(scores, axis=-1, keepdims=True)
    exponent = jnp.exp(scores - row_peak)
    row_total = jnp.sum(exponent, axis=-1, keepdims=True)
    prob_low = (exponent / row_total).astype(jnp.bfloat16)
    pieces = jnp.einsum("hqk,khd->qhd", prob_low, value_rows, preferred_element_type=jnp.float32)
    sums_log = [row_peak + jnp.log(row_total)]
    return (pieces, sums_log)


def attend_backward(query_rows, key_rows, value_rows, grad_out, doc_ids, sums_log, factor):
    total_rows = query_rows.shape[0]
    block_rows = min(512, total_rows)
    query_parts = []
    grad_keys = jnp.zeros(key_rows.shape, jnp.float32)
    grad_values = jnp.zeros(value_rows.shape, jnp.float32)
    for block_index, row_first in enumerate(range(0, total_rows, block_rows)):
        row_last = row_first + block_rows
        scores, allowed = block_scores(query_rows, key_rows, doc_ids, row_first, row_last, factor)
        prob_rows = jnp.where(allowed[None], jnp.exp(scores - sums_log[block_index]), 0.0)
        prob_low = prob_rows.astype(jnp.bfloat16)
        grad_probs = jnp.einsum(
            "qhd,khd->hqk", grad_out, value_rows, preferred_element_type=jnp.float32
        )
        inner_sum = jnp.sum(prob_rows * grad_probs, axis=-1, keepdims=True)
        grad_scores = (prob_rows * (grad_probs - inner_sum) * factor).astype(jnp.bfloat16)
        query_parts.append(
            jnp.einsum("hqk,khd->qhd", grad_scores, key_rows, preferred_element_type=jnp.float32)
        )
        grad_keys = grad_keys.at[:row_last].add(
            jnp.einsum("hqk,qhd->khd", grad_scores, query_rows, preferred_element_type=jnp.float32)
        )
        grad_values = grad_values.at[:row_last].add(
            jnp.einsum("hqk,qhd->khd", prob_low, grad_out, preferred_element_type=jnp.float32)
        )
    return (query_parts[0], grad_keys, grad_values)


def local(
    tokens,
    out_grad,
    doc_lengths,
    w_qkv,
    w_out,
    gains,
    biases,
    head_scale,
    w_fc1,
    w_fc2,
    mid_gain,
    ffn_biases,
):
    qkv_full, out_full, gain_full, bias_full = (
        lax.all_gather(w_qkv, ("dp", "tensor"), axis=0, tiled=True),
        lax.all_gather(w_out, ("dp", "tensor"), axis=0, tiled=True),
        lax.all_gather(gains.astype(jnp.bfloat16), ("dp", "tensor"), axis=0, tiled=True).astype(
            gains.dtype
        ),
        lax.all_gather(biases.astype(jnp.bfloat16), ("dp", "tensor"), axis=0, tiled=True).astype(
            biases.dtype
        ),
    )
    fc1_rows, fc2_cols = (
        lax.all_gather(w_fc1, "dp", axis=0, tiled=True),
        lax.all_gather(w_fc2, "dp", axis=1, tiled=True),
    )
    model_width = tokens.shape[1]
    local_rows = tokens.shape[0]
    head_dim = model_width // HEADS
    factor = 1.0 / math.sqrt(head_dim)
    doc_ends = jnp.cumsum(doc_lengths[0])[:-1]
    places = jnp.arange(local_rows)
    doc_ids = jnp.sum((places[:, None] >= doc_ends[None, :]).astype(jnp.int32), axis=1)
    inputs = tokens.astype(jnp.float32)
    normed_one, inverse_one = normalize(inputs)
    normed_in = (normed_one * gain_full[:, 0] + bias_full[:, 0]).astype(jnp.bfloat16)
    zero_bias = jnp.zeros((model_width,), jnp.float32)
    qkv_bias = jnp.concatenate([bias_full[:, 1], zero_bias, bias_full[:, 2]])
    projected = (
        jnp.dot(normed_in, qkv_full, preferred_element_type=jnp.float32) + qkv_bias
    ).astype(jnp.bfloat16)
    query_rows = projected[:, :model_width].reshape(local_rows, HEADS, head_dim)
    key_rows = projected[:, model_width : 2 * model_width].reshape(local_rows, HEADS, head_dim)
    value_rows = projected[:, 2 * model_width :].reshape(local_rows, HEADS, head_dim)
    attended, sums_log = attend_forward(query_rows, key_rows, value_rows, doc_ids, factor)
    attended = attended.reshape(local_rows, model_width)
    scale_wide = jnp.repeat(head_scale, head_dim)
    scaled = (attended * scale_wide).astype(jnp.bfloat16)
    branch = jnp.dot(scaled, out_full, preferred_element_type=jnp.float32) + bias_full[:, 3]
    normed_post, inverse_post = normalize(branch)
    middle = inputs + normed_post * gain_full[:, 1] + bias_full[:, 4]
    normed_two, inverse_two = normalize(middle)
    normed_mid = (normed_two * gain_full[:, 2] + bias_full[:, 5]).astype(jnp.bfloat16)
    gathered = lax.all_gather(normed_mid, "tensor", axis=0, tiled=True)
    hidden_pre = jnp.dot(gathered, fc1_rows, preferred_element_type=jnp.float32) + ffn_biases[0]
    activated, gelu_pull = jax.vjp(jax.nn.gelu, hidden_pre)
    act_sum, act_square = (
        lax.psum(jnp.sum(activated, axis=1).astype(jnp.bfloat16), "tensor").astype(jnp.float32),
        lax.psum(jnp.sum(activated * activated, axis=1).astype(jnp.bfloat16), "tensor").astype(
            jnp.float32
        ),
    )
    center = act_sum / FF
    inverse_mid = lax.rsqrt(act_square / FF - center * center + EPS)[:, None]
    normed_act = (activated - center[:, None]) * inverse_mid
    hidden = (normed_act * mid_gain + ffn_biases[1]).astype(jnp.bfloat16)
    hidden_rows = hidden
    ffn_out = lax.psum_scatter(
        jnp.dot(hidden_rows, fc2_cols, preferred_element_type=jnp.float32).astype(jnp.bfloat16),
        "tensor",
        scatter_dimension=0,
        tiled=True,
    ).astype(jnp.float32)
    shard_rows = lax.all_gather(out_grad, "tensor", axis=0, tiled=True)
    grad_piece = jnp.einsum("rd,fd->rf", shard_rows, fc2_cols, preferred_element_type=jnp.float32)
    hidden_rows = hidden
    fc2_run = jnp.einsum("rf,rd->fd", hidden_rows, shard_rows, preferred_element_type=jnp.float32)
    mid_gain_part = jnp.sum(grad_piece * normed_act, axis=0)
    mid_bias_part = jnp.sum(grad_piece, axis=0)
    grad_normed_act = grad_piece * mid_gain
    first_sum, second_sum = (
        lax.psum(jnp.sum(grad_normed_act, axis=1).astype(jnp.bfloat16), "tensor").astype(
            jnp.float32
        ),
        lax.psum(
            jnp.sum(grad_normed_act * normed_act, axis=1).astype(jnp.bfloat16), "tensor"
        ).astype(jnp.float32),
    )
    grad_act = inverse_mid * (
        grad_normed_act - first_sum[:, None] / FF - normed_act * (second_sum[:, None] / FF)
    )
    grad_pre = gelu_pull(grad_act)[0].astype(jnp.bfloat16)
    fc1_part = jnp.einsum("rd,rf->df", gathered, grad_pre, preferred_element_type=jnp.float32)
    fc1_bias_part = jnp.sum(grad_pre.astype(jnp.float32), axis=0)
    grad_normed_mid = lax.psum_scatter(
        jnp.einsum("rf,df->rd", grad_pre, fc1_rows, preferred_element_type=jnp.float32).astype(
            jnp.bfloat16
        ),
        "tensor",
        scatter_dimension=0,
        tiled=True,
    ).astype(jnp.float32)
    ffn_bias_part = jnp.stack([fc1_bias_part, mid_bias_part])
    fc1_grad, fc2_grad = (
        lax.psum_scatter(
            fc1_part.astype(jnp.bfloat16), "dp", scatter_dimension=0, tiled=True
        ).astype(jnp.float32),
        lax.psum_scatter(
            fc2_run.astype(jnp.bfloat16), "dp", scatter_dimension=1, tiled=True
        ).astype(jnp.float32),
    )
    mid_gain_grad, ffn_bias_grad = lax.psum((mid_gain_part, ffn_bias_part), "dp")
    mixed_out = (middle + ffn_out + bias_full[:, 6]).astype(jnp.bfloat16)
    final_grad = out_grad.astype(jnp.float32)
    grad_middle = final_grad + normalize_back(
        grad_normed_mid * gain_full[:, 2], normed_two, inverse_two
    )
    grad_post = normalize_back(grad_middle * gain_full[:, 1], normed_post, inverse_post).astype(
        jnp.bfloat16
    )
    out_local = jnp.einsum("td,te->de", scaled, grad_post, preferred_element_type=jnp.float32)
    grad_scaled = jnp.einsum("te,de->td", grad_post, out_full, preferred_element_type=jnp.float32)
    scale_local = jnp.sum(
        (grad_scaled * attended).reshape(local_rows, HEADS, head_dim), axis=(0, 2)
    )
    grad_attended = (
        (grad_scaled * scale_wide).astype(jnp.bfloat16).reshape(local_rows, HEADS, head_dim)
    )
    grad_query, grad_keys, grad_values = attend_backward(
        query_rows, key_rows, value_rows, grad_attended, doc_ids, sums_log, factor
    )
    grad_projected = jnp.concatenate(
        [
            grad_query.reshape(local_rows, model_width),
            grad_keys.reshape(local_rows, model_width),
            grad_values.reshape(local_rows, model_width),
        ],
        axis=1,
    ).astype(jnp.bfloat16)
    qkv_local = jnp.einsum(
        "td,te->de", normed_in, grad_projected, preferred_element_type=jnp.float32
    )
    grad_normed_in = jnp.einsum(
        "te,de->td", grad_projected, qkv_full, preferred_element_type=jnp.float32
    )
    token_grad = grad_middle + normalize_back(
        grad_normed_in * gain_full[:, 0], normed_one, inverse_one
    )
    projected_sums = jnp.sum(grad_projected.astype(jnp.float32), axis=0)
    gains_local = jnp.stack(
        [
            jnp.sum(grad_normed_in * normed_one, axis=0),
            jnp.sum(grad_middle * normed_post, axis=0),
            jnp.sum(grad_normed_mid * normed_two, axis=0),
        ],
        axis=1,
    )
    biases_local = jnp.stack(
        [
            jnp.sum(grad_normed_in, axis=0),
            projected_sums[:model_width],
            projected_sums[2 * model_width :],
            jnp.sum(grad_post.astype(jnp.float32), axis=0),
            jnp.sum(grad_middle, axis=0),
            jnp.sum(grad_normed_mid, axis=0),
            jnp.sum(final_grad, axis=0),
        ],
        axis=1,
    )
    qkv_grad, out_weight_grad, gains_grad, biases_grad = (
        lax.psum_scatter(qkv_local, ("dp", "tensor"), scatter_dimension=0, tiled=True),
        lax.psum_scatter(out_local, ("dp", "tensor"), scatter_dimension=0, tiled=True),
        lax.psum_scatter(gains_local, ("dp", "tensor"), scatter_dimension=0, tiled=True),
        lax.psum_scatter(biases_local, ("dp", "tensor"), scatter_dimension=0, tiled=True),
    )
    scale_grad = lax.psum(scale_local, ("dp", "tensor"))
    return (
        mixed_out,
        token_grad,
        qkv_grad,
        out_weight_grad,
        gains_grad,
        biases_grad,
        scale_grad,
        fc1_grad,
        fc2_grad,
        mid_gain_grad,
        ffn_bias_grad,
    )


def solution(mesh):
    return jax.shard_map(
        local,
        mesh=mesh,
        in_specs=(
            P(("dp", "tensor"), None),
            P(("dp", "tensor"), None),
            P(("dp", "tensor"), None),
            P(("dp", "tensor"), None),
            P(("dp", "tensor"), None),
            P(("dp", "tensor"), None),
            P(("dp", "tensor"), None),
            P(),
            P("dp", "tensor"),
            P("tensor", "dp"),
            P("tensor"),
            P(None, "tensor"),
        ),
        out_specs=(
            P(("dp", "tensor"), None),
            P(("dp", "tensor"), None),
            P(("dp", "tensor"), None),
            P(("dp", "tensor"), None),
            P(("dp", "tensor"), None),
            P(("dp", "tensor"), None),
            P(),
            P("dp", "tensor"),
            P("tensor", "dp"),
            P("tensor"),
            P(None, "tensor"),
        ),
        check_vma=False,
    )
```

profile of v0, /device:TPU:0, one launch (start us, length us, event | category | flops | bytes accessed | tf_op | source)
XLA Modules:
  0.0 1065.0 jit_solution(10372817947228937396)
XLA Ops:
  15.0 43.3 %all-gather = bf16[32,32,3]{1,2,0:T(4,128)(2,1)S(1)} all-gather(bf16[1,32,3]{1,2,0:T(4,128)(2,1)S(1)} %convert_bitcast_fusion.1), channel_id=1, replica_groups=mesh['dp'=4,'tensor'=8] {'dp','tensor'}, dimensions={0}, use_global_device_ids=true | all-gather | bytes 6336 | tf_op jit(solution)/shard_map/all_gather | solution.py:99
  58.4 37.3 %all-gather.1 = bf16[32,32,7]{1,2,0:T(8,128)(2,1)S(1)} all-gather(bf16[1,32,7]{1,2,0:T(8,128)(2,1)S(1)} %convert_bitcast_fusion), channel_id=1, replica_groups=mesh['dp'=4,'tensor'=8] {'dp','tensor'}, dimensions={0}, use_global_device_ids=true | all-gather | bytes 14784 | tf_op jit(solution)/shard_map/all_gather | solution.py:102
  105.0 36.3 %all-gather.11.cloned.1.call-done = bf16[1024,1024]{1,0:T(8,128)(2,1)} async-done(((bf16[32,1024]{1,0:T(8,128)(2,1)}), bf16[1024,1024]{1,0:T(8,128)(2,1)}) %all-gather.11.cloned.1.call-update) | async-done | bytes 2097168 | tf_op jit(solution)/shard_map/all_gather | solution.py:98
  146.6 25.3 %all-gather.17.cloned.1.call-done = bf16[512,1024]{1,0:T(8,128)(2,1)} async-done(((bf16[512,256]{1,0:T(8,128)(2,1)}), bf16[512,1024]{1,0:T(8,128)(2,1)}) %all-gather.17.cloned.1.call-update) | async-done | bytes 1048592 | tf_op jit(solution)/shard_map/all_gather | solution.py:108
  171.9 36.8 %all-gather.19.cloned.1.call-done = bf16[2048,1024]{1,0:T(8,128)(2,1)} async-done(((bf16[256,1024]{1,0:T(8,128)(2,1)}), bf16[2048,1024]{1,0:T(8,128)(2,1)}) %all-gather.19.cloned.1.call-update) | async-done | bytes 4194320 | tf_op jit(solution)/shard_map/all_gather | solution.py:157
  208.7 6.8 fusion.88
  221.1 17.0 %all-gather.15.cloned.1.call-done = bf16[1024,512]{1,0:T(8,128)(2,1)} async-done(((bf16[256,512]{1,0:T(8,128)(2,1)}), bf16[1024,512]{1,0:T(8,128)(2,1)}) %all-gather.15.cloned.1.call-update) | async-done | bytes 1048592 | tf_op jit(solution)/shard_map/all_gather | solution.py:107
  238.1 38.6 %all-gather.13.cloned.1.call-done = bf16[2048,1024]{1,0:T(8,128)(2,1)} async-done(((bf16[256,1024]{1,0:T(8,128)(2,1)}), bf16[2048,1024]{1,0:T(8,128)(2,1)}) %all-gather.13.cloned.1.call-update) | async-done | bytes 4194320 | tf_op jit(solution)/shard_map/all_gather | solution.py:137
  276.7 8.3 fusion.78
  285.0 13.4 %all-reduce.2 = (bf16[2048]{0:T(1024)(128)(2,1)S(1)}, bf16[2048]{0:T(1024)(128)(2,1)S(1)}) all-reduce(bf16[2048]{0:T(1024)(128)(2,1)S(1)} %get-tuple-element.55, bf16[2048]{0:T(1024)(128)(2,1)S(1)} %get-tuple-element.54), channel_id=1, replica_groups=mesh['dp'=4,'tensor'=8] {'tensor'}, use_global_device_ids=true, to_apply=%region_13.14 | all-reduce | flops 4096 | bytes 16384 | tf_op jit(solution)/shard_map/psum | solution.py:142
  303.8 12.5 %all-reduce.1 = (bf16[2048]{0:T(1024)(128)(2,1)S(1)}, bf16[2048]{0:T(1024)(128)(2,1)S(1)}) all-reduce(bf16[2048]{0:T(1024)(128)(2,1)S(1)} %get-tuple-element.52, bf16[2048]{0:T(1024)(128)(2,1)S(1)} %get-tuple-element.53), channel_id=1, replica_groups=mesh['dp'=4,'tensor'=8] {'tensor'}, use_global_device_ids=true, to_apply=%region_18.19 | all-reduce | flops 4096 | bytes 16384 | tf_op jit(solution)/shard_map/psum | solution.py:168
  316.3 7.3 convert_reduce_fusion
  329.5 8.3 convolution_convert_fusion.1
  344.7 7.9 convolution_convert_fusion.2
  352.9 28.1 %reduce-scatter.15.cloned.1.call-done = bf16[256,1024]{1,0:T(8,128)(2,1)} async-done(((bf16[2048,1024]{1,0:T(8,128)(2,1)}), bf16[256,1024]{1,0:T(8,128)(2,1)}) %reduce-scatter.15.cloned.1.call-update) | async-done | bytes 524304 | tf_op jit(solution)/shard_map/reduce_scatter | solution.py:178
  382.6 53.5 %reduce-scatter.13.cloned.1.call-done = bf16[256,1024]{1,0:T(8,128)(2,1)} async-done(((bf16[2048,1024]{1,0:T(8,128)(2,1)}), bf16[256,1024]{1,0:T(8,128)(2,1)}) %reduce-scatter.13.cloned.1.call-update) | async-done | bytes 524304 | tf_op jit(solution)/shard_map/reduce_scatter | solution.py:151
  444.2 8.8 fusion.31
  453.0 8.9 fusion.34
  486.0 12.6 %all-reduce = (f32[512]{0:T(512)}, f32[2,512]{1,0:T(2,128)}) all-reduce(f32[512]{0:T(512)S(1)} %get-tuple-element.51, f32[2,512]{1,0:T(2,128)S(1)} %pad_maximum_fusion.3), channel_id=1, replica_groups=mesh['dp'=4,'tensor'=8] {'dp'}, use_global_device_ids=true, to_apply=%region_46.47 | all-reduce | flops 1536 | bytes 12288 | tf_op jit(solution)/shard_map/psum | solution.py:195
  502.4 37.0 %psum.53 = f32[16]{0:T(128)} all-reduce(f32[16]{0:T(128)S(1)} %reduce_sum.325), channel_id=1, replica_groups=mesh['dp'=4,'tensor'=8] {'dp','tensor'}, use_global_device_ids=true, to_apply=%region_42.43 | all-reduce | flops 16 | bytes 128 | tf_op jit(solution)/shard_map/psum | solution.py:259
  540.8 88.1 %reduce-scatter.25.cloned.1.call-done = f32[32,3]{1,0:T(8,128)} async-done(((f32[1024,3]{1,0:T(8,128)}), f32[32,3]{1,0:T(8,128)}) %reduce-scatter.25.cloned.1.call-update) | async-done | bytes 400
  630.3 130.4 %reduce-scatter.27.cloned.1.call-done = f32[32,7]{1,0:T(8,128)} async-done(((f32[1024,7]{1,0:T(8,128)}), f32[32,7]{1,0:T(8,128)}) %reduce-scatter.27.cloned.1.call-update) | async-done | bytes 912
  762.1 138.4 %reduce-scatter.19.cloned.1.call-done = f32[32,1024]{1,0:T(8,128)} async-done(((f32[1024,1024]{1,0:T(8,128)}), f32[32,1024]{1,0:T(8,128)}) %reduce-scatter.19.cloned.1.call-update) | async-done | bytes 131088 | tf_op jit(solution)/shard_map/reduce_scatter | solution.py:255
  900.5 157.8 %reduce-scatter.17.cloned.1.call-done = f32[32,3072]{1,0:T(8,128)} async-done(((f32[1024,3072]{1,0:T(8,128)}), f32[32,3072]{1,0:T(8,128)}) %reduce-scatter.17.cloned.1.call-update) | async-done | bytes 393232 | tf_op jit(solution)/shard_map/reduce_scatter | solution.py:254
  (135 shorter events, 87.7 us)
Async XLA Ops:
  7.2 88.8 %all-gather.9.cloned.1.call-start = ((), (), s32[]{:S(2)}) async-start(), calls=%async_computation.8 | async-start | bytes 6488064 | tf_op jit(solution)/shard_map/all_gather | solution.py:97
  7.9 133.4 %all-gather.11.cloned.1.call-start = ((), (), s32[]{:S(2)}) async-start(), calls=%async_computation.9 | async-start | bytes 2162688 | tf_op jit(solution)/shard_map/all_gather | solution.py:98
  8.7 163.3 %all-gather.17.cloned.1.call-start = ((), (), s32[]{:S(2)}) async-start(), calls=%async_computation.12 | async-start | bytes 1310720 | tf_op jit(solution)/shard_map/all_gather | solution.py:108
  9.4 199.3 %all-gather.19.cloned.1.call-start = ((), (), s32[]{:S(2)}) async-start(), calls=%async_computation.14 | async-start | bytes 4718592 | tf_op jit(solution)/shard_map/all_gather | solution.py:157
  10.0 228.1 %all-gather.15.cloned.1.call-start = ((), (), s32[]{:S(2)}) async-start(), calls=%async_computation.11 | async-start | bytes 1310720 | tf_op jit(solution)/shard_map/all_gather | solution.py:107
  10.6 266.1 %all-gather.13.cloned.1.call-start = ((), (), s32[]{:S(2)}) async-start(), calls=%async_computation.10 | async-start | bytes 4718592 | tf_op jit(solution)/shard_map/all_gather | solution.py:137
  101.2 2.2 copy-start.11
  141.3 5.4 copy-start.15
  146.4 234.7 %reduce-scatter.15.cloned.1.call-start = ((), (), s32[]{:S(2)}) async-start(), calls=%async_computation.15 | async-start | bytes 4718592 | tf_op jit(solution)/shard_map/reduce_scatter | solution.py:178
  276.7 21.7 %copy-start.14 = (f32[512]{0:T(512)S(1)}, f32[512]{0:T(512)}, u32[]{:S(2)}) copy-start(f32[512]{0:T(512)} %param.30) | copy-start | bytes 6148
  316.3 8.6 copy-start.16
  329.4 106.7 %reduce-scatter.13.cloned.1.call-start = ((), (), s32[]{:S(2)}) async-start(), calls=%async_computation.13 | async-start | bytes 4718592 | tf_op jit(solution)/shard_map/reduce_scatter | solution.py:151
  337.8 160.8 %reduce-scatter.21.cloned.1.call-start = ((), (), s32[]{:S(2)}) async-start(), calls=%async_computation.18 | async-start | bytes 1310720 | tf_op jit(solution)/shard_map/reduce_scatter | solution.py:188
  344.7 156.0 %reduce-scatter.23.cloned.1.call-start = ((), (), s32[]{:S(2)}) async-start(), calls=%async_computation.19 | async-start | bytes 1310720 | tf_op jit(solution)/shard_map/reduce_scatter | solution.py:191
  352.7 276.3 %reduce-scatter.25.cloned.1.call-start = ((), (), s32[]{:S(2)}) async-start(), calls=%async_computation.20 | async-start | bytes 540672
  436.2 4.2 copy-start.4
  441.3 11.7 %copy-start.9 = (bf16[256,1024]{0,1:T(8,128)(2,1)}, bf16[256,1024]{0,1:T(8,128)(2,1)S(1)}, u32[]{:S(2)}) copy-start(bf16[256,1024]{0,1:T(8,128)(2,1)S(1)} %copy.89) | copy-start | bytes 1572868
  461.9 3.5 copy-start.3
  465.4 6.3 copy-start.5
  474.3 286.4 %reduce-scatter.27.cloned.1.call-start = ((), (), s32[]{:S(2)}) async-start(), calls=%async_computation.21 | async-start | bytes 540672
  475.5 425.0 %reduce-scatter.19.cloned.1.call-start = ((), (), s32[]{:S(2)}) async-start(), calls=%async_computation.17 | async-start | bytes 4325376 | tf_op jit(solution)/shard_map/reduce_scatter | solution.py:255
  478.3 580.0 %reduce-scatter.17.cloned.1.call-start = ((), (), s32[]{:S(2)}) async-start(), calls=%async_computation.16 | async-start | bytes 12976128 | tf_op jit(solution)/shard_map/reduce_scatter | solution.py:254
  485.9 53.5 %copy-start.2 = (f32[256,1024]{1,0:T(8,128)S(1)}, f32[256,1024]{1,0:T(8,128)}, u32[]{:S(2)}) copy-start(f32[256,1024]{1,0:T(8,128)} %copy-done.1) | copy-start | bytes 3145732
  485.9 53.5 %copy-start.13 = (f32[256,1024]{1,0:T(8,128)S(1)}, f32[256,1024]{1,0:T(8,128)}, u32[]{:S(2)}) copy-start(f32[256,1024]{1,0:T(8,128)} %get-tuple-element.119) | copy-start | bytes 3145732
  (7 other events, 11.2 us)
Sparse Core Ops, SparseCore 0:
  10.9 72.5 all-gather.8
  86.3 54.9 all-gather.10
  142.8 29.0 all-gather.16
  173.7 35.0 all-gather.18
  210.1 27.9 all-gather.14
  240.4 36.1 all-gather.12
  329.5 51.4 reduce-scatter.14
  384.8 51.3 reduce-scatter.12
  438.5 27.1 reduce-scatter.20
  467.8 25.9 reduce-scatter.22
  496.1 132.8 reduce-scatter.24
  631.1 129.5 reduce-scatter.26
  763.6 136.9 reduce-scatter.18
  907.0 151.2 reduce-scatter.16
where the time goes:
time: 1070 us
  waiting for transfers between devices  754 us (70%)
  blocking collectives  156 us (15%)
  matrix products  92.5 us (9%)
  other arithmetic  31.7 us (3%)
  local copies, waits for them, and re-layouts  15.7 us (1%)
  between operations  14.6 us (1%)
    unnamed x16, waiting for transfers between devices  222 us
    reduce_scatter x1, waiting for transfers between devices, local(): lax.psum_scatter(qkv_local, ('dp', 'tensor'), scatter_dimension=0, tiled=...  158 us
    reduce_scatter x1, waiting for transfers between devices, local(): lax.psum_scatter(out_local, ('dp', 'tensor'), scatter_dimension=0, tiled=...  138 us
    reduce_scatter x1, waiting for transfers between devices, local(): lax.psum_scatter(jnp.dot(hidden_rows, fc2_cols, preferred_element_type=jn...  53.5 us
    all_gather x1, blocking collectives, local(): lax.all_gather(gains.astype(jnp.bfloat16), ('dp', 'tensor'), axis=0, tile...  43.3 us
    all_gather x1, waiting for transfers between devices, local(): gathered = lax.all_gather(normed_mid, 'tensor', axis=0, tiled=True)  38.6 us
    all_gather x1, blocking collectives, local(): lax.all_gather(biases.astype(jnp.bfloat16), ('dp', 'tensor'), axis=0, til...  37.3 us
    psum x1, blocking collectives, local(): scale_grad = lax.psum(scale_local, ('dp', 'tensor'))  37 us
  transfers between devices with their start and end apart: 14, of which 11 were waited for; matrix products, arithmetic and copies ran while one was open for 10% of the time, Pallas kernels for 0%

commit v1 on v0

--- a/solution.py
+++ b/solution.py
@@ -1,8 +1,11 @@
+import functools
 import math
 
 import jax
 import jax.numpy as jnp
 from jax import lax
+from jax.experimental import pallas as pl
+from jax.experimental.pallas import tpu as pltpu
 from jax.sharding import PartitionSpec as P
 
 HEADS = 16
@@ -79,7 +82,7 @@
     return (query_parts[0], grad_keys, grad_values)
 
 
-def local(
+def plain(
     tokens,
     out_grad,
     doc_lengths,
@@ -272,9 +275,780 @@
     )
 
 
+MESH = pl.DeviceIdType.MESH
+ANY = pl.BlockSpec(memory_space=pl.ANY)
+IN_VMEM = pl.BlockSpec(memory_space=pltpu.VMEM)
+
+
+def place():
+    z = lax.axis_index("dp")
+    t = lax.axis_index("tensor")
+    return z, lax.div(t, 4), lax.rem(lax.div(t, 2), 2), lax.rem(t, 2)
+
+
+def at(z, y, x, c):
+    return (z, y * 4 + x * 2 + c)
+
+
+def greet(partners):
+    barrier = pltpu.get_barrier_semaphore()
+    for partner in partners:
+        pl.semaphore_signal(barrier, inc=1, device_id=partner, device_id_type=MESH)
+    pl.semaphore_wait(barrier, len(partners))
+
+
+class Sends:
+    def __init__(self, send_sems, recv_sems):
+        self.send_sems, self.recv_sems, self.copies = send_sems, recv_sems, []
+
+    def start(self, src, dst, target):
+        index = len(self.copies)
+        copy = pltpu.make_async_remote_copy(
+            src_ref=src,
+            dst_ref=dst,
+            send_sem=self.send_sems.at[index],
+            recv_sem=self.recv_sems.at[index],
+            device_id=target,
+            device_id_type=MESH,
+        )
+        copy.start()
+        self.copies.append(copy)
+        return copy
+
+    def finish(self):
+        for copy in self.copies:
+            copy.wait_send()
+
+
+def gather_kernel(
+    nz,
+    qkv_ref,
+    out_ref,
+    vec_ref,
+    fc1_ref,
+    fc2_ref,
+    grad_ref,
+    qkv_all,
+    out_all,
+    vec_all,
+    fc1_all,
+    fc2_all,
+    grad_all,
+    local_sems,
+    send_sems,
+    recv_sems,
+):
+    z, y, x, c = place()
+    to_x, to_y, to_c = at(z, y, 1 - x, c), at(z, 1 - y, x, c), at(z, y, x, 1 - c)
+    others = [lax.rem(z + k, nz) for k in range(1, nz)]
+    slots = [z] + [lax.rem(z + nz - k, nz) for k in range(1, nz)]
+    peers = [at(other, y, x, c) for other in others]
+    greet([to_x, to_y, to_c] + peers)
+    sends = Sends(send_sems, recv_sems)
+    shards = ((qkv_ref, qkv_all), (out_ref, out_all))
+    mine = []
+    width1, width2 = fc1_ref.shape[0], fc2_ref.shape[1]
+    own = [
+        (qkv_ref, qkv_all.at[z, y, x, c]),
+        (out_ref, out_all.at[z, y, x, c]),
+        (vec_ref, vec_all.at[z, y, x, c]),
+        (fc1_ref, fc1_all.at[pl.ds(pl.multiple_of(z * width1, width1), width1)]),
+        (fc2_ref, fc2_all.at[:, pl.ds(pl.multiple_of(z * width2, width2), width2)]),
+        (grad_ref, grad_all.at[y, x, c]),
+    ]
+    for index, (src, dst) in enumerate(own):
+        copy = pltpu.make_async_copy(src, dst, local_sems.at[index])
+        copy.start()
+        mine.append(copy)
+
+    def halves(ref):
+        half = ref.shape[-1] // 2
+        return pl.ds(0, half), pl.ds(half, half)
+
+    vec_z = [sends.start(vec_ref, vec_all.at[z, y, x, c], peer) for peer in peers]
+    vec_x = [sends.start(vec_ref, vec_all.at[z, y, x, c], to_x)]
+    qkv_z = [sends.start(qkv_ref, qkv_all.at[z, y, x, c], peer) for peer in peers]
+
+    def first(src, whole, slot, from_input):
+        lo, hi = halves(src)
+        one = src if from_input else whole.at[slot, y, x, c]
+        return (
+            sends.start(one.at[:, lo], whole.at[slot, y, x, c, :, lo], to_x),
+            sends.start(one.at[:, hi], whole.at[slot, y, x, c, :, hi], to_y),
+        )
+
+    def second(whole, slot):
+        lo, hi = halves(whole)
+        return (
+            sends.start(whole.at[slot, y, :, c, :, lo], whole.at[slot, y, :, c, :, lo], to_y),
+            sends.start(whole.at[slot, :, x, c, :, hi], whole.at[slot, :, x, c, :, hi], to_x),
+        )
+
+    def third(whole, slot):
+        return sends.start(whole.at[slot, :, :, c], whole.at[slot, :, :, c], to_c)
+
+    def wait_all(copies):
+        for copy in copies:
+            copy.wait_recv()
+
+    def spread(src, whole, arrivals, between):
+        stage_a = [first(src, whole, z, True)]
+        stage_b = []
+        for k in range(1, nz):
+            arrivals[k - 1].wait_recv()
+            stage_a.append(first(src, whole, slots[k], False))
+            if k == 1:
+                between()
+            if k >= 2:
+                wait_all(stage_a[k - 2])
+                stage_b.append(second(whole, slots[k - 2]))
+        for k in range(len(stage_b), nz):
+            wait_all(stage_a[k])
+            stage_b.append(second(whole, slots[k]))
+        return stage_b
+
+    rest = {}
+
+    def after_qkv_z():
+        rest["out_z"] = [sends.start(out_ref, out_all.at[z, y, x, c], peer) for peer in peers]
+        rest["fc"] = []
+        for peer in peers:
+            rest["fc"].append(sends.start(fc1_ref, own[3][1], peer))
+            rest["fc"].append(sends.start(fc2_ref, own[4][1], peer))
+
+    for copy in mine[:3]:
+        copy.wait()
+    qkv_b = spread(qkv_ref, qkv_all, qkv_z, after_qkv_z)
+    wait_all(vec_z)
+    for k in range(1, nz):
+        vec_x.append(
+            sends.start(vec_all.at[slots[k], y, x, c], vec_all.at[slots[k], y, x, c], to_x)
+        )
+    out_b = spread(out_ref, out_all, rest.get("out_z", []), lambda: None)
+    wait_all(vec_x)
+    vec_y = sends.start(vec_all.at[:, y, :, c], vec_all.at[:, y, :, c], to_y)
+    lo, hi = halves(grad_ref)
+    grad_a = (
+        sends.start(grad_ref.at[:, lo], grad_all.at[y, x, c, :, lo], to_x),
+        sends.start(grad_ref.at[:, hi], grad_all.at[y, x, c, :, hi], to_y),
+    )
+    qkv_c = []
+    for k in range(nz):
+        wait_all(qkv_b[k])
+        qkv_c.append(third(qkv_all, slots[k]))
+    vec_y.wait_recv()
+    vec_c = sends.start(vec_all.at[:, :, :, c], vec_all.at[:, :, :, c], to_c)
+    mine[5].wait()
+    wait_all(grad_a)
+    grad_b = (
+        sends.start(grad_all.at[y, :, c, :, lo], grad_all.at[y, :, c, :, lo], to_y),
+        sends.start(grad_all.at[:, x, c, :, hi], grad_all.at[:, x, c, :, hi], to_x),
+    )
+    out_c = []
+    for k in range(nz):
+        wait_all(out_b[k])
+        out_c.append(third(out_all, slots[k]))
+    wait_all(grad_b)
+    grad_c = sends.start(grad_all.at[:, :, c], grad_all.at[:, :, c], to_c)
+    wait_all(qkv_c + out_c + [vec_c, grad_c] + rest.get("fc", []))
+    mine[3].wait()
+    mine[4].wait()
+    sends.finish()
+
+
+def gather(nz, w_qkv, w_out, vectors, w_fc1, w_fc2, out_grad):
+    def whole(shard, lead):
+        return jax.ShapeDtypeStruct(lead + shard.shape, shard.dtype)
+
+    every, plane = (nz, 2, 2, 2), (2, 2, 2)
+    count = 4 * (nz - 1) + 5 * 2 * nz + 64
+    return pl.pallas_call(
+        functools.partial(gather_kernel, nz),
+        name="gather",
+        out_shape=(
+            whole(w_qkv, every),
+            whole(w_out, every),
+            whole(vectors, every),
+            jax.ShapeDtypeStruct((w_fc1.shape[0] * nz, w_fc1.shape[1]), w_fc1.dtype),
+            jax.ShapeDtypeStruct((w_fc2.shape[0], w_fc2.shape[1] * nz), w_fc2.dtype),
+            whole(out_grad, plane),
+        ),
+        in_specs=[ANY] * 6,
+        out_specs=[ANY] * 6,
+        scratch_shapes=[
+            pltpu.SemaphoreType.DMA((6,)),
+            pltpu.SemaphoreType.DMA((count,)),
+            pltpu.SemaphoreType.DMA((count,)),
+        ],
+        compiler_params=pltpu.CompilerParams(collective_id=1, has_side_effects=True),
+    )(w_qkv, w_out, vectors, w_fc1, w_fc2, out_grad)
+
+
+def spread_kernel(rows_ref, all_ref, local_sem, send_sems, recv_sems):
+    z, y, x, c = place()
+    to_x, to_y, to_c = at(z, y, 1 - x, c), at(z, 1 - y, x, c), at(z, y, x, 1 - c)
+    greet([to_x, to_y, to_c])
+    sends = Sends(send_sems, recv_sems)
+    half = rows_ref.shape[1] // 2
+    lo, hi = pl.ds(0, half), pl.ds(half, half)
+    pieces = 4
+    rows = rows_ref.shape[0] // pieces
+    mine = pltpu.make_async_copy(rows_ref, all_ref.at[y, x, c], local_sem)
+    mine.start()
+    stage = []
+    for k in range(pieces):
+        part = pl.ds(k * rows, rows)
+        stage.append(
+            (
+                sends.start(rows_ref.at[part, lo], all_ref.at[y, x, c, part, lo], to_x),
+                sends.start(rows_ref.at[part, hi], all_ref.at[y, x, c, part, hi], to_y),
+            )
+        )
+    mine.wait()
+    later = []
+    for k in range(pieces):
+        part = pl.ds(k * rows, rows)
+        for copy in stage[k]:
+            copy.wait_recv()
+        one, two = all_ref.at[y, :, c, part, lo], all_ref.at[:, x, c, part, hi]
+        later.append((sends.start(one, one, to_y), sends.start(two, two, to_x)))
+    last = []
+    for k in range(pieces):
+        part = pl.ds(k * rows, rows)
+        for copy in later[k]:
+            copy.wait_recv()
+        all_four = all_ref.at[:, :, c, part]
+        last.append(sends.start(all_four, all_four, to_c))
+    for copy in last:
+        copy.wait_recv()
+    sends.finish()
+
+
+def spread_rows(rows):
+    return pl.pallas_call(
+        spread_kernel,
+        name="spread_rows",
+        out_shape=jax.ShapeDtypeStruct((2, 2, 2) + rows.shape, rows.dtype),
+        in_specs=[ANY],
+        out_specs=ANY,
+        scratch_shapes=[
+            pltpu.SemaphoreType.DMA,
+            pltpu.SemaphoreType.DMA((20,)),
+            pltpu.SemaphoreType.DMA((20,)),
+        ],
+        compiler_params=pltpu.CompilerParams(collective_id=2, has_side_effects=True),
+    )(rows)
+
+
+def sums_kernel(mine_ref, total_ref, pair, got, send_sems, recv_sems):
+    z, y, x, c = place()
+    to_c = at(z, y, x, 1 - c)
+    planes = [at(z, y, 1 - x, c), at(z, 1 - y, x, c), at(z, 1 - y, 1 - x, c)]
+    greet([to_c] + planes)
+    sends = Sends(send_sems, recv_sems)
+    sends.start(mine_ref, got.at[3], to_c).wait_recv()
+    pair[...] = mine_ref[...] + got[3]
+    arrivals = [sends.start(pair, got.at[k], plane) for k, plane in enumerate(planes)]
+    for copy in arrivals:
+        copy.wait_recv()
+    total_ref[...] = (pair[...] + got[0]) + (got[1] + got[2])
+    sends.finish()
+
+
+def tensor_sums(mine):
+    return pl.pallas_call(
+        sums_kernel,
+        name="tensor_sums",
+        out_shape=jax.ShapeDtypeStruct(mine.shape, mine.dtype),
+        in_specs=[IN_VMEM],
+        out_specs=IN_VMEM,
+        scratch_shapes=[
+            pltpu.VMEM(mine.shape, mine.dtype),
+            pltpu.VMEM((4,) + mine.shape, mine.dtype),
+            pltpu.SemaphoreType.DMA((4,)),
+            pltpu.SemaphoreType.DMA((4,)),
+        ],
+        compiler_params=pltpu.CompilerParams(collective_id=3, has_side_effects=True),
+    )(mine)
+
+
+def add_low(left, right):
+    return (left.astype(jnp.float32) + right.astype(jnp.float32)).astype(jnp.bfloat16)
+
+
+def fold_kernel(
+    nz,
+    pieces,
+    first_ref,
+    second_ref,
+    fc1_ref,
+    fc2_ref,
+    small_ref,
+    first_out,
+    second_out,
+    fc1_out,
+    fc2_out,
+    small_out,
+    from_core,
+    sums,
+    from_one,
+    from_two,
+    got1,
+    got2,
+    got_small,
+    send_sems,
+    recv_sems,
+):
+    z, y, x, c = place()
+    to_x, to_y, to_c = at(z, y, 1 - x, c), at(z, 1 - y, x, c), at(z, y, x, 1 - c)
+    others = [lax.rem(z + k, nz) for k in range(1, nz)]
+    peers = [at(other, y, x, c) for other in others]
+    greet([to_x, to_y, to_c] + peers)
+    sends = Sends(send_sems, recv_sems)
+    width1, width2 = fc1_out.shape[0], fc2_out.shape[1]
+
+    def block1(which):
+        return fc1_ref.at[pl.ds(pl.multiple_of(which * width1, width1), width1)]
+
+    def block2(which):
+        return fc2_ref.at[:, pl.ds(pl.multiple_of(which * width2, width2), width2)]
+
+    rows = first_ref.shape[3] // pieces
+    half = first_ref.shape[4] // 2
+    lo, hi = pl.ds(0, half), pl.ds(half, half)
+    parts = [pl.ds(k * rows, rows) for k in range(pieces)]
+    jobs = [(i, k) for i in range(2) for k in range(pieces)]
+    refs, outs = (first_ref, second_ref), (first_out, second_out)
+    stage_c = {
+        (i, k): sends.start(
+            refs[i].at[:, :, 1 - c, parts[k]], from_core.at[i, :, :, parts[k]], to_c
+        )
+        for i, k in jobs
+    }
+    far = []
+    for k, peer in enumerate(peers):
+        far.append(sends.start(small_ref, got_small.at[k], peer))
+        far.append(sends.start(block1(others[k]), got1.at[k], peer))
+        far.append(sends.start(block2(others[k]), got2.at[k], peer))
+
+    stage_1, stage_2 = {}, {}
+
+    def after_core(i, k):
+        part = parts[k]
+        stage_c[i, k].wait_recv()
+        for yy in range(2):
+            for xx in range(2):
+                sums[i, yy, xx, part] = add_low(
+                    refs[i][yy, xx, c, part], from_core[i, yy, xx, part]
+                )
+        stage_1[i, k] = (
+            sends.start(sums.at[i, :, 1 - x, part, lo], from_one.at[i, :, part, lo], to_x),
+            sends.start(sums.at[i, 1 - y, :, part, hi], from_one.at[i, :, part, hi], to_y),
+        )
+
+    def after_one(i, k):
+        part = parts[k]
+        for copy in stage_1[i, k]:
+            copy.wait_recv()
+        for yy in range(2):
+            sums[i, yy, x, part, lo] = add_low(
+                sums[i, yy, x, part, lo], from_one[i, yy, part, lo]
+            )
+        for xx in range(2):
+            sums[i, y, xx, part, hi] = add_low(
+                sums[i, y, xx, part, hi], from_one[i, xx, part, hi]
+            )
+        stage_2[i, k] = (
+            sends.start(sums.at[i, 1 - y, x, part, lo], from_two.at[i, part, lo], to_y),
+            sends.start(sums.at[i, y, 1 - x, part, hi], from_two.at[i, part, hi], to_x),
+        )
+
+    def after_two(i, k):
+        part = parts[k]
+        for copy in stage_2[i, k]:
+            copy.wait_recv()
+        outs[i][part] = sums[i, y, x, part].astype(jnp.float32) + from_two[i, part].astype(
+            jnp.float32
+        )
+
+    for n in range(len(jobs) + 2):
+        if n < len(jobs):
+            after_core(*jobs[n])
+        if 1 <= n < len(jobs) + 1:
+            after_one(*jobs[n - 1])
+        if n >= 2:
+            after_two(*jobs[n - 2])
+    for copy in far:
+        copy.wait_recv()
+    own1, own2, small = block1(z)[...].astype(jnp.float32), block2(z)[...].astype(jnp.float32), small_ref[...]
+    for k in range(nz - 1):
+        own1 = own1 + got1[k].astype(jnp.float32)
+        own2 = own2 + got2[k].astype(jnp.float32)
+        small = small + got_small[k]
+    fc1_out[...] = own1
+    fc2_out[...] = own2
+    small_out[...] = small
+    sends.finish()
+
+
+def fold(nz, first, second, fc1, fc2, small):
+    rows, columns = first.shape[3:]
+    low = jnp.bfloat16
+    pieces = 2
+    count = 5 * 2 * pieces + 3 * (nz - 1)
+    out1, out2 = (fc1.shape[0] // nz, fc1.shape[1]), (fc2.shape[0], fc2.shape[1] // nz)
+    kept = (jnp.float32,)
+    return pl.pallas_call(
+        functools.partial(fold_kernel, nz, pieces),
+        name="fold",
+        out_shape=tuple(
+            jax.ShapeDtypeStruct(shape, *kept)
+            for shape in ((rows, columns), (rows, columns), out1, out2, small.shape)
+        ),
+        in_specs=[IN_VMEM] * 5,
+        out_specs=[IN_VMEM] * 5,
+        scratch_shapes=[
+            pltpu.VMEM((2, 2, 2, rows, columns), low),
+            pltpu.VMEM((2, 2, 2, rows, columns), low),
+            pltpu.VMEM((2, 2, rows, columns), low),
+            pltpu.VMEM((2, rows, columns), low),
+            pltpu.VMEM((nz - 1,) + out1, low),
+            pltpu.VMEM((nz - 1,) + out2, low),
+            pltpu.VMEM((nz - 1,) + small.shape, jnp.float32),
+            pltpu.SemaphoreType.DMA((count,)),
+            pltpu.SemaphoreType.DMA((count,)),
+        ],
+        compiler_params=pltpu.CompilerParams(
+            collective_id=4, has_side_effects=True, vmem_limit_bytes=60 * 2**20
+        ),
+    )(first, second, fc1, fc2, small)
+
+
+def total_kernel(
+    nz,
+    grad_ref,
+    small_ref,
+    grad_out,
+    small_out,
+    from_core,
+    sums,
+    from_one,
+    from_two,
+    from_far,
+    small_sum,
+    small_got,
+    send_sems,
+    recv_sems,
+):
+    z, y, x, c = place()
+    to_x, to_y, to_c = at(z, y, 1 - x, c), at(z, 1 - y, x, c), at(z, y, x, 1 - c)
+    others = [lax.rem(z + k, nz) for k in range(1, nz)]
+    order = others + [z]
+    peers = [at(other, y, x, c) for other in others]
+    greet([to_x, to_y, to_c] + peers)
+    sends = Sends(send_sems, recv_sems)
+    half = grad_ref.shape[-1] // 2
+    lo, hi = pl.ds(0, half), pl.ds(half, half)
+    stage_c = [
+        sends.start(grad_ref.at[which, :, :, 1 - c], from_core.at[which], to_c)
+        for which in order
+    ]
+    small_c = sends.start(small_ref, small_got.at[0], to_c)
+    stage_1, stage_2, far = {}, {}, {}
+
+    def after_core(k):
+        which = order[k]
+        stage_c[k].wait_recv()
+        for yy in range(2):
+            for xx in range(2):
+                sums[which, yy, xx] = add_low(
+                    grad_ref[which, yy, xx, c], from_core[which, yy, xx]
+                )
+        stage_1[k] = (
+            sends.start(sums.at[which, :, 1 - x, :, lo], from_one.at[which, :, :, lo], to_x),
+            sends.start(sums.at[which, 1 - y, :, :, hi], from_one.at[which, :, :, hi], to_y),
+        )
+
+    def after_one(k):
+        which = order[k]
+        for copy in stage_1[k]:
+            copy.wait_recv()
+        for yy in range(2):
+            sums[which, yy, x, :, lo] = add_low(
+                sums[which, yy, x, :, lo], from_one[which, yy, :, lo]
+            )
+        for xx in range(2):
+            sums[which, y, xx, :, hi] = add_low(
+                sums[which, y, xx, :, hi], from_one[which, xx, :, hi]
+            )
+        stage_2[k] = (
+            sends.start(sums.at[which, 1 - y, x, :, lo], from_two.at[which, :, lo], to_y),
+            sends.start(sums.at[which, y, 1 - x, :, hi], from_two.at[which, :, hi], to_x),
+        )
+
+    def after_two(k):
+        which = order[k]
+        for copy in stage_2[k]:
+            copy.wait_recv()
+        if k < nz - 1:
+            sums[which, y, x] = add_low(sums[which, y, x], from_two[which])
+            far[k] = sends.start(sums.at[which, y, x], from_far.at[k], peers[k])
+
+    steps = []
+    small_c.wait_recv()
+    small_sum[0] = small_ref[...] + small_got[0]
+    small_x = sends.start(small_sum.at[0], small_got.at[1], to_x)
+    for n in range(nz + 2):
+        if n < nz:
+            after_core(n)
+        if 1 <= n < nz + 1:
+            after_one(n - 1)
+        if n >= 2:
+            after_two(n - 2)
+        if n == 1:
+            small_x.wait_recv()
+            small_sum[1] = small_sum[0] + small_got[1]
+            small_y = sends.start(small_sum.at[1], small_got.at[2], to_y)
+        if n == 3:
+            small_y.wait_recv()
+            small_sum[2] = small_sum[1] + small_got[2]
+            small_far = [
+                sends.start(small_sum.at[2], small_got.at[3 + k], peer)
+                for k, peer in enumerate(peers)
+            ]
+    total = sums[z, y, x].astype(jnp.float32) + from_two[z].astype(jnp.float32)
+    for k in range(nz - 1):
+        far[k].wait_recv()
+        total = total + from_far[k].astype(jnp.float32)
+    grad_out[...] = total
+    small = small_sum[2]
+    for k in range(nz - 1):
+        small_far[k].wait_recv()
+        small = small + small_got[3 + k]
+    small_out[...] = small
+    sends.finish()
+
+
+def total_all(nz, grad, small):
+    rows, columns = grad.shape[4:]
+    low = jnp.bfloat16
+    count = 5 * nz + (nz - 1) + 3 + (nz - 1)
+    return pl.pallas_call(
+        functools.partial(total_kernel, nz),
+        name="total_all",
+        out_shape=(
+            jax.ShapeDtypeStruct((rows, columns), jnp.float32),
+            jax.ShapeDtypeStruct(small.shape, jnp.float32),
+        ),
+        in_specs=[IN_VMEM] * 2,
+        out_specs=[IN_VMEM] * 2,
+        scratch_shapes=[
+            pltpu.VMEM((nz, 2, 2, rows, columns), low),
+            pltpu.VMEM((nz, 2, 2, rows, columns), low),
+            pltpu.VMEM((nz, 2, rows, columns), low),
+            pltpu.VMEM((nz, rows, columns), low),
+            pltpu.VMEM((nz - 1, rows, columns), low),
+            pltpu.VMEM((3,) + small.shape, jnp.float32),
+            pltpu.VMEM((nz + 2,) + small.shape, jnp.float32),
+            pltpu.SemaphoreType.DMA((count,)),
+            pltpu.SemaphoreType.DMA((count,)),
+        ],
+        compiler_params=pltpu.CompilerParams(
+            collective_id=5, has_side_effects=True, vmem_limit_bytes=60 * 2**20
+        ),
+    )(grad, small)
+
+
+def fused(
+    nz,
+    tokens,
+    out_grad,
+    doc_lengths,
+    w_qkv,
+    w_out,
+    gains,
+    biases,
+    head_scale,
+    w_fc1,
+    w_fc2,
+    mid_gain,
+    ffn_biases,
+):
+    model_width = tokens.shape[1]
+    local_rows = tokens.shape[0]
+    head_dim = model_width // HEADS
+    factor = 1.0 / math.sqrt(head_dim)
+    share = gains.shape[0]
+    vectors = jnp.concatenate(
+        [gains, biases, jnp.zeros((share, 128 - gains.shape[1] - biases.shape[1]), jnp.float32)],
+        axis=1,
+    )
+    qkv_full, out_full, vec_full, fc1_rows, fc2_cols, shard_rows = gather(
+        nz, w_qkv, w_out, vectors, w_fc1, w_fc2, out_grad
+    )
+    qkv_full = qkv_full.reshape(model_width, -1)
+    out_full = out_full.reshape(model_width, -1)
+    vec_full = vec_full.reshape(model_width, 128)
+    shard_rows = shard_rows.reshape(-1, model_width)
+    vec_rows = vec_full[:, :10].T
+    gain_full = vec_rows[:3]
+    bias_full = vec_rows[3:]
+    doc_ends = jnp.cumsum(doc_lengths[0])[:-1]
+    places = jnp.arange(local_rows)
+    doc_ids = jnp.sum((places[:, None] >= doc_ends[None, :]).astype(jnp.int32), axis=1)
+    inputs = tokens.astype(jnp.float32)
+    normed_one, inverse_one = normalize(inputs)
+    normed_in = (normed_one * gain_full[0] + bias_full[0]).astype(jnp.bfloat16)
+    zero_bias = jnp.zeros((model_width,), jnp.float32)
+    qkv_bias = jnp.concatenate([bias_full[1], zero_bias, bias_full[2]])
+    projected = (
+        jnp.dot(normed_in, qkv_full, preferred_element_type=jnp.float32) + qkv_bias
+    ).astype(jnp.bfloat16)
+    query_rows = projected[:, :model_width].reshape(local_rows, HEADS, head_dim)
+    key_rows = projected[:, model_width : 2 * model_width].reshape(local_rows, HEADS, head_dim)
+    value_rows = projected[:, 2 * model_width :].reshape(local_rows, HEADS, head_dim)
+    attended, sums_log = attend_forward(query_rows, key_rows, value_rows, doc_ids, factor)
+    attended = attended.reshape(local_rows, model_width)
+    scale_wide = jnp.repeat(head_scale, head_dim)
+    scaled = (attended * scale_wide).astype(jnp.bfloat16)
+    branch = jnp.dot(scaled, out_full, preferred_element_type=jnp.float32) + bias_full[3]
+    normed_post, inverse_post = normalize(branch)
+    middle = inputs + normed_post * gain_full[1] + bias_full[4]
+    normed_two, inverse_two = normalize(middle)
+    normed_mid = (normed_two * gain_full[2] + bias_full[5]).astype(jnp.bfloat16)
+    gathered = spread_rows(normed_mid).reshape(-1, model_width)
+    group_rows = gathered.shape[0]
+    hidden_pre = jnp.dot(gathered, fc1_rows, preferred_element_type=jnp.float32) + ffn_biases[0]
+    activated, gelu_pull = jax.vjp(jax.nn.gelu, hidden_pre)
+    grad_piece = jnp.einsum("rd,fd->rf", shard_rows, fc2_cols, preferred_element_type=jnp.float32)
+    grad_normed_act = grad_piece * mid_gain
+    row_sums = jnp.stack(
+        [
+            jnp.sum(activated, axis=1),
+            jnp.sum(activated * activated, axis=1),
+            jnp.sum(grad_normed_act, axis=1),
+            jnp.sum(grad_normed_act * activated, axis=1),
+        ]
+        + [jnp.zeros((group_rows,), jnp.float32)] * 4
+    )
+    row_sums = tensor_sums(row_sums) / FF
+    center = row_sums[0]
+    inverse_mid = lax.rsqrt(row_sums[1] - center * center + EPS)
+    first_mean = row_sums[2]
+    second_mean = inverse_mid * (row_sums[3] - center * row_sums[2])
+    inverse_mid = inverse_mid[:, None]
+    normed_act = (activated - center[:, None]) * inverse_mid
+    hidden = (normed_act * mid_gain + ffn_biases[1]).astype(jnp.bfloat16)
+    ffn_part = jnp.dot(hidden, fc2_cols, preferred_element_type=jnp.float32).astype(jnp.bfloat16)
+    fc2_part = jnp.einsum("rf,rd->fd", hidden, shard_rows, preferred_element_type=jnp.float32)
+    grad_act = inverse_mid * (
+        grad_normed_act - first_mean[:, None] - normed_act * second_mean[:, None]
+    )
+    grad_pre = gelu_pull(grad_act)[0].astype(jnp.bfloat16)
+    fc1_part = jnp.einsum("rd,rf->df", gathered, grad_pre, preferred_element_type=jnp.float32)
+    mid_part = jnp.einsum("rf,df->rd", grad_pre, fc1_rows, preferred_element_type=jnp.float32)
+    units = fc1_rows.shape[1]
+    unit_sums = jnp.concatenate(
+        [
+            jnp.sum(grad_piece * normed_act, axis=0)[None],
+            jnp.sum(grad_pre.astype(jnp.float32), axis=0)[None],
+            jnp.sum(grad_piece, axis=0)[None],
+            jnp.zeros((5, units), jnp.float32),
+        ]
+    )
+    plane = (2, 2, 2, local_rows, model_width)
+    grad_normed_mid, ffn_out, fc1_grad, fc2_grad, unit_sums = fold(
+        nz,
+        mid_part.astype(jnp.bfloat16).reshape(plane),
+        ffn_part.reshape(plane),
+        fc1_part.astype(jnp.bfloat16),
+        fc2_part.astype(jnp.bfloat16),
+        unit_sums,
+    )
+    mid_gain_grad, ffn_bias_grad = unit_sums[0], unit_sums[1:3]
+    mixed_out = (middle + ffn_out + bias_full[6]).astype(jnp.bfloat16)
+    final_grad = out_grad.astype(jnp.float32)
+    grad_middle = final_grad + normalize_back(
+        grad_normed_mid * gain_full[2], normed_two, inverse_two
+    )
+    grad_post = normalize_back(grad_middle * gain_full[1], normed_post, inverse_post).astype(
+        jnp.bfloat16
+    )
+    out_local = jnp.einsum("td,te->de", scaled, grad_post, preferred_element_type=jnp.float32)
+    grad_scaled = jnp.einsum("te,de->td", grad_post, out_full, preferred_element_type=jnp.float32)
+    scale_local = jnp.sum(
+        (grad_scaled * attended).reshape(local_rows, HEADS, head_dim), axis=(0, 2)
+    )
+    grad_attended = (
+        (grad_scaled * scale_wide).astype(jnp.bfloat16).reshape(local_rows, HEADS, head_dim)
+    )
+    grad_query, grad_keys, grad_values = attend_backward(
+        query_rows, key_rows, value_rows, grad_attended, doc_ids, sums_log, factor
+    )
+    grad_projected = jnp.concatenate(
+        [
+            grad_query.reshape(local_rows, model_width),
+            grad_keys.reshape(local_rows, model_width),
+            grad_values.reshape(local_rows, model_width),
+        ],
+        axis=1,
+    ).astype(jnp.bfloat16)
+    qkv_local = jnp.einsum(
+        "td,te->de", normed_in, grad_projected, preferred_element_type=jnp.float32
+    )
+    grad_normed_in = jnp.einsum(
+        "te,de->td", grad_projected, qkv_full, preferred_element_type=jnp.float32
+    )
+    token_grad = grad_middle + normalize_back(
+        grad_normed_in * gain_full[0], normed_one, inverse_one
+    )
+    projected_sums = jnp.sum(grad_projected.astype(jnp.float32), axis=0)
+    small = jnp.stack(
+        [
+            jnp.sum(grad_normed_in * normed_one, axis=0),
+            jnp.sum(grad_middle * normed_post, axis=0),
+            jnp.sum(grad_normed_mid * normed_two, axis=0),
+            jnp.sum(grad_normed_in, axis=0),
+            projected_sums[:model_width],
+            projected_sums[2 * model_width :],
+            jnp.sum(grad_post.astype(jnp.float32), axis=0),
+            jnp.sum(grad_middle, axis=0),
+            jnp.sum(grad_normed_mid, axis=0),
+            jnp.sum(final_grad, axis=0),
+            jnp.pad(scale_local, (0, model_width - HEADS)),
+        ]
+        + [jnp.zeros((model_width,), jnp.float32)] * 5
+    )
+    weights = jnp.concatenate(
+        [qkv_local.astype(jnp.bfloat16), out_local.astype(jnp.bfloat16)], axis=1
+    ).reshape(nz, 2, 2, 2, share, -1)
+    weight_grad, small = total_all(nz, weights, small)
+    index = lax.axis_index("dp") * 8 + lax.axis_index("tensor")
+    ours = lax.dynamic_slice(small, (0, index * share), (10, share)).T
+    return (
+        mixed_out,
+        token_grad,
+        weight_grad[:, : w_qkv.shape[1]],
+        weight_grad[:, w_qkv.shape[1] :],
+        ours[:, :3],
+        ours[:, 3:],
+        small[10, :HEADS],
+        fc1_grad,
+        fc2_grad,
+        mid_gain_grad,
+        ffn_bias_grad,
+    )
+
+
+def layer(nz, nt, tokens, out_grad, doc_lengths, w_qkv, *rest):
+    if nt == 8 and nz > 1 and w_qkv.shape[0] % 16 == 0:
+        return fused(nz, tokens, out_grad, doc_lengths, w_qkv, *rest)
+    return plain(tokens, out_grad, doc_lengths, w_qkv, *rest)
+
+
 def solution(mesh):
     return jax.shard_map(
-        local,
+        functools.partial(layer, mesh.shape["dp"], mesh.shape["tensor"]),
         mesh=mesh,
         in_specs=(
             P(("dp", "tensor"), None),

time: 1070 us -> 416 us (0.39)
  waiting for transfers between devices: 754 us -> 0 us
  Pallas kernels: 0 us -> 261 us
  blocking collectives: 156 us -> 0 us
  between operations: 14.6 us -> 1.37 us
  local copies, waits for them, and re-layouts: 15.7 us -> 27 us
    reduce_scatter x6 -> x0, waiting for transfers between devices: 378 us -> none  [the longest x1 158 us: local(): lax.psum_scatter(qkv_local, ('dp', 'tensor'), scatter_dimension=0, tiled=...]
    pallas_call x0 -> x5, Pallas kernels: none -> 261 us  [the longest x1 87.7 us: gather(): pl.pallas_call(functools.partial(gather_kernel, nz), name='gather', out_s...]
    unnamed x16 -> x0, waiting for transfers between devices: 222 us -> none
    all_gather x6 -> x0, waiting for transfers between devices: 154 us -> none  [the longest x1 38.6 us: local(): gathered = lax.all_gather(normed_mid, 'tensor', axis=0, tiled=True)]
    all_gather x2 -> x0, blocking collectives: 80.6 us -> none  [the longest x1 43.3 us: local(): lax.all_gather(gains.astype(jnp.bfloat16), ('dp', 'tensor'), axis=0, tile...]
    psum x4 -> x0, blocking collectives: 75.5 us -> none  [the longest x1 37 us: local(): scale_grad = lax.psum(scale_local, ('dp', 'tensor'))]
  transfers between devices with their start and end apart: 14 -> 0, of which waited for: 11 -> 0; matrix products, arithmetic and copies ran while one was open for 10% -> 0% of each run, Pallas kernels for 0% -> 0%
where the time goes in v1:
time: 416 us; the launch traced here: 409 us
  Pallas kernels  261 us (63%)
  matrix products  90.7 us (22%)
  other arithmetic  28.9 us (7%)
  local copies, waits for them, and re-layouts  27 us (6%)
    pallas_call x1, Pallas kernels, gather(): pl.pallas_call(functools.partial(gather_kernel, nz), name='gather', out_s...  87.7 us
    pallas_call x1, Pallas kernels, total_all(): pl.pallas_call(functools.partial(total_kernel, nz), name='total_all', out...  69.1 us
    pallas_call x1, Pallas kernels, fold(): pl.pallas_call(functools.partial(fold_kernel, nz, pieces), name='fold', o...  60.6 us
    pallas_call x1, Pallas kernels, spread_rows(): pl.pallas_call(spread_kernel, name='spread_rows', out_shape=jax.ShapeDtyp...  33.9 us
    dot_general x1, matrix products, fused(): jnp.dot(gathered, fc1_rows, preferred_element_type=jnp.float32)  10.2 us
    dot_general x1, matrix products, attend_backward(): jnp.einsum('hqk,qhd->khd', grad_scores, query_rows, preferred_element_typ...  9.7 us
    dot_general x1, matrix products, attend_backward(): jnp.einsum('hqk,khd->qhd', grad_scores, key_rows, preferred_element_type=...  9.65 us
    pallas_call x1, Pallas kernels, tensor_sums(): pl.pallas_call(sums_kernel, name='tensor_sums', out_shape=jax.ShapeDtypeS...  9.39 us

profile of v1, /device:TPU:0, one launch (start us, length us, event | category | flops | bytes accessed | tf_op | source)
XLA Modules:
  0.0 408.7 jit_solution(3967989728360961786)
XLA Ops:
  6.9 87.7 %gather.1 = (bf16[4,2,2,2,32,3072]{5,4,3,2,1,0:T(8,128)(2,1)}, bf16[4,2,2,2,32,1024]{5,4,3,2,1,0:T(8,128)(2,1)}, f32[4,2,2,2,32,128]{5,4,3,2,1,0:T(8,128)}, bf16...) custom-call(bf16[32,3072]{1,0:T(8,128)(2,1)} %qkv_ref.1, ...), custom_call_target="tpu_custom_call" | custom-call | tf_op jit(solution)/shard_map/gather/pallas_call | solution.py:465
  95.9 4.9 %fusion.9 = bf16[256,3072]{1,0:T(8,128)(2,1)S(1)} fusion(bf16[1024,3072]{1,0:T(8,128)(2,1)} %bitcast.176, f32[3072]{0:T(1024)S(1)} %pad_maximum_fusion.2, bf16[256,1024]{1,0:T(8,128)(2,1)} %param.20, f32[1024]{0:T(1024)S(1)} %bitcast.168, f32[1024]{0:T(1024)S(1)} %bitcast.140, f32[256]{0:T(256)S(1)} %get-tuple-element.138, f32[256]{0:T(256)S(1)} %get-tuple-element.137), kind=kOutput, calls=%fused_computation.27 | convolution fusion | flops 1613758464 | bytes 8411136 | tf_op jit(solution)/shard_map/dot_general | solution.py:905
  102.0 6.6 %fusion.81 = (f32[512]{0:T(512)S(1)}, f32[2048,512]{1,0:T(8,128)}) fusion(bf16[2048,1024]{1,0:T(8,128)(2,1)} %bitcast.178, bf16[512,1024]{1,0:T(8,128)(2,1)S(1)} %copy-done.24), kind=kOutput, calls=%fused_computation.136 | convolution fusion | flops 2148531712 | bytes 9439232 | tf_op jit(solution)/shard_map/rd,fd->rf/dot_general | solution.py:923
  108.6 5.6 %copy.65 = f32[2048,512]{0,1:T(8,128)} copy(f32[2048,512]{1,0:T(8,128)} %get-tuple-element.146) | data formatting | bytes 8388608 | tf_op jit(solution)/shard_map/rd,fd->rf/dot_general | solution.py:923
  116.1 2.4 fusion.48
  118.5 2.6 copy.71
  125.6 33.9 %spread_rows.1 = bf16[2,2,2,256,1024]{4,3,2,1,0:T(8,128)(2,1)} custom-call(bf16[256,1024]{1,0:T(8,128)(2,1)} %add_convert_fusion.2.rows_ref), custom_call_target="tpu_custom_call" | custom-call | tf_op jit(solution)/shard_map/spread_rows/pallas_call | solution.py:528
  159.5 10.2 %multiply_reduce_fusion.2 = (f32[2048]{0:T(1024)S(1)}, f32[2048]{0:T(1024)S(1)}, f32[2048]{0:T(1024)S(1)}, f32[2048]{0:T(1024)S(1)}, f32[2048,512]{0,1:T(8,128)}) fusion(f32[2048,512]{0,1:T(8,128)} %copy.65, f32[512]{0:T(512)S(1)} %copy-done.21, f32[512]{0:T(512)S(1)} %bitcast.160, bf16[2048,1024]{1,0:T(8,128)(2,1)} %bitcast.102, ...), kind=kOutput, calls=%fused_computation.20 | convolution fusion | flops 2164252672 | bytes 13668352 | tf_op jit(solution)/shard_map/dot_general | solution.py:921
  170.4 9.4 %tensor_sums.1 = f32[8,2048]{1,0:T(8,128)} custom-call(f32[8,2048]{1,0:T(8,128)} %stack.62.mine_ref), custom_call_target="tpu_custom_call" | custom-call | tf_op jit(solution)/shard_map/tensor_sums/pallas_call | solution.py:559
  180.7 8.5 %convolution_convert_fusion.4.fc2_ref = bf16[512,1024]{1,0:T(8,128)(2,1)} fusion(bf16[2048,1024]{1,0:T(8,128)(2,1)} %bitcast.179, f32[512]{0:T(512)S(1)} %bitcast.174, f32[2048]{0:T(1024)S(1)} %bitcast.126, f32[2048]{0:T(1024)S(1)} %get-tuple-element.127, f32[512]{0:T(512)S(1)} %copy-done.21, f32[2048,512]{0,1:T(8,128)} %get-tuple-element.144, ...), kind=kOutput, calls=%fused_computation.47 | convolution fusion | flops 2162688000 | bytes 9459712 | tf_op jit(solution)/shard_map/rf,rd->fd/dot_general | solution.py:943
  189.3 6.5 %convert_reduce_fusion = (f32[512]{0:T(512)S(1)}, bf16[2048,512]{0,1:T(8,128)(2,1)S(1)}, f32[512]{0:T(512)S(1)}) fusion(f32[2048]{0:T(1024)S(1)} %get-tuple-element.128, f32[2048]{0:T(1024)S(1)} %bitcast.127, f32[2048,512]{0,1:T(8,128)S(1)} %copy-done.9, f32[512]{0:T(512)S(1)} %bitcast.162, f32[2048]{0:T(1024)S(1)} %bitcast.130, ...), kind=kLoop, calls=%fused_computation.16 | loop fusion | flops 34601984 | bytes 10526720 | tf_op jit(solution)/shard_map/reduce_sum | solution.py:954
  195.7 5.4 %convolution_convert_fusion.1 = bf16[2048,1024]{1,0:T(8,128)(2,1)} fusion(bf16[512,1024]{1,0:T(8,128)(2,1)S(1)} %copy-done.25, f32[512]{0:T(512)S(1)} %bitcast.175, f32[2048]{0:T(1024)S(1)} %bitcast.128, f32[2048]{0:T(1024)S(1)} %get-tuple-element.127, f32[512]{0:T(512)S(1)} %copy-done.21, f32[2048,512]{0,1:T(8,128)S(1)} %copy-done.9, f32[512]{0:T(512)S(1)} %bitcast.163), kind=kOutput, calls=%fused_computation.28 | convolution fusion | flops 2164260864 | bytes 9459712 | tf_op jit(solution)/shard_map/dot_general | solution.py:942
  201.2 3.4 convolution_convert_fusion.5.fc1_ref
  205.2 4.4 %convolution_convert_fusion.2 = bf16[2048,1024]{1,0:T(8,128)(2,1)} fusion(bf16[2048,512]{0,1:T(8,128)(2,1)S(1)} %get-tuple-element.103, bf16[1024,512]{1,0:T(8,128)(2,1)S(1)} %copy-done.23), kind=kOutput, calls=%fused_computation.29 | convolution fusion | flops 2149580800 | bytes 7340032 | tf_op jit(solution)/shard_map/rf,df->rd/dot_general | solution.py:949
  209.6 60.6 %fold.1 = (f32[256,1024]{1,0:T(8,128)}, f32[256,1024]{1,0:T(8,128)}, f32[256,512]{1,0:T(8,128)}, f32[512,256]{1,0:T(8,128)}, f32[8,512]{1,0:T(8,128)}) custom-call(bf16[2,2,2,256,1024]{4,3,2,1,0:T(8,128)(2,1)} %bitcast.101, bf16[2,2,2,256,1024]{4,3,2,1,0:T(8,128)(2,1)} %bitcast.100, bf16[1024,512]{1,0:T(8,128)(2,1)} %convolution_convert_fusion.5.fc1_ref, ...), custom_call_target="tpu_custom_call" | custom-call | tf_op jit(solution)/shard_map/fold/pallas_call | solution.py:701
  274.6 3.4 multiply_reduce_fusion.7
  279.5 4.3 %fusion.25 = bf16[16,64,256]{2,1,0:T(8,128)(2,1)} fusion(bf16[256,16,64]{0,2,1:T(8,128)(2,1)S(1)} %bitcast.106, f32[16,256,256]{1,2,0:T(8,128)} %copy-done, f32[16,256]{1,0:T(8,128)S(1)} %log_add_fusion, pred[256,256]{0,1:T(8,128)(4,1)S(1)} %fusion.50), kind=kOutput, calls=%fused_computation.52 | convolution fusion | flops 139722752 | bytes 5324800 | tf_op jit(solution)/shard_map/hqk,qhd->khd/dot_general | solution.py:80
  285.8 3.9 fusion.82
  289.7 9.7 %fusion.28 = bf16[16,64,256]{2,1,0:T(8,128)(2,1)} fusion(bf16[256,16,64]{0,2,1:T(8,128)(2,1)} %bitcast.111, f32[16,256,256]{1,2,0:T(8,128)} %fusion.82, f32[16,256,256]{1,2,0:T(8,128)} %copy-done, f32[16,256]{1,0:T(8,128)S(1)} %log_add_fusion, pred[256,256]{0,1:T(8,128)(4,1)S(1)} %fusion.50), kind=kOutput, calls=%fused_computation.53 | convolution fusion | flops 148115712 | bytes 9519104 | tf_op jit(solution)/shard_map/hqk,khd->qhd/dot_general | solution.py:74
  299.3 9.7 %fusion.31 = bf16[16,64,256]{2,1,0:T(8,128)(2,1)} fusion(bf16[256,16,64]{0,2,1:T(8,128)(2,1)} %bitcast.109, f32[16,256,256]{1,2,0:T(8,128)} %fusion.82, f32[16,256,256]{1,2,0:T(8,128)} %copy-done, f32[16,256]{1,0:T(8,128)S(1)} %log_add_fusion, pred[256,256]{0,1:T(8,128)(4,1)S(1)} %fusion.50), kind=kOutput, calls=%fused_computation.54 | convolution fusion | flops 148115712 | bytes 9519104 | tf_op jit(solution)/shard_map/hqk,qhd->khd/dot_general | solution.py:77
  309.0 5.6 %fusion.45 = (f32[1024]{0:T(1024)S(1)}, f32[256]{0:T(256)S(1)}, f32[256]{0:T(256)S(1)}, f32[1024]{0:T(1024)S(1)}, f32[256,1024]{1,0:T(8,128)S(1)}) fusion(bf16[256,1024]{1,0:T(8,128)(2,1)} %param.20, f32[256]{0:T(256)S(1)} %get-tuple-element.138, f32[256]{0:T(256)S(1)} %get-tuple-element.137, f32[1024]{0:T(1024)S(1)} %bitcast.141, ...), kind=kOutput, calls=%fused_computation.66 | convolution fusion | flops 1617950208 | bytes 9453568 | tf_op jit(solution)/shard_map/te,de->td/dot_general | solution.py:999
  317.9 6.3 %convolution_convert_fusion = bf16[1024,3072]{1,0:T(8,128)(2,1)} fusion(bf16[256,1024]{1,0:T(8,128)(2,1)} %param.20, f32[1024]{0:T(1024)S(1)} %bitcast.169, f32[1024]{0:T(1024)S(1)} %bitcast.143, f32[256]{0:T(256)S(1)} %get-tuple-element.138, f32[256]{0:T(256)S(1)} %get-tuple-element.137, bf16[256,1024]{0,1:T(8,128)(2,1)} %bitcast.114, ...), kind=kOutput, calls=%fused_computation.4 | convolution fusion | flops 1620049920 | bytes 8398848 | tf_op jit(solution)/shard_map/td,te->de/dot_general | solution.py:996
  324.2 7.0 %pad_maximum_fusion = bf16[1024,4096]{1,0:T(8,128)(2,1)} fusion(bf16[1024,1024]{1,0:T(8,128)(2,1)S(1)} %convolution_convert_fusion.3, bf16[1024,3072]{1,0:T(8,128)(2,1)} %convolution_convert_fusion), kind=kLoop, calls=%fused_computation.1 | loop fusion | flops 16777216 | bytes 16777216 | tf_op jit(solution)/shard_map/concatenate | solution.py:1022
  331.2 69.1 %total_all.1 = (f32[32,4096]{1,0:T(8,128)}, f32[16,1024]{1,0:T(8,128)}) custom-call(bf16[4,2,2,2,32,4096]{5,4,3,2,1,0:T(8,128)(2,1)} %bitcast.97, f32[16,1024]{1,0:T(8,128)} %stack.75.small_ref), custom_call_target="tpu_custom_call" | custom-call | tf_op jit(solution)/shard_map/total_all/pallas_call | solution.py:836
  (119 shorter events, 36.3 us)
Async XLA Ops:
  101.2 13.1 %copy-start.15 = (bf16[256,1024]{0,1:T(8,128)(2,1)}, bf16[256,1024]{0,1:T(8,128)(2,1)S(1)}, u32[]{:S(2)}) copy-start(bf16[256,1024]{0,1:T(8,128)(2,1)S(1)} %copy.63) | copy-start | bytes 1572868
  101.4 12.9 %copy-start.14 = (bf16[256,1024]{0,1:T(8,128)(2,1)}, bf16[256,1024]{0,1:T(8,128)(2,1)S(1)}, u32[]{:S(2)}) copy-start(bf16[256,1024]{0,1:T(8,128)(2,1)S(1)} %copy.62) | copy-start | bytes 1572868
  101.6 14.4 %copy-start.10 = (bf16[256,1024]{0,1:T(8,128)(2,1)}, bf16[256,1024]{0,1:T(8,128)(2,1)S(1)}, u32[]{:S(2)}) copy-start(bf16[256,1024]{0,1:T(8,128)(2,1)S(1)} %copy.61) | copy-start | bytes 1572868
  115.2 3.3 copy-start
  116.1 5.0 %copy-start.4 = (bf16[4,2,2,2,32,1024]{5,4,3,2,1,0:T(8,128)(2,1)S(1)}, bf16[4,2,2,2,32,1024]{5,4,3,2,1,0:T(8,128)(2,1)}, u32[]{:S(2)}) copy-start(bf16[4,2,2,2,32,1024]{5,4,3,2,1,0:T(8,128)(2,1)} %get-tuple-element.66) | copy-start | bytes 6291460
  123.0 36.5 %copy-start.21 = (f32[512]{0:T(512)S(1)}, f32[512]{0:T(512)}, u32[]{:S(2)}) copy-start(f32[512]{0:T(512)} %param.30) | copy-start | bytes 6148
  180.7 8.5 %copy-start.1 = (f32[2048,512]{0,1:T(8,128)S(1)}, f32[2048,512]{0,1:T(8,128)}, u32[]{:S(2)}) copy-start(f32[2048,512]{0,1:T(8,128)} %copy.65) | copy-start | bytes 12582916
  180.7 8.5 %copy-start.9 = (f32[2048,512]{0,1:T(8,128)S(1)}, f32[2048,512]{0,1:T(8,128)}, u32[]{:S(2)}) copy-start(f32[2048,512]{0,1:T(8,128)} %get-tuple-element.144) | copy-start | bytes 12582916
  189.2 6.5 %copy-start.25 = (bf16[512,1024]{1,0:T(8,128)(2,1)S(1)}, bf16[512,1024]{1,0:T(8,128)(2,1)}, u32[]{:S(2)}) copy-start(bf16[512,1024]{1,0:T(8,128)(2,1)} %get-tuple-element.69) | copy-start | bytes 3145732
  195.7 5.4 %copy-start.8 = (bf16[2,2,2,256,1024]{4,3,2,1,0:T(8,128)(2,1)S(1)}, bf16[2,2,2,256,1024]{4,3,2,1,0:T(8,128)(2,1)}, u32[]{:S(2)}) copy-start(bf16[2,2,2,256,1024]{4,3,2,1,0:T(8,128)(2,1)} %spread_rows.1) | copy-start | bytes 12582916
  201.2 4.0 copy-start.23
  209.6 64.9 %copy-start.13 = (bf16[256,1024]{1,0:T(8,128)(2,1)S(1)}, bf16[256,1024]{1,0:T(8,128)(2,1)}, u32[]{:S(2)}) copy-start(bf16[256,1024]{1,0:T(8,128)(2,1)} %grad_ref.1) | copy-start | bytes 1572868
  274.5 3.8 copy-start.2
  274.5 3.8 copy-start.5
  278.3 5.5 %copy-start.7 = (bf16[256,1024]{1,0:T(8,128)(2,1)}, bf16[256,1024]{1,0:T(8,128)(2,1)S(1)}, u32[]{:S(2)}) copy-start(bf16[256,1024]{1,0:T(8,128)(2,1)S(1)} %get-tuple-element.100) | copy-start | bytes 1572868
  279.5 4.3 %copy-start.12 = (bf16[256,1024]{0,1:T(8,128)(2,1)}, bf16[256,1024]{0,1:T(8,128)(2,1)S(1)}, u32[]{:S(2)}) copy-start(bf16[256,1024]{0,1:T(8,128)(2,1)S(1)} %copy.67) | copy-start | bytes 1572868
  279.5 4.3 %copy-start.3 = (f32[256,1024]{1,0:T(8,128)S(1)}, f32[256,1024]{1,0:T(8,128)}, u32[]{:S(2)}) copy-start(f32[256,1024]{1,0:T(8,128)} %copy.71) | copy-start | bytes 3145732
  279.5 6.3 %copy-start.11 = (bf16[256,1024]{0,1:T(8,128)(2,1)S(1)}, bf16[256,1024]{0,1:T(8,128)(2,1)}, u32[]{:S(2)}) copy-start(bf16[256,1024]{0,1:T(8,128)(2,1)} %copy-done.10) | copy-start | bytes 1572868
  309.0 5.6 %copy-start.6 = (bf16[256,1024]{1,0:T(8,128)(2,1)S(1)}, bf16[256,1024]{1,0:T(8,128)(2,1)}, u32[]{:S(2)}) copy-start(bf16[256,1024]{1,0:T(8,128)(2,1)} %param.20) | copy-start | bytes 1572868
  309.0 7.0 %copy-start.16 = (bf16[16,64,256]{2,1,0:T(8,128)(2,1)S(1)}, bf16[16,64,256]{2,1,0:T(8,128)(2,1)}, u32[]{:S(2)}) copy-start(bf16[16,64,256]{2,1,0:T(8,128)(2,1)} %fusion.25) | copy-start | bytes 1572868
  309.0 7.0 %copy-start.17 = (bf16[16,64,256]{2,1,0:T(8,128)(2,1)S(1)}, bf16[16,64,256]{2,1,0:T(8,128)(2,1)}, u32[]{:S(2)}) copy-start(bf16[16,64,256]{2,1,0:T(8,128)(2,1)} %fusion.28) | copy-start | bytes 1572868
  309.0 7.0 %copy-start.18 = (bf16[16,64,256]{2,1,0:T(8,128)(2,1)S(1)}, bf16[16,64,256]{2,1,0:T(8,128)(2,1)}, u32[]{:S(2)}) copy-start(bf16[16,64,256]{2,1,0:T(8,128)(2,1)} %fusion.31) | copy-start | bytes 1572868
  331.2 75.6 %copy-start.20 = (f32[256,512]{1,0:T(8,128)S(1)}, f32[256,512]{1,0:T(8,128)}, u32[]{:S(2)}) copy-start(f32[256,512]{1,0:T(8,128)} %get-tuple-element.168) | copy-start | bytes 1572868
  331.2 76.4 %copy-start.19 = (f32[512,256]{1,0:T(8,128)S(1)}, f32[512,256]{1,0:T(8,128)}, u32[]{:S(2)}) copy-start(f32[512,256]{1,0:T(8,128)} %get-tuple-element.169) | copy-start | bytes 1572868
  (2 other events, 3.0 us)

commit v2 on v1

--- a/solution.py
+++ b/solution.py
@@ -484,108 +484,319 @@
     )(w_qkv, w_out, vectors, w_fc1, w_fc2, out_grad)
 
 
-def spread_kernel(rows_ref, all_ref, local_sem, send_sems, recv_sems):
+def add_low(left, right):
+    return (left.astype(jnp.float32) + right.astype(jnp.float32)).astype(jnp.bfloat16)
+
+
+SQRT_2_PI = math.sqrt(2.0 / math.pi)
+NT = (((1,), (1,)), ((), ()))
+TN = (((0,), (0,)), ((), ()))
+
+
+def dot(left, right, dims=None):
+    if dims is None:
+        return jnp.dot(left, right, preferred_element_type=jnp.float32)
+    return lax.dot_general(left, right, dims, preferred_element_type=jnp.float32)
+
+
+def ffn_kernel(
+    mid_ref,
+    og_ref,
+    fc1_ref,
+    fc2_ref,
+    unit_ref,
+    gnm_out,
+    ffn_part,
+    fc1_part,
+    fc2_part,
+    unit_out,
+    mid_all,
+    act,
+    slope,
+    grad,
+    hidden,
+    grad_pre,
+    mid_part,
+    pre,
+    columns,
+    stats,
+    pair,
+    got,
+    totals,
+    from_core,
+    sums,
+    from_one,
+    from_two,
+    local_sem,
+    send_sems,
+    recv_sems,
+):
     z, y, x, c = place()
     to_x, to_y, to_c = at(z, y, 1 - x, c), at(z, 1 - y, x, c), at(z, y, x, 1 - c)
-    greet([to_x, to_y, to_c])
+    to_xy = at(z, 1 - y, 1 - x, c)
+    greet([to_x, to_y, to_c, to_xy])
     sends = Sends(send_sems, recv_sems)
-    half = rows_ref.shape[1] // 2
+    rows = mid_ref.shape[0]
+    width = mid_ref.shape[1]
+    units = fc1_ref.shape[1]
+    half = rows // 2
     lo, hi = pl.ds(0, half), pl.ds(half, half)
-    pieces = 4
-    rows = rows_ref.shape[0] // pieces
-    mine = pltpu.make_async_copy(rows_ref, all_ref.at[y, x, c], local_sem)
+    one_x = sends.start(mid_ref.at[lo], mid_all.at[y, x, c, lo], to_x)
+    one_y = sends.start(mid_ref.at[hi], mid_all.at[y, x, c, hi], to_y)
+    own_c = sends.start(mid_ref, mid_all.at[y, x, c], to_c)
+    two_y = sends.start(mid_ref.at[lo], mid_all.at[y, x, c, lo], to_y)
+    two_x = sends.start(mid_ref.at[hi], mid_all.at[y, x, c, hi], to_x)
+    mine = pltpu.make_async_copy(mid_ref, mid_all.at[y, x, c], local_sem)
     mine.start()
-    stage = []
-    for k in range(pieces):
-        part = pl.ds(k * rows, rows)
-        stage.append(
-            (
-                sends.start(rows_ref.at[part, lo], all_ref.at[y, x, c, part, lo], to_x),
-                sends.start(rows_ref.at[part, hi], all_ref.at[y, x, c, part, hi], to_y),
+    step = 32
+    lane = lax.broadcasted_iota(jnp.int32, (step, 128), 1)
+
+    def grads(yy, xx, cc):
+        grad[yy, xx, cc] = dot(og_ref[yy, xx, cc], fc2_ref[...], NT)
+
+    def forward(yy, xx, cc):
+        pre[...] = dot(mid_all[yy, xx, cc], fc1_ref[...])
+
+        def block(k, carry):
+            part = pl.ds(pl.multiple_of(k * step, step), step)
+            u = pre[part] + unit_ref[0:1]
+            square = u * u
+            th = jnp.tanh(SQRT_2_PI * u * (1.0 + 0.044715 * square))
+            lift = 0.5 + 0.5 * th
+            a = u * lift
+            act[yy, xx, cc, part] = a
+            slope[yy, xx, cc, part] = lift + (0.5 * SQRT_2_PI) * u * (1.0 - th * th) * (
+                1.0 + (3 * 0.044715) * square
             )
-        )
+            gm = grad[yy, xx, cc, part] * unit_ref[1:2]
+            four = [
+                jnp.sum(a, axis=1, keepdims=True),
+                jnp.sum(a * a, axis=1, keepdims=True),
+                jnp.sum(gm, axis=1, keepdims=True),
+                jnp.sum(gm * a, axis=1, keepdims=True),
+            ]
+            tile = jnp.where(lane == 0, four[0], 0.0)
+            for j in range(1, 4):
+                tile = jnp.where(lane == j, four[j], tile)
+            columns[part] = tile
+            return carry
+
+        lax.fori_loop(0, rows // step, block, 0)
+        stats[yy, xx, cc] = columns[...].T[:8]
+
+    grads(y, x, c)
     mine.wait()
-    later = []
-    for k in range(pieces):
-        part = pl.ds(k * rows, rows)
-        for copy in stage[k]:
-            copy.wait_recv()
-        one, two = all_ref.at[y, :, c, part, lo], all_ref.at[:, x, c, part, hi]
-        later.append((sends.start(one, one, to_y), sends.start(two, two, to_x)))
-    last = []
-    for k in range(pieces):
-        part = pl.ds(k * rows, rows)
-        for copy in later[k]:
-            copy.wait_recv()
-        all_four = all_ref.at[:, :, c, part]
-        last.append(sends.start(all_four, all_four, to_c))
-    for copy in last:
+    forward(y, x, c)
+    grads(y, x, 1 - c)
+    grads(y, 1 - x, c)
+    one_x.wait_recv()
+    one_y.wait_recv()
+    ref_x, ref_y = mid_all.at[y, 1 - x, c, lo], mid_all.at[1 - y, x, c, hi]
+    three_y = sends.start(ref_x, ref_x, to_y)
+    three_x = sends.start(ref_y, ref_y, to_x)
+    c_one = [sends.start(ref_x, ref_x, to_c), sends.start(ref_y, ref_y, to_c)]
+    grads(1 - y, x, c)
+    own_c.wait_recv()
+    forward(y, x, 1 - c)
+    grads(y, 1 - x, 1 - c)
+    grads(1 - y, x, 1 - c)
+    two_x.wait_recv()
+    two_y.wait_recv()
+    ref_x, ref_y = mid_all.at[y, 1 - x, c, hi], mid_all.at[1 - y, x, c, lo]
+    c_two = [sends.start(ref_x, ref_x, to_c), sends.start(ref_y, ref_y, to_c)]
+    forward(y, 1 - x, c)
+    forward(1 - y, x, c)
+    grads(1 - y, 1 - x, c)
+    grads(1 - y, 1 - x, 1 - c)
+    for copy in c_one + c_two:
         copy.wait_recv()
-    sends.finish()
-
-
-def spread_rows(rows):
-    return pl.pallas_call(
-        spread_kernel,
-        name="spread_rows",
-        out_shape=jax.ShapeDtypeStruct((2, 2, 2) + rows.shape, rows.dtype),
-        in_specs=[ANY],
-        out_specs=ANY,
-        scratch_shapes=[
-            pltpu.SemaphoreType.DMA,
-            pltpu.SemaphoreType.DMA((20,)),
-            pltpu.SemaphoreType.DMA((20,)),
-        ],
-        compiler_params=pltpu.CompilerParams(collective_id=2, has_side_effects=True),
-    )(rows)
-
-
-def sums_kernel(mine_ref, total_ref, pair, got, send_sems, recv_sems):
-    z, y, x, c = place()
-    to_c = at(z, y, x, 1 - c)
-    planes = [at(z, y, 1 - x, c), at(z, 1 - y, x, c), at(z, 1 - y, 1 - x, c)]
-    greet([to_c] + planes)
-    sends = Sends(send_sems, recv_sems)
-    sends.start(mine_ref, got.at[3], to_c).wait_recv()
-    pair[...] = mine_ref[...] + got[3]
-    arrivals = [sends.start(pair, got.at[k], plane) for k, plane in enumerate(planes)]
+    forward(y, 1 - x, 1 - c)
+    three_x.wait_recv()
+    three_y.wait_recv()
+    ref_xy = mid_all.at[1 - y, 1 - x, c]
+    c_three = sends.start(ref_xy, ref_xy, to_c)
+    forward(1 - y, x, 1 - c)
+    forward(1 - y, 1 - x, c)
+    c_three.wait_recv()
+    forward(1 - y, 1 - x, 1 - c)
+
+    sends.start(stats, got.at[3], to_c).wait_recv()
+    pair[...] = stats[...] + got[3]
+    arrivals = [
+        sends.start(pair, got.at[k], plane) for k, plane in enumerate((to_x, to_y, to_xy))
+    ]
     for copy in arrivals:
         copy.wait_recv()
-    total_ref[...] = (pair[...] + got[0]) + (got[1] + got[2])
+    total = (pair[...] + got[0]) + (got[1] + got[2])
+    total = total * (1.0 / (units * 8))
+    center, second = total[:, :, :, 0:1], total[:, :, :, 1:2]
+    first, cross = total[:, :, :, 2:3], total[:, :, :, 3:4]
+    inverse = lax.rsqrt(second - center * center + EPS)
+    totals[:, :, :, 0:1] = center
+    totals[:, :, :, 1:2] = inverse
+    totals[:, :, :, 2:3] = first
+    totals[:, :, :, 3:4] = inverse * (cross - center * first)
+    totals[:, :, :, 4:8] = jnp.zeros_like(total[:, :, :, 4:8])
+    unit_out[...] = jnp.zeros_like(unit_out)
+
+    def backward(yy, xx, cc):
+        columns[...] = jnp.concatenate(
+            [totals[yy, xx, cc], jnp.zeros((120, rows), jnp.float32)], axis=0
+        ).T
+
+        def block(k, carry):
+            part = pl.ds(pl.multiple_of(k * step, step), step)
+            center, inverse = columns[part, 0:1], columns[part, 1:2]
+            first, second = columns[part, 2:3], columns[part, 3:4]
+            gain = unit_ref[1:2]
+            g = grad[yy, xx, cc, part]
+            normed = (act[yy, xx, cc, part] - center) * inverse
+            hidden[yy, xx, cc, part] = (normed * gain + unit_ref[2:3]).astype(jnp.bfloat16)
+            back = inverse * (g * gain - first - normed * second)
+            low = (back * slope[yy, xx, cc, part]).astype(jnp.bfloat16)
+            grad_pre[yy, xx, cc, part] = low
+            eight = (step // 8, 8, units)
+            return (
+                carry[0] + jnp.sum((g * normed).reshape(eight), axis=0),
+                carry[1] + jnp.sum(low.astype(jnp.float32).reshape(eight), axis=0),
+                carry[2] + jnp.sum(g.reshape(eight), axis=0),
+            )
+
+        zero = jnp.zeros((8, units), jnp.float32)
+        parts = lax.fori_loop(0, rows // step, block, (zero, zero, zero))
+        for j, part in enumerate(parts):
+            unit_out[j : j + 1] += jnp.sum(part, axis=0, keepdims=True)
+        mid_part[yy, xx, cc] = dot(grad_pre[yy, xx, cc], fc1_ref[...], NT).astype(jnp.bfloat16)
+
+    left, right = pl.ds(0, width // 2), pl.ds(width // 2, width // 2)
+    order = [(1 - y, 1 - x), (y, 1 - x), (1 - y, x), (y, x)]
+    cores = []
+    for yy, xx in order:
+        backward(yy, xx, 1 - c)
+        cores.append(sends.start(mid_part.at[yy, xx, 1 - c], from_core.at[yy, xx], to_c))
+    stage_x, stage_y = [], []
+    for k, (yy, xx) in enumerate(order):
+        backward(yy, xx, c)
+        cores[k].wait_recv()
+        sums[yy, xx] = add_low(mid_part[yy, xx, c], from_core[yy, xx])
+        if k in (0, 1):
+            stage_x.append(
+                sends.start(sums.at[yy, xx, :, left], from_one.at[0, yy, :, left], to_x)
+            )
+        if k in (0, 2):
+            stage_y.append(
+                sends.start(sums.at[yy, xx, :, right], from_one.at[1, xx, :, right], to_y)
+            )
+
+    def ffn_of(yy, xx, cc):
+        ffn_part[yy, xx, cc] = dot(hidden[yy, xx, cc], fc2_ref[...]).astype(jnp.bfloat16)
+
+    for yy, xx in order[:2]:
+        ffn_of(yy, xx, 1 - c)
+        ffn_of(yy, xx, c)
+    for copy in (stage_x[0], stage_y[0]):
+        copy.wait_recv()
+    sums[1 - y, x, :, left] = add_low(sums[1 - y, x, :, left], from_one[0, 1 - y, :, left])
+    sums[y, 1 - x, :, right] = add_low(sums[y, 1 - x, :, right], from_one[1, 1 - x, :, right])
+    last_y = sends.start(sums.at[1 - y, x, :, left], from_two.at[:, left], to_y)
+    last_x = sends.start(sums.at[y, 1 - x, :, right], from_two.at[:, right], to_x)
+    for yy, xx in order[2:]:
+        ffn_of(yy, xx, 1 - c)
+        ffn_of(yy, xx, c)
+    blocks = 4
+
+    def fc1_block(k, carry):
+        part = pl.ds(pl.multiple_of(k * (width // blocks), 128), width // blocks)
+        block = jnp.zeros((width // blocks, units), jnp.float32)
+        for j in range(8):
+            yxc = (j // 4, (j // 2) % 2, j % 2)
+            block = block + dot(mid_all[(*yxc, slice(None), part)], grad_pre[yxc], TN)
+        fc1_part[part] = block.astype(jnp.bfloat16)
+        return carry
+
+    def fc2_block(k, carry):
+        part = pl.ds(pl.multiple_of(k * (width // blocks), 128), width // blocks)
+        block = jnp.zeros((units, width // blocks), jnp.float32)
+        for j in range(8):
+            yxc = (j // 4, (j // 2) % 2, j % 2)
+            block = block + dot(hidden[yxc], og_ref[(*yxc, slice(None), part)], TN)
+        fc2_part[:, part] = block.astype(jnp.bfloat16)
+        return carry
+
+    lax.fori_loop(0, blocks, fc1_block, 0)
+    for copy in (stage_x[1], stage_y[1]):
+        copy.wait_recv()
+    lax.fori_loop(0, blocks, fc2_block, 0)
+    last_x.wait_recv()
+    last_y.wait_recv()
+    own = sums[y, x].astype(jnp.float32)
+    gnm_out[:, left] = (
+        own[:, : width // 2]
+        + from_one[0, y, :, left].astype(jnp.float32)
+        + from_two[:, left].astype(jnp.float32)
+    )
+    gnm_out[:, right] = (
+        own[:, width // 2 :]
+        + from_one[1, x, :, right].astype(jnp.float32)
+        + from_two[:, right].astype(jnp.float32)
+    )
     sends.finish()
 
 
-def tensor_sums(mine):
+def ffn(mid, og_all, fc1, fc2, unit_rows):
+    rows, width = mid.shape
+    units = fc1.shape[1]
+    low, plane = jnp.bfloat16, (2, 2, 2)
+    sds = jax.ShapeDtypeStruct
+    count = 32
     return pl.pallas_call(
-        sums_kernel,
-        name="tensor_sums",
-        out_shape=jax.ShapeDtypeStruct(mine.shape, mine.dtype),
-        in_specs=[IN_VMEM],
-        out_specs=IN_VMEM,
+        ffn_kernel,
+        name="ffn",
+        out_shape=(
+            sds((rows, width), jnp.float32),
+            sds(plane + (rows, width), low),
+            sds(fc1.shape, low),
+            sds(fc2.shape, low),
+            sds((8, units), jnp.float32),
+        ),
+        in_specs=[IN_VMEM] * 5,
+        out_specs=[IN_VMEM] * 5,
         scratch_shapes=[
-            pltpu.VMEM(mine.shape, mine.dtype),
-            pltpu.VMEM((4,) + mine.shape, mine.dtype),
-            pltpu.SemaphoreType.DMA((4,)),
-            pltpu.SemaphoreType.DMA((4,)),
+            pltpu.VMEM(plane + (rows, width), low),
+            pltpu.VMEM(plane + (rows, units), jnp.float32),
+            pltpu.VMEM(plane + (rows, units), jnp.float32),
+            pltpu.VMEM(plane + (rows, units), jnp.float32),
+            pltpu.VMEM(plane + (rows, units), low),
+            pltpu.VMEM(plane + (rows, units), low),
+            pltpu.VMEM(plane + (rows, width), low),
+            pltpu.VMEM((rows, units), jnp.float32),
+            pltpu.VMEM((rows, 128), jnp.float32),
+            pltpu.VMEM(plane + (8, rows), jnp.float32),
+            pltpu.VMEM(plane + (8, rows), jnp.float32),
+            pltpu.VMEM((4,) + plane + (8, rows), jnp.float32),
+            pltpu.VMEM(plane + (8, rows), jnp.float32),
+            pltpu.VMEM((2, 2, rows, width), low),
+            pltpu.VMEM((2, 2, rows, width), low),
+            pltpu.VMEM((2, 2, rows, width), low),
+            pltpu.VMEM((rows, width), low),
+            pltpu.SemaphoreType.DMA,
+            pltpu.SemaphoreType.DMA((count,)),
+            pltpu.SemaphoreType.DMA((count,)),
         ],
-        compiler_params=pltpu.CompilerParams(collective_id=3, has_side_effects=True),
-    )(mine)
-
-
-def add_low(left, right):
-    return (left.astype(jnp.float32) + right.astype(jnp.float32)).astype(jnp.bfloat16)
+        compiler_params=pltpu.CompilerParams(
+            collective_id=2, has_side_effects=True, vmem_limit_bytes=62 * 2**20
+        ),
+    )(mid, og_all, fc1, fc2, unit_rows)
 
 
 def fold_kernel(
     nz,
     pieces,
     first_ref,
-    second_ref,
     fc1_ref,
     fc2_ref,
     small_ref,
     first_out,
-    second_out,
     fc1_out,
     fc2_out,
     small_out,
@@ -617,8 +828,8 @@
     half = first_ref.shape[4] // 2
     lo, hi = pl.ds(0, half), pl.ds(half, half)
     parts = [pl.ds(k * rows, rows) for k in range(pieces)]
-    jobs = [(i, k) for i in range(2) for k in range(pieces)]
-    refs, outs = (first_ref, second_ref), (first_out, second_out)
+    jobs = [(i, k) for i in range(1) for k in range(pieces)]
+    refs, outs = (first_ref,), (first_out,)
     stage_c = {
         (i, k): sends.start(
             refs[i].at[:, :, 1 - c, parts[k]], from_core.at[i, :, :, parts[k]], to_c
@@ -691,7 +902,7 @@
     sends.finish()
 
 
-def fold(nz, first, second, fc1, fc2, small):
+def fold(nz, first, fc1, fc2, small):
     rows, columns = first.shape[3:]
     low = jnp.bfloat16
     pieces = 2
@@ -703,15 +914,15 @@
         name="fold",
         out_shape=tuple(
             jax.ShapeDtypeStruct(shape, *kept)
-            for shape in ((rows, columns), (rows, columns), out1, out2, small.shape)
-        ),
-        in_specs=[IN_VMEM] * 5,
-        out_specs=[IN_VMEM] * 5,
+            for shape in ((rows, columns), out1, out2, small.shape)
+        ),
+        in_specs=[IN_VMEM] * 4,
+        out_specs=[IN_VMEM] * 4,
         scratch_shapes=[
-            pltpu.VMEM((2, 2, 2, rows, columns), low),
-            pltpu.VMEM((2, 2, 2, rows, columns), low),
-            pltpu.VMEM((2, 2, rows, columns), low),
-            pltpu.VMEM((2, rows, columns), low),
+            pltpu.VMEM((1, 2, 2, rows, columns), low),
+            pltpu.VMEM((1, 2, 2, rows, columns), low),
+            pltpu.VMEM((1, 2, rows, columns), low),
+            pltpu.VMEM((1, rows, columns), low),
             pltpu.VMEM((nz - 1,) + out1, low),
             pltpu.VMEM((nz - 1,) + out2, low),
             pltpu.VMEM((nz - 1,) + small.shape, jnp.float32),
@@ -721,7 +932,7 @@
         compiler_params=pltpu.CompilerParams(
             collective_id=4, has_side_effects=True, vmem_limit_bytes=60 * 2**20
         ),
-    )(first, second, fc1, fc2, small)
+    )(first, fc1, fc2, small)
 
 
 def total_kernel(
@@ -889,7 +1100,6 @@
     qkv_full = qkv_full.reshape(model_width, -1)
     out_full = out_full.reshape(model_width, -1)
     vec_full = vec_full.reshape(model_width, 128)
-    shard_rows = shard_rows.reshape(-1, model_width)
     vec_rows = vec_full[:, :10].T
     gain_full = vec_rows[:3]
     bias_full = vec_rows[3:]
@@ -916,55 +1126,14 @@
     middle = inputs + normed_post * gain_full[1] + bias_full[4]
     normed_two, inverse_two = normalize(middle)
     normed_mid = (normed_two * gain_full[2] + bias_full[5]).astype(jnp.bfloat16)
-    gathered = spread_rows(normed_mid).reshape(-1, model_width)
-    group_rows = gathered.shape[0]
-    hidden_pre = jnp.dot(gathered, fc1_rows, preferred_element_type=jnp.float32) + ffn_biases[0]
-    activated, gelu_pull = jax.vjp(jax.nn.gelu, hidden_pre)
-    grad_piece = jnp.einsum("rd,fd->rf", shard_rows, fc2_cols, preferred_element_type=jnp.float32)
-    grad_normed_act = grad_piece * mid_gain
-    row_sums = jnp.stack(
-        [
-            jnp.sum(activated, axis=1),
-            jnp.sum(activated * activated, axis=1),
-            jnp.sum(grad_normed_act, axis=1),
-            jnp.sum(grad_normed_act * activated, axis=1),
-        ]
-        + [jnp.zeros((group_rows,), jnp.float32)] * 4
-    )
-    row_sums = tensor_sums(row_sums) / FF
-    center = row_sums[0]
-    inverse_mid = lax.rsqrt(row_sums[1] - center * center + EPS)
-    first_mean = row_sums[2]
-    second_mean = inverse_mid * (row_sums[3] - center * row_sums[2])
-    inverse_mid = inverse_mid[:, None]
-    normed_act = (activated - center[:, None]) * inverse_mid
-    hidden = (normed_act * mid_gain + ffn_biases[1]).astype(jnp.bfloat16)
-    ffn_part = jnp.dot(hidden, fc2_cols, preferred_element_type=jnp.float32).astype(jnp.bfloat16)
-    fc2_part = jnp.einsum("rf,rd->fd", hidden, shard_rows, preferred_element_type=jnp.float32)
-    grad_act = inverse_mid * (
-        grad_normed_act - first_mean[:, None] - normed_act * second_mean[:, None]
-    )
-    grad_pre = gelu_pull(grad_act)[0].astype(jnp.bfloat16)
-    fc1_part = jnp.einsum("rd,rf->df", gathered, grad_pre, preferred_element_type=jnp.float32)
-    mid_part = jnp.einsum("rf,df->rd", grad_pre, fc1_rows, preferred_element_type=jnp.float32)
-    units = fc1_rows.shape[1]
-    unit_sums = jnp.concatenate(
-        [
-            jnp.sum(grad_piece * normed_act, axis=0)[None],
-            jnp.sum(grad_pre.astype(jnp.float32), axis=0)[None],
-            jnp.sum(grad_piece, axis=0)[None],
-            jnp.zeros((5, units), jnp.float32),
-        ]
-    )
-    plane = (2, 2, 2, local_rows, model_width)
-    grad_normed_mid, ffn_out, fc1_grad, fc2_grad, unit_sums = fold(
-        nz,
-        mid_part.astype(jnp.bfloat16).reshape(plane),
-        ffn_part.reshape(plane),
-        fc1_part.astype(jnp.bfloat16),
-        fc2_part.astype(jnp.bfloat16),
-        unit_sums,
-    )
+    units = w_fc1.shape[1]
+    unit_rows = jnp.concatenate(
+        [ffn_biases[:1], mid_gain[None], ffn_biases[1:], jnp.zeros((5, units), jnp.float32)]
+    )
+    grad_normed_mid, ffn_part, fc1_part, fc2_part, unit_sums = ffn(
+        normed_mid, shard_rows, fc1_rows, fc2_cols, unit_rows
+    )
+    ffn_out, fc1_grad, fc2_grad, unit_sums = fold(nz, ffn_part, fc1_part, fc2_part, unit_sums)
     mid_gain_grad, ffn_bias_grad = unit_sums[0], unit_sums[1:3]
     mixed_out = (middle + ffn_out + bias_full[6]).astype(jnp.bfloat16)
     final_grad = out_grad.astype(jnp.float32)

time: 416 us -> 390 us (0.938)
  the two profiles are of different devices: /device:TPU:0 before, /device:TPU:9 now
where the time goes in v2:
time: 390 us; the launch traced here: 384 us
  Pallas kernels  282 us (72%)
  matrix products  55.7 us (14%)
  local copies, waits for them, and re-layouts  24.8 us (6%)
  other arithmetic  20 us (5%)
    pallas_call x1, Pallas kernels, gather(): pl.pallas_call(functools.partial(gather_kernel, nz), name='gather', out_s...  101 us
    pallas_call x1, Pallas kernels, total_all(): pl.pallas_call(functools.partial(total_kernel, nz), name='total_all', out...  63.8 us
    pallas_call x1, Pallas kernels, ffn(): pl.pallas_call(ffn_kernel, name='ffn', out_shape=(sds((rows, width), jnp....  63.5 us
    pallas_call x1, Pallas kernels, fold(): pl.pallas_call(functools.partial(fold_kernel, nz, pieces), name='fold', o...  53.2 us
    dot_general x1, matrix products, attend_backward(): jnp.einsum('hqk,qhd->khd', grad_scores, query_rows, preferred_element_typ...  9.67 us
    dot_general x1, matrix products, attend_backward(): jnp.einsum('hqk,khd->qhd', grad_scores, key_rows, preferred_element_type=...  9.63 us
    unnamed x41, local copies, waits for them, and re-layouts  9.62 us

profile of v2, /device:TPU:9, one launch (start us, length us, event | category | flops | bytes accessed | tf_op | source)
XLA Modules:
  0.0 383.6 jit_solution(15531904387835013782)
XLA Ops:
  2.9 101.3 %gather.1 = (bf16[4,2,2,2,32,3072]{5,4,3,2,1,0:T(8,128)(2,1)}, bf16[4,2,2,2,32,1024]{5,4,3,2,1,0:T(8,128)(2,1)}, f32[4,2,2,2,32,128]{5,4,3,2,1,0:T(8,128)}, bf16...) custom-call(bf16[32,3072]{1,0:T(8,128)(2,1)} %qkv_ref.1, ...), custom_call_target="tpu_custom_call" | custom-call | tf_op jit(solution)/shard_map/gather/pallas_call | solution.py:465
  106.8 4.9 %fusion.2 = bf16[256,3072]{1,0:T(8,128)(2,1)S(1)} fusion(bf16[1024,3072]{1,0:T(8,128)(2,1)} %bitcast.126, f32[3072]{0:T(1024)S(1)} %pad_maximum_fusion.2, bf16[256,1024]{1,0:T(8,128)(2,1)} %param.20, f32[1024]{0:T(1024)S(1)} %bitcast.120, f32[1024]{0:T(1024)S(1)} %bitcast.102, f32[256]{0:T(256)S(1)} %get-tuple-element.133, f32[256]{0:T(256)S(1)} %get-tuple-element.132), kind=kOutput, calls=%fused_computation.11 | convolution fusion | flops 1613758464 | bytes 8411136 | tf_op jit(solution)/shard_map/dot_general | solution.py:1115
  113.6 2.0 copy-done
  116.8 4.6 %fusion.41 = (bf16[256,16,64]{0,2,1:T(8,128)(2,1)S(1)}, f32[16,64,256]{2,1,0:T(8,128)}) fusion(f32[16]{0:T(128)S(1)} %copy-done.16, bf16[256,16,64]{0,2,1:T(8,128)(2,1)S(1)} %bitcast.74, f32[16,256,256]{1,2,0:T(8,128)} %copy-done, f32[16,256]{1,0:T(8,128)S(1)} %fusion.3, f32[16,256]{1,0:T(8,128)S(1)} %get-tuple-element.134, pred[256,256]{0,1:T(8,128)(4,1)S(1)} %fusion.43), kind=kOutput, calls=%fused_computation.49 | convolution fusion | flops 139984896 | bytes 6389824 | tf_op jit(solution)/shard_map/hqk,khd->qhd/dot_general | solution.py:52
  125.5 63.5 %ffn.1 = (f32[256,1024]{1,0:T(8,128)}, bf16[2,2,2,256,1024]{4,3,2,1,0:T(8,128)(2,1)}, bf16[1024,512]{1,0:T(8,128)(2,1)}, bf16[512,1024]{1,0:T(8,128)(2,1)}, f32[8,512]{1,0:T(8,128)}) custom-call(bf16[256,1024]{1,0:T(8,128)(2,1)} %add_convert_fusion.1.mid_ref, bf16[2,2,2,256,1024]{4,3,2,1,0:T(8,128)(2,1)} %get-tuple-element.71.og_ref, ...), custom_call_target="tpu_custom_call" | custom-call | tf_op jit(solution)/shard_map/ffn/pallas_call | solution.py:752
  189.0 53.2 %fold.1 = (f32[256,1024]{1,0:T(8,128)}, f32[256,512]{1,0:T(8,128)}, f32[512,256]{1,0:T(8,128)}, f32[8,512]{1,0:T(8,128)}) custom-call(bf16[2,2,2,256,1024]{4,3,2,1,0:T(8,128)(2,1)} %get-tuple-element.74.first_ref, bf16[1024,512]{1,0:T(8,128)(2,1)} %get-tuple-element.75.fc1_ref, bf16[512,1024]{1,0:T(8,128)(2,1)} %get-tuple-element.76.fc2_ref, ...), custom_call_target="tpu_custom_call" | custom-call | tf_op jit(solution)/shard_map/fold/pallas_call | solution.py:912
  242.7 3.4 multiply_reduce_fusion.3
  247.2 1.6 copy.65
  248.9 3.3 multiply_reduce_fusion.1
  252.2 2.0 copy.61
  254.3 4.0 %fusion.71 = f32[16,256,256]{1,2,0:T(8,128)} fusion(bf16[256,16,64]{0,2,1:T(8,128)(2,1)} %bitcast.76, bf16[256,16,64]{0,2,1:T(8,128)(2,1)} %bitcast.75), kind=kOutput, calls=%fused_computation.110 | convolution fusion | flops 134217728 | bytes 5242880 | tf_op jit(solution)/shard_map/qhd,khd->hqk/dot_general | solution.py:68
  258.3 9.6 %fusion.21 = bf16[16,64,256]{2,1,0:T(8,128)(2,1)} fusion(bf16[256,16,64]{0,2,1:T(8,128)(2,1)} %bitcast.81, f32[16,256,256]{1,2,0:T(8,128)} %fusion.71, f32[16,256,256]{1,2,0:T(8,128)} %copy-done, f32[16,256]{1,0:T(8,128)S(1)} %log_add_fusion, pred[256,256]{0,1:T(8,128)(4,1)S(1)} %fusion.43), kind=kOutput, calls=%fused_computation.32 | convolution fusion | flops 148115712 | bytes 9519104 | tf_op jit(solution)/shard_map/hqk,khd->qhd/dot_general | solution.py:74
  268.0 9.7 %fusion.24 = bf16[16,64,256]{2,1,0:T(8,128)(2,1)} fusion(bf16[256,16,64]{0,2,1:T(8,128)(2,1)} %bitcast.79, f32[16,256,256]{1,2,0:T(8,128)} %fusion.71, f32[16,256,256]{1,2,0:T(8,128)} %copy-done, f32[16,256]{1,0:T(8,128)S(1)} %log_add_fusion, pred[256,256]{0,1:T(8,128)(4,1)S(1)} %fusion.43), kind=kOutput, calls=%fused_computation.33 | convolution fusion | flops 148115712 | bytes 9519104 | tf_op jit(solution)/shard_map/hqk,qhd->khd/dot_general | solution.py:77
  277.6 3.7 fusion.18
  281.9 5.8 %fusion.38 = (f32[1024]{0:T(1024)S(1)}, f32[256]{0:T(256)S(1)}, f32[256]{0:T(256)S(1)}, f32[1024]{0:T(1024)S(1)}, f32[256,1024]{1,0:T(8,128)}) fusion(bf16[256,1024]{1,0:T(8,128)(2,1)S(1)} %copy-done.4, f32[256]{0:T(256)S(1)} %get-tuple-element.133, f32[256]{0:T(256)S(1)} %get-tuple-element.132, f32[1024]{0:T(1024)S(1)} %bitcast.103, ...), kind=kOutput, calls=%fused_computation.45 | convolution fusion | flops 1617950208 | bytes 9453568 | tf_op jit(solution)/shard_map/te,de->td/dot_general | solution.py:1168
  289.3 6.2 %convolution_convert_fusion = bf16[1024,3072]{1,0:T(8,128)(2,1)} fusion(bf16[256,1024]{1,0:T(8,128)(2,1)S(1)} %copy-done.4, f32[1024]{0:T(1024)S(1)} %bitcast.121, f32[1024]{0:T(1024)S(1)} %bitcast.104, f32[256]{0:T(256)S(1)} %get-tuple-element.133, f32[256]{0:T(256)S(1)} %get-tuple-element.132, bf16[256,1024]{0,1:T(8,128)(2,1)} %bitcast.91, ...), kind=kOutput, calls=%fused_computation.2 | convolution fusion | flops 1620049920 | bytes 8398848 | tf_op jit(solution)/shard_map/td,te->de/dot_general | solution.py:1165
  295.5 2.1 convolution_convert_fusion.1
  297.6 7.6 %pad_maximum_fusion = bf16[1024,4096]{1,0:T(8,128)(2,1)} fusion(bf16[1024,1024]{1,0:T(8,128)(2,1)} %convolution_convert_fusion.1, bf16[1024,3072]{1,0:T(8,128)(2,1)} %convolution_convert_fusion), kind=kLoop, calls=%fused_computation.1 | loop fusion | flops 16777216 | bytes 16777216 | tf_op jit(solution)/shard_map/concatenate | solution.py:1191
  305.2 63.8 %total_all.1 = (f32[32,4096]{1,0:T(8,128)}, f32[16,1024]{1,0:T(8,128)}) custom-call(bf16[4,2,2,2,32,4096]{5,4,3,2,1,0:T(8,128)(2,1)} %bitcast.71, f32[16,1024]{1,0:T(8,128)} %stack.51.small_ref), custom_call_target="tpu_custom_call" | custom-call | tf_op jit(solution)/shard_map/total_all/pallas_call | solution.py:1047
  368.9 1.8 slice.151
  370.7 1.6 slice.152
  375.4 1.4 fusion.37
  379.4 1.9 copy.76
  381.3 1.9 copy.77
  (89 shorter events, 21.5 us)
Async XLA Ops:
  111.7 0.7 copy-start.17
  112.1 4.4 %copy-start.8 = (bf16[256,1024]{0,1:T(8,128)(2,1)}, bf16[256,1024]{0,1:T(8,128)(2,1)S(1)}, u32[]{:S(2)}) copy-start(bf16[256,1024]{0,1:T(8,128)(2,1)S(1)} %copy.58) | copy-start | bytes 1572868
  112.3 4.2 %copy-start.9 = (bf16[256,1024]{0,1:T(8,128)(2,1)}, bf16[256,1024]{0,1:T(8,128)(2,1)S(1)}, u32[]{:S(2)}) copy-start(bf16[256,1024]{0,1:T(8,128)(2,1)S(1)} %copy.59) | copy-start | bytes 1572868
  112.7 4.0 %copy-start.16 = (f32[16]{0:T(128)S(1)}, f32[16]{0:T(128)}, u32[]{:S(2)}) copy-start(f32[16]{0:T(128)} %param.27) | copy-start | bytes 196
  113.6 2.0 copy-start
  116.7 4.6 %copy-start.7 = (bf16[256,1024]{0,1:T(8,128)(2,1)}, bf16[256,1024]{0,1:T(8,128)(2,1)S(1)}, u32[]{:S(2)}) copy-start(bf16[256,1024]{0,1:T(8,128)(2,1)S(1)} %copy.57) | copy-start | bytes 1572868
  116.7 4.6 %copy-start.3 = (bf16[4,2,2,2,32,1024]{5,4,3,2,1,0:T(8,128)(2,1)S(1)}, bf16[4,2,2,2,32,1024]{5,4,3,2,1,0:T(8,128)(2,1)}, u32[]{:S(2)}) copy-start(bf16[4,2,2,2,32,1024]{5,4,3,2,1,0:T(8,128)(2,1)} %get-tuple-element.70) | copy-start | bytes 6291460
  116.8 5.5 %copy-start.4 = (bf16[256,1024]{1,0:T(8,128)(2,1)S(1)}, bf16[256,1024]{1,0:T(8,128)(2,1)}, u32[]{:S(2)}) copy-start(bf16[256,1024]{1,0:T(8,128)(2,1)} %param.20) | copy-start | bytes 1572868
  121.4 3.4 copy-start.14
  121.4 3.5 copy-start.15
  122.7 1.0 copy-start.1
  189.0 53.2 %copy-start.2 = (f32[256,1024]{1,0:T(8,128)S(1)}, f32[256,1024]{1,0:T(8,128)}, u32[]{:S(2)}) copy-start(f32[256,1024]{1,0:T(8,128)} %copy-done.1) | copy-start | bytes 3145732
  189.0 53.2 %copy-start.6 = (f32[256,1024]{1,0:T(8,128)S(1)}, f32[256,1024]{1,0:T(8,128)}, u32[]{:S(2)}) copy-start(f32[256,1024]{1,0:T(8,128)} %get-tuple-element.79) | copy-start | bytes 3145732
  277.6 3.8 copy-start.11
  277.6 3.8 copy-start.12
  281.4 6.4 %copy-start.13 = (bf16[16,64,256]{2,1,0:T(8,128)(2,1)}, bf16[16,64,256]{2,1,0:T(8,128)(2,1)S(1)}, u32[]{:S(2)}) copy-start(bf16[16,64,256]{2,1,0:T(8,128)(2,1)S(1)} %fusion.18) | copy-start | bytes 1572868
  289.3 6.2 %copy-start.5 = (bf16[256,1024]{1,0:T(8,128)(2,1)S(1)}, bf16[256,1024]{1,0:T(8,128)(2,1)}, u32[]{:S(2)}) copy-start(bf16[256,1024]{1,0:T(8,128)(2,1)} %get-tuple-element.104) | copy-start | bytes 1572868
  305.2 70.3 %copy-start.10 = (f32[256,1024]{1,0:T(8,128)S(1)}, f32[256,1024]{1,0:T(8,128)}, u32[]{:S(2)}) copy-start(f32[256,1024]{1,0:T(8,128)} %get-tuple-element.139) | copy-start | bytes 3145732

commit v3 on v2

--- a/solution.py
+++ b/solution.py
@@ -789,34 +789,115 @@
     )(mid, og_all, fc1, fc2, unit_rows)
 
 
-def fold_kernel(
+def centered(values):
+    center = jnp.mean(values, axis=-1, keepdims=True)
+    spread = jnp.mean(values * values, axis=-1, keepdims=True) - center * center
+    inverse = lax.rsqrt(spread + EPS)
+    return (values - center) * inverse, inverse
+
+
+def centered_back(grad, normed, inverse):
+    first = jnp.mean(grad, axis=-1, keepdims=True)
+    second = jnp.mean(grad * normed, axis=-1, keepdims=True)
+    return inverse * (grad - first - normed * second)
+
+
+def eights(values):
+    return jnp.sum(values.reshape(values.shape[0] // 8, 8, values.shape[1]), axis=0)
+
+
+def doc_mask(doc_ref, rows):
+    query = lax.broadcasted_iota(jnp.int32, (rows, rows), 0)
+    key = lax.broadcasted_iota(jnp.int32, (rows, rows), 1)
+    query_doc, key_doc = jnp.zeros_like(query), jnp.zeros_like(key)
+    end = 0
+    for j in range(doc_ref.shape[1] - 1):
+        end = end + doc_ref[0, j]
+        query_doc = query_doc + (query >= end).astype(jnp.int32)
+        key_doc = key_doc + (key >= end).astype(jnp.int32)
+    allowed = jnp.logical_and(query_doc == key_doc, key <= query)
+    return allowed.astype(jnp.float32)
+
+
+def back_kernel(
     nz,
-    pieces,
-    first_ref,
+    gnm_ref,
+    ffn_ref,
     fc1_ref,
     fc2_ref,
-    small_ref,
-    first_out,
+    unit_ref,
+    proj_ref,
+    att_ref,
+    lse_ref,
+    branch_ref,
+    middle_ref,
+    scaled_ref,
+    nin_ref,
+    qkv_ref,
+    out_ref,
+    vec_ref,
+    og_ref,
+    tok_ref,
+    doc_ref,
+    mixed_out,
+    token_out,
+    weight_out,
+    gains_out,
+    biases_out,
+    scale_out,
     fc1_out,
     fc2_out,
-    small_out,
-    from_core,
-    sums,
-    from_one,
-    from_two,
+    unit_out,
+    f_core,
+    f_sums,
+    f_one,
+    f_two,
     got1,
     got2,
-    got_small,
+    got_unit,
+    w_part,
+    w_core,
+    w_sums,
+    w_one,
+    w_two,
+    w_far,
+    gpost,
+    gmid,
+    gatt,
+    gni,
+    dproj,
+    nin_t,
+    mask,
+    accs,
+    small,
+    small_got,
+    turned,
+    local_sems,
     send_sems,
     recv_sems,
 ):
     z, y, x, c = place()
     to_x, to_y, to_c = at(z, y, 1 - x, c), at(z, 1 - y, x, c), at(z, y, x, 1 - c)
+    to_xy = at(z, 1 - y, 1 - x, c)
     others = [lax.rem(z + k, nz) for k in range(1, nz)]
     peers = [at(other, y, x, c) for other in others]
-    greet([to_x, to_y, to_c] + peers)
+    greet([to_x, to_y, to_c, to_xy] + peers)
     sends = Sends(send_sems, recv_sems)
+    rows, width = middle_ref.shape
+    low = jnp.bfloat16
+    f32 = jnp.float32
+    share = weight_out.shape[0]
     width1, width2 = fc1_out.shape[0], fc2_out.shape[1]
+
+    pieces = 2
+    parts = [pl.ds(k * (rows // pieces), rows // pieces) for k in range(pieces)]
+    left, right = pl.ds(0, width // 2), pl.ds(width // 2, width // 2)
+    f_c = [
+        sends.start(ffn_ref.at[:, :, 1 - c, part], f_core.at[:, :, part], to_c) for part in parts
+    ]
+    locals_ = [
+        pltpu.make_async_copy(ffn_ref.at[:, :, c], f_sums, local_sems.at[0]),
+    ]
 
     def block1(which):
         return fc1_ref.at[pl.ds(pl.multiple_of(which * width1, width1), width1)]
@@ -824,250 +905,388 @@
     def block2(which):
         return fc2_ref.at[:, pl.ds(pl.multiple_of(which * width2, width2), width2)]
 
-    rows = first_ref.shape[3] // pieces
-    half = first_ref.shape[4] // 2
-    lo, hi = pl.ds(0, half), pl.ds(half, half)
-    parts = [pl.ds(k * rows, rows) for k in range(pieces)]
-    jobs = [(i, k) for i in range(1) for k in range(pieces)]
-    refs, outs = (first_ref,), (first_out,)
-    stage_c = {
-        (i, k): sends.start(
-            refs[i].at[:, :, 1 - c, parts[k]], from_core.at[i, :, :, parts[k]], to_c
-        )
-        for i, k in jobs
-    }
+    locals_.append(pltpu.make_async_copy(block1(z), got1.at[nz - 1], local_sems.at[1]))
+    locals_.append(pltpu.make_async_copy(block2(z), got2.at[nz - 1], local_sems.at[2]))
+    for copy in locals_:
+        copy.start()
     far = []
     for k, peer in enumerate(peers):
-        far.append(sends.start(small_ref, got_small.at[k], peer))
+        far.append(sends.start(unit_ref, got_unit.at[k], peer))
         far.append(sends.start(block1(others[k]), got1.at[k], peer))
         far.append(sends.start(block2(others[k]), got2.at[k], peer))
 
-    stage_1, stage_2 = {}, {}
-
-    def after_core(i, k):
+    f_first, f_second = [], []
+
+    def ffn_one(k):
         part = parts[k]
-        stage_c[i, k].wait_recv()
+        f_c[k].wait_recv()
+        if k == 0:
+            locals_[0].wait()
         for yy in range(2):
             for xx in range(2):
-                sums[i, yy, xx, part] = add_low(
-                    refs[i][yy, xx, c, part], from_core[i, yy, xx, part]
+                f_sums[yy, xx, part] = add_low(f_sums[yy, xx, part], f_core[yy, xx, part])
+        f_first.append(
+            (
+                sends.start(f_sums.at[:, 1 - x, part, left], f_one.at[0, :, part, left], to_x),
+                sends.start(f_sums.at[1 - y, :, part, right], f_one.at[1, :, part, right], to_y),
+            )
+        )
+
+    def ffn_two(k):
+        part = parts[k]
+        for copy in f_first[k]:
+            copy.wait_recv()
+        f_sums[1 - y, x, part, left] = add_low(
+            f_sums[1 - y, x, part, left], f_one[0, 1 - y, part, left]
+        )
+        f_sums[y, 1 - x, part, right] = add_low(
+            f_sums[y, 1 - x, part, right], f_one[1, 1 - x, part, right]
+        )
+        f_second.append(
+            (
+                sends.start(f_sums.at[1 - y, x, part, left], f_two.at[part, left], to_y),
+                sends.start(f_sums.at[y, 1 - x, part, right], f_two.at[part, right], to_x),
+            )
+        )
+
+    def ffn_three(k):
+        part = parts[k]
+        for copy in f_second[k]:
+            copy.wait_recv()
+        for i, (cols, at_) in enumerate(((left, y), (right, x))):
+            total = (
+                f_sums[y, x, part, cols].astype(f32)
+                + f_one[i, at_, part, cols].astype(f32)
+                + f_two[part, cols].astype(f32)
+            )
+            mixed_out[part, cols] = (
+                middle_ref[part, cols] + total + vec_ref[9:10, cols]
+            ).astype(low)
+
+    spans = [(0, width)] + [(width + g * 3 * width // 4, 3 * width // 4) for g in range(4)]
+    w_first, w_second, w_third, w_c = {}, {}, {}, {}
+
+    def sides(j):
+        start, size = spans[j]
+        return pl.ds(start, size), pl.ds(start, size // 2), pl.ds(start + size // 2, size // 2)
+
+    def w_zero(j):
+        every = sides(j)[0]
+        w_c[j] = sends.start(w_part.at[:, :, :, 1 - c, :, every], w_core.at[..., every], to_c)
+
+    def w_step1(j):
+        every, lo, hi = sides(j)
+        w_c[j].wait_recv()
+
+        def one(which, carry):
+            for yy in range(2):
+                for xx in range(2):
+                    w_sums[which, yy, xx, :, every] = add_low(
+                        w_part[which, yy, xx, c, :, every], w_core[which, yy, xx, :, every]
+                    )
+            return carry
+
+        lax.fori_loop(0, nz, one, 0)
+        w_first[j] = (
+            sends.start(w_sums.at[:, :, 1 - x, :, lo], w_one.at[:, :, :, lo], to_x),
+            sends.start(w_sums.at[:, 1 - y, :, :, hi], w_one.at[:, :, :, hi], to_y),
+        )
+
+    def w_step2(j):
+        every, lo, hi = sides(j)
+        for copy in w_first[j]:
+            copy.wait_recv()
+
+        def one(which, carry):
+            for k in range(2):
+                w_sums[which, k, x, :, lo] = add_low(
+                    w_sums[which, k, x, :, lo], w_one[which, k, :, lo]
                 )
-        stage_1[i, k] = (
-            sends.start(sums.at[i, :, 1 - x, part, lo], from_one.at[i, :, part, lo], to_x),
-            sends.start(sums.at[i, 1 - y, :, part, hi], from_one.at[i, :, part, hi], to_y),
+                w_sums[which, y, k, :, hi] = add_low(
+                    w_sums[which, y, k, :, hi], w_one[which, k, :, hi]
+                )
+            return carry
+
+        lax.fori_loop(0, nz, one, 0)
+        w_second[j] = (
+            sends.start(w_sums.at[:, 1 - y, x, :, lo], w_two.at[:, :, lo], to_y),
+            sends.start(w_sums.at[:, y, 1 - x, :, hi], w_two.at[:, :, hi], to_x),
         )
 
-    def after_one(i, k):
-        part = parts[k]
-        for copy in stage_1[i, k]:
+    def w_step3(j):
+        every = sides(j)[0]
+        for copy in w_second[j]:
             copy.wait_recv()
-        for yy in range(2):
-            sums[i, yy, x, part, lo] = add_low(
-                sums[i, yy, x, part, lo], from_one[i, yy, part, lo]
+        for which in range(nz):
+            w_sums[which, y, x, :, every] = add_low(
+                w_sums[which, y, x, :, every], w_two[which, :, every]
             )
-        for xx in range(2):
-            sums[i, y, xx, part, hi] = add_low(
-                sums[i, y, xx, part, hi], from_one[i, xx, part, hi]
+        w_third[j] = [
+            sends.start(w_sums.at[others[k], y, x, :, every], w_far.at[k, :, every], peer)
+            for k, peer in enumerate(peers)
+        ]
+
+    def w_step4(j):
+        start, size = spans[j]
+        every = sides(j)[0]
+        total = w_sums[z, y, x, :, every].astype(f32)
+        for k in range(nz - 1):
+            w_third[j][k].wait_recv()
+            total = total + w_far[k, :, every].astype(f32)
+        if j == 0:
+            weight_out[:, 3 * width :] = total
+        else:
+            third = size // 3
+            for i in range(3):
+                first = i * width + (j - 1) * third
+                weight_out[:, first : first + third] = total[:, i * third : (i + 1) * third]
+
+    accs[...] = jnp.zeros_like(accs)
+    step = 32
+
+    def norms(k, carry):
+        part = pl.ds(pl.multiple_of(k * step, step), step)
+        normed_two, inverse_two = centered(middle_ref[part])
+        grad = gnm_ref[part]
+        og = og_ref[part].astype(f32)
+        grad_middle = og + centered_back(grad * vec_ref[2:3], normed_two, inverse_two)
+        accs[2] += eights(grad * normed_two)
+        accs[8] += eights(grad)
+        accs[9] += eights(og)
+        normed_post, inverse_post = centered(branch_ref[part])
+        post = centered_back(grad_middle * vec_ref[1:2], normed_post, inverse_post).astype(low)
+        accs[1] += eights(grad_middle * normed_post)
+        accs[7] += eights(grad_middle)
+        accs[6] += eights(post.astype(f32))
+        gpost[part] = post
+        gmid[part] = grad_middle
+        return carry
+
+    lax.fori_loop(0, rows // step, norms, 0)
+    mask[...] = doc_mask(doc_ref, rows)
+    ffn_one(0)
+    ffn_one(1)
+    quarter = width // 4
+
+    def scaled_block(k, carry):
+        part = pl.ds(pl.multiple_of(k * quarter, quarter), quarter)
+        block = dot(gpost[...], out_ref[part], NT)
+        accs[10, :, part] = eights(block * att_ref[:, part])
+        gatt[:, part] = (block * vec_ref[10:11, part]).astype(low)
+        return carry
+
+    lax.fori_loop(0, 4, scaled_block, 0)
+
+    def out_block(k, carry):
+        part = pl.ds(pl.multiple_of(k * (width // nz), width // nz), width // nz)
+        block = dot(scaled_ref[:, part], gpost[...], TN).astype(low)
+        w_part[k, :, :, :, :, pl.ds(0, width)] = block.reshape(2, 2, 2, share, width)
+        return carry
+
+    lax.fori_loop(0, nz, out_block, 0)
+    w_zero(0)
+    nin_t[...] = nin_ref[...].T
+    head = 64
+    lane = lax.broadcasted_iota(jnp.int32, (1, 128), 1)
+    is_low = lane < head
+    factor = 1.0 / math.sqrt(head)
+    lane_wide = lax.broadcasted_iota(jnp.int32, (rows, 128), 1)
+    keep = (is_low.astype(low), (lane >= head).astype(low))
+
+    def pair(p, carry):
+        q_at = pl.ds(pl.multiple_of(p * 128, 128), 128)
+        k_at = pl.ds(pl.multiple_of(width + p * 128, 128), 128)
+        v_at = pl.ds(pl.multiple_of(2 * width + p * 128, 128), 128)
+        q2, k2, v2, do2 = proj_ref[:, q_at], proj_ref[:, k_at], proj_ref[:, v_at], gatt[:, q_at]
+        lses = lse_ref[...]
+        found = []
+        for i in range(2):
+            scores = dot(q2 * keep[i], k2, NT) * factor
+            scores = jnp.where(mask[...] > 0, scores, NEGATIVE)
+            lse = jnp.sum(jnp.where(lane_wide == 2 * p + i, lses, 0.0), axis=1, keepdims=True)
+            prob = jnp.exp(scores - lse)
+            grad_prob = dot(do2 * keep[i], v2, NT)
+            inner = jnp.sum(prob * grad_prob, axis=1, keepdims=True)
+            ds = (prob * (grad_prob - inner) * factor).astype(low)
+            found.append(
+                (dot(ds, k2), dot(ds, q2, TN), dot(prob.astype(low), do2, TN))
             )
-        stage_2[i, k] = (
-            sends.start(sums.at[i, 1 - y, x, part, lo], from_two.at[i, part, lo], to_y),
-            sends.start(sums.at[i, y, 1 - x, part, hi], from_two.at[i, part, hi], to_x),
-        )
-
-    def after_two(i, k):
-        part = parts[k]
-        for copy in stage_2[i, k]:
-            copy.wait_recv()
-        outs[i][part] = sums[i, y, x, part].astype(jnp.float32) + from_two[i, part].astype(
-            jnp.float32
-        )
-
-    for n in range(len(jobs) + 2):
-        if n < len(jobs):
-            after_core(*jobs[n])
-        if 1 <= n < len(jobs) + 1:
-            after_one(*jobs[n - 1])
-        if n >= 2:
-            after_two(*jobs[n - 2])
+        for where, a, b in zip((q_at, k_at, v_at), *found):
+            dproj[:, where] = jnp.where(is_low, a, b).astype(low)
+        accs[4, :, q_at] = eights(dproj[:, q_at].astype(f32))
+        accs[5, :, q_at] = eights(dproj[:, v_at].astype(f32))
+        return carry
+
+    def wgrad(j):
+        start, size = spans[j]
+        third = size // 3
+
+        def one(k, carry):
+            part = pl.ds(pl.multiple_of(k * (width // nz), width // nz), width // nz)
+            for i in range(3):
+                first = i * width + (j - 1) * third
+                block = dot(nin_t[part], dproj[:, first : first + third]).astype(low)
+                w_part[k, :, :, :, :, pl.ds(start + i * third, third)] = block.reshape(
+                    2, 2, 2, share, third
+                )
+            return carry
+
+        lax.fori_loop(0, nz, one, 0)
+        w_zero(j)
+
+    lax.fori_loop(0, 2, pair, 0)
+    wgrad(1)
+    w_step1(0)
+    ffn_two(0)
+    lax.fori_loop(2, 4, pair, 0)
+    wgrad(2)
+    w_step1(1)
+    ffn_two(1)
+    lax.fori_loop(4, 6, pair, 0)
+    wgrad(3)
+    w_step1(2)
+    lax.fori_loop(6, 8, pair, 0)
+    wgrad(4)
+    w_step1(3)
+    w_step1(4)
+
+    def gni_block(k, carry):
+        part = pl.ds(pl.multiple_of(k * quarter, quarter), quarter)
+        gni[:, part] = dot(dproj[...], qkv_ref[part], NT)
+        return carry
+
+    lax.fori_loop(0, 4, gni_block, 0)
+
+    def tokens_back(k, carry):
+        part = pl.ds(pl.multiple_of(k * step, step), step)
+        normed, inverse = centered(tok_ref[part].astype(f32))
+        grad = gni[part]
+        token_out[part] = gmid[part] + centered_back(grad * vec_ref[0:1], normed, inverse)
+        accs[0] += eights(grad * normed)
+        accs[3] += eights(grad)
+        return carry
+
+    lax.fori_loop(0, rows // step, tokens_back, 0)
+    for j in range(16):
+        small[0, j : j + 1] = jnp.sum(accs[j], axis=0, keepdims=True)
+    small_c = sends.start(small.at[0], small_got.at[0], to_c)
+    w_step2(0)
+    small_c.wait_recv()
+    small[1] = small[0] + small_got[0]
+    small_p = [
+        sends.start(small.at[1], small_got.at[1 + k], to)
+        for k, to in enumerate((to_x, to_y, to_xy))
+    ]
+    ffn_three(0)
+    ffn_three(1)
+    w_step2(1)
+    for copy in small_p:
+        copy.wait_recv()
+    small[2] = (small[1] + small_got[1]) + (small_got[2] + small_got[3])
+    small_z = [
+        sends.start(small.at[2], small_got.at[4 + k], peer) for k, peer in enumerate(peers)
+    ]
+    w_step3(0)
+    w_step2(2)
+    w_step3(1)
+    w_step2(3)
+    w_step3(2)
+    w_step2(4)
+    w_step3(3)
+    w_step4(0)
+    total = small[2]
+    for k in range(nz - 1):
+        small_z[k].wait_recv()
+        total = total + small_got[4 + k]
+    scale_out[...] = total[8:16]
+    index = (lax.axis_index("dp") * 8 + lax.axis_index("tensor")) * share
+    mine = pl.ds(pl.multiple_of(index, share), share)
+    pad = jnp.zeros((112, width), f32)
+    turned[...] = jnp.concatenate([total, pad], axis=0).T
+    gains_out[...] = turned[mine, 0:3]
+    turned[...] = jnp.concatenate([total[3:10], pad, total[:9]], axis=0).T
+    biases_out[...] = turned[mine, 0:7]
+    w_step4(1)
+    w_step4(2)
+    w_step3(4)
     for copy in far:
         copy.wait_recv()
-    own1, own2, small = block1(z)[...].astype(jnp.float32), block2(z)[...].astype(jnp.float32), small_ref[...]
+    for copy in locals_[1:]:
+        copy.wait()
+    own1, own2, unit = got1[nz - 1].astype(f32), got2[nz - 1].astype(f32), unit_ref[...]
     for k in range(nz - 1):
-        own1 = own1 + got1[k].astype(jnp.float32)
-        own2 = own2 + got2[k].astype(jnp.float32)
-        small = small + got_small[k]
+        own1 = own1 + got1[k].astype(f32)
+        own2 = own2 + got2[k].astype(f32)
+        unit = unit + got_unit[k]
     fc1_out[...] = own1
     fc2_out[...] = own2
-    small_out[...] = small
+    unit_out[...] = unit
+    w_step4(3)
+    w_step4(4)
     sends.finish()
 
 
-def fold(nz, first, fc1, fc2, small):
-    rows, columns = first.shape[3:]
-    low = jnp.bfloat16
-    pieces = 2
-    count = 5 * 2 * pieces + 3 * (nz - 1)
-    out1, out2 = (fc1.shape[0] // nz, fc1.shape[1]), (fc2.shape[0], fc2.shape[1] // nz)
-    kept = (jnp.float32,)
+def back(nz, *operands):
+    (gnm, ffn_part, fc1, fc2, unit, proj, att, lse, branch, middle, scaled, nin, qkv, out, vec) = (
+        operands[:15]
+    )
+    rows, width = middle.shape
+    share = width // (nz * 8)
+    columns = proj.shape[1] + width
+    low, f32 = jnp.bfloat16, jnp.float32
+    sds = jax.ShapeDtypeStruct
+    fc1_own, fc2_own = (fc1.shape[0] // nz, fc1.shape[1]), (fc2.shape[0], fc2.shape[1] // nz)
+    count = 64 + 8 * nz
+    specs = [IN_VMEM] + [ANY] * 3 + [IN_VMEM] * 13 + [pl.BlockSpec(memory_space=pltpu.SMEM)]
     return pl.pallas_call(
-        functools.partial(fold_kernel, nz, pieces),
-        name="fold",
-        out_shape=tuple(
-            jax.ShapeDtypeStruct(shape, *kept)
-            for shape in ((rows, columns), out1, out2, small.shape)
+        functools.partial(back_kernel, nz),
+        name="back",
+        out_shape=(
+            sds((rows, width), low),
+            sds((rows, width), f32),
+            sds((share, columns), f32),
+            sds((share, 3), f32),
+            sds((share, 7), f32),
+            sds((8, width), f32),
+            sds(fc1_own, f32),
+            sds(fc2_own, f32),
+            sds(unit.shape, f32),
         ),
-        in_specs=[IN_VMEM] * 4,
-        out_specs=[IN_VMEM] * 4,
+        in_specs=specs,
+        out_specs=[IN_VMEM] * 9,
         scratch_shapes=[
-            pltpu.VMEM((1, 2, 2, rows, columns), low),
-            pltpu.VMEM((1, 2, 2, rows, columns), low),
-            pltpu.VMEM((1, 2, rows, columns), low),
-            pltpu.VMEM((1, rows, columns), low),
-            pltpu.VMEM((nz - 1,) + out1, low),
-            pltpu.VMEM((nz - 1,) + out2, low),
-            pltpu.VMEM((nz - 1,) + small.shape, jnp.float32),
+            pltpu.VMEM((2, 2, rows, width), low),
+            pltpu.VMEM((2, 2, rows, width), low),
+            pltpu.VMEM((2, 2, rows, width), low),
+            pltpu.VMEM((rows, width), low),
+            pltpu.VMEM((nz,) + fc1_own, low),
+            pltpu.VMEM((nz,) + fc2_own, low),
+            pltpu.VMEM((nz - 1,) + unit.shape, f32),
+            pltpu.VMEM((nz, 2, 2, 2, share, columns), low),
+            pltpu.VMEM((nz, 2, 2, share, columns), low),
+            pltpu.VMEM((nz, 2, 2, share, columns), low),
+            pltpu.VMEM((nz, 2, share, columns), low),
+            pltpu.VMEM((nz, share, columns), low),
+            pltpu.VMEM((nz - 1, share, columns), low),
+            pltpu.VMEM((rows, width), low),
+            pltpu.VMEM((rows, width), f32),
+            pltpu.VMEM((rows, width), low),
+            pltpu.VMEM((rows, width), f32),
+            pltpu.VMEM((rows, 3 * width), low),
+            pltpu.VMEM((width, rows), low),
+            pltpu.VMEM((rows, rows), f32),
+            pltpu.VMEM((16, 8, width), f32),
+            pltpu.VMEM((3, 16, width), f32),
+            pltpu.VMEM((nz + 3, 16, width), f32),
+            pltpu.VMEM((width, 128), f32),
+            pltpu.SemaphoreType.DMA((3,)),
             pltpu.SemaphoreType.DMA((count,)),
             pltpu.SemaphoreType.DMA((count,)),
         ],
         compiler_params=pltpu.CompilerParams(
-            collective_id=4, has_side_effects=True, vmem_limit_bytes=60 * 2**20
+            collective_id=3, has_side_effects=True, vmem_limit_bytes=63 * 2**20
         ),
-    )(first, fc1, fc2, small)
-
-
-def total_kernel(
-    nz,
-    grad_ref,
-    small_ref,
-    grad_out,
-    small_out,
-    from_core,
-    sums,
-    from_one,
-    from_two,
-    from_far,
-    small_sum,
-    small_got,
-    send_sems,
-    recv_sems,
-):
-    z, y, x, c = place()
-    to_x, to_y, to_c = at(z, y, 1 - x, c), at(z, 1 - y, x, c), at(z, y, x, 1 - c)
-    others = [lax.rem(z + k, nz) for k in range(1, nz)]
-    order = others + [z]
-    peers = [at(other, y, x, c) for other in others]
-    greet([to_x, to_y, to_c] + peers)
-    sends = Sends(send_sems, recv_sems)
-    half = grad_ref.shape[-1] // 2
-    lo, hi = pl.ds(0, half), pl.ds(half, half)
-    stage_c = [
-        sends.start(grad_ref.at[which, :, :, 1 - c], from_core.at[which], to_c)
-        for which in order
-    ]
-    small_c = sends.start(small_ref, small_got.at[0], to_c)
-    stage_1, stage_2, far = {}, {}, {}
-
-    def after_core(k):
-        which = order[k]
-        stage_c[k].wait_recv()
-        for yy in range(2):
-            for xx in range(2):
-                sums[which, yy, xx] = add_low(
-                    grad_ref[which, yy, xx, c], from_core[which, yy, xx]
-                )
-        stage_1[k] = (
-            sends.start(sums.at[which, :, 1 - x, :, lo], from_one.at[which, :, :, lo], to_x),
-            sends.start(sums.at[which, 1 - y, :, :, hi], from_one.at[which, :, :, hi], to_y),
-        )
-
-    def after_one(k):
-        which = order[k]
-        for copy in stage_1[k]:
-            copy.wait_recv()
-        for yy in range(2):
-            sums[which, yy, x, :, lo] = add_low(
-                sums[which, yy, x, :, lo], from_one[which, yy, :, lo]
-            )
-        for xx in range(2):
-            sums[which, y, xx, :, hi] = add_low(
-                sums[which, y, xx, :, hi], from_one[which, xx, :, hi]
-            )
-        stage_2[k] = (
-            sends.start(sums.at[which, 1 - y, x, :, lo], from_two.at[which, :, lo], to_y),
-            sends.start(sums.at[which, y, 1 - x, :, hi], from_two.at[which, :, hi], to_x),
-        )
-
-    def after_two(k):
-        which = order[k]
-        for copy in stage_2[k]:
-            copy.wait_recv()
-        if k < nz - 1:
-            sums[which, y, x] = add_low(sums[which, y, x], from_two[which])
-            far[k] = sends.start(sums.at[which, y, x], from_far.at[k], peers[k])
-
-    steps = []
-    small_c.wait_recv()
-    small_sum[0] = small_ref[...] + small_got[0]
-    small_x = sends.start(small_sum.at[0], small_got.at[1], to_x)
-    for n in range(nz + 2):
-        if n < nz:
-            after_core(n)
-        if 1 <= n < nz + 1:
-            after_one(n - 1)
-        if n >= 2:
-            after_two(n - 2)
-        if n == 1:
-            small_x.wait_recv()
-            small_sum[1] = small_sum[0] + small_got[1]
-            small_y = sends.start(small_sum.at[1], small_got.at[2], to_y)
-        if n == 3:
-            small_y.wait_recv()
-            small_sum[2] = small_sum[1] + small_got[2]
-            small_far = [
-                sends.start(small_sum.at[2], small_got.at[3 + k], peer)
-                for k, peer in enumerate(peers)
-            ]
-    total = sums[z, y, x].astype(jnp.float32) + from_two[z].astype(jnp.float32)
-    for k in range(nz - 1):
-        far[k].wait_recv()
-        total = total + from_far[k].astype(jnp.float32)
-    grad_out[...] = total
-    small = small_sum[2]
-    for k in range(nz - 1):
-        small_far[k].wait_recv()
-        small = small + small_got[3 + k]
-    small_out[...] = small
-    sends.finish()
-
-
-def total_all(nz, grad, small):
-    rows, columns = grad.shape[4:]
-    low = jnp.bfloat16
-    count = 5 * nz + (nz - 1) + 3 + (nz - 1)
-    return pl.pallas_call(
-        functools.partial(total_kernel, nz),
-        name="total_all",
-        out_shape=(
-            jax.ShapeDtypeStruct((rows, columns), jnp.float32),
-            jax.ShapeDtypeStruct(small.shape, jnp.float32),
-        ),
-        in_specs=[IN_VMEM] * 2,
-        out_specs=[IN_VMEM] * 2,
-        scratch_shapes=[
-            pltpu.VMEM((nz, 2, 2, rows, columns), low),
-            pltpu.VMEM((nz, 2, 2, rows, columns), low),
-            pltpu.VMEM((nz, 2, rows, columns), low),
-            pltpu.VMEM((nz, rows, columns), low),
-            pltpu.VMEM((nz - 1, rows, columns), low),
-            pltpu.VMEM((3,) + small.shape, jnp.float32),
-            pltpu.VMEM((nz + 2,) + small.shape, jnp.float32),
-            pltpu.SemaphoreType.DMA((count,)),
-            pltpu.SemaphoreType.DMA((count,)),
-        ],
-        compiler_params=pltpu.CompilerParams(
-            collective_id=5, has_side_effects=True, vmem_limit_bytes=60 * 2**20
-        ),
-    )(grad, small)
+    )(*operands)
 
 
 def fused(
@@ -1133,79 +1352,51 @@
     grad_normed_mid, ffn_part, fc1_part, fc2_part, unit_sums = ffn(
         normed_mid, shard_rows, fc1_rows, fc2_cols, unit_rows
     )
-    ffn_out, fc1_grad, fc2_grad, unit_sums = fold(nz, ffn_part, fc1_part, fc2_part, unit_sums)
-    mid_gain_grad, ffn_bias_grad = unit_sums[0], unit_sums[1:3]
-    mixed_out = (middle + ffn_out + bias_full[6]).astype(jnp.bfloat16)
-    final_grad = out_grad.astype(jnp.float32)
-    grad_middle = final_grad + normalize_back(
-        grad_normed_mid * gain_full[2], normed_two, inverse_two
-    )
-    grad_post = normalize_back(grad_middle * gain_full[1], normed_post, inverse_post).astype(
-        jnp.bfloat16
-    )
-    out_local = jnp.einsum("td,te->de", scaled, grad_post, preferred_element_type=jnp.float32)
-    grad_scaled = jnp.einsum("te,de->td", grad_post, out_full, preferred_element_type=jnp.float32)
-    scale_local = jnp.sum(
-        (grad_scaled * attended).reshape(local_rows, HEADS, head_dim), axis=(0, 2)
-    )
-    grad_attended = (
-        (grad_scaled * scale_wide).astype(jnp.bfloat16).reshape(local_rows, HEADS, head_dim)
-    )
-    grad_query, grad_keys, grad_values = attend_backward(
-        query_rows, key_rows, value_rows, grad_attended, doc_ids, sums_log, factor
-    )
-    grad_projected = jnp.concatenate(
-        [
-            grad_query.reshape(local_rows, model_width),
-            grad_keys.reshape(local_rows, model_width),
-            grad_values.reshape(local_rows, model_width),
-        ],
-        axis=1,
-    ).astype(jnp.bfloat16)
-    qkv_local = jnp.einsum(
-        "td,te->de", normed_in, grad_projected, preferred_element_type=jnp.float32
-    )
-    grad_normed_in = jnp.einsum(
-        "te,de->td", grad_projected, qkv_full, preferred_element_type=jnp.float32
-    )
-    token_grad = grad_middle + normalize_back(
-        grad_normed_in * gain_full[0], normed_one, inverse_one
-    )
-    projected_sums = jnp.sum(grad_projected.astype(jnp.float32), axis=0)
-    small = jnp.stack(
-        [
-            jnp.sum(grad_normed_in * normed_one, axis=0),
-            jnp.sum(grad_middle * normed_post, axis=0),
-            jnp.sum(grad_normed_mid * normed_two, axis=0),
-            jnp.sum(grad_normed_in, axis=0),
-            projected_sums[:model_width],
-            projected_sums[2 * model_width :],
-            jnp.sum(grad_post.astype(jnp.float32), axis=0),
-            jnp.sum(grad_middle, axis=0),
-            jnp.sum(grad_normed_mid, axis=0),
-            jnp.sum(final_grad, axis=0),
-            jnp.pad(scale_local, (0, model_width - HEADS)),
-        ]
-        + [jnp.zeros((model_width,), jnp.float32)] * 5
-    )
-    weights = jnp.concatenate(
-        [qkv_local.astype(jnp.bfloat16), out_local.astype(jnp.bfloat16)], axis=1
-    ).reshape(nz, 2, 2, 2, share, -1)
-    weight_grad, small = total_all(nz, weights, small)
-    index = lax.axis_index("dp") * 8 + lax.axis_index("tensor")
-    ours = lax.dynamic_slice(small, (0, index * share), (10, share)).T
+    lse = jnp.pad(sums_log[0][:, :, 0].T, ((0, 0), (0, 128 - HEADS)))
+    vec = jnp.concatenate([vec_rows, scale_wide[None], jnp.zeros((5, model_width), jnp.float32)])
+    (
+        mixed_out,
+        token_grad,
+        weight_grad,
+        gains_grad,
+        biases_grad,
+        scale_sums,
+        fc1_grad,
+        fc2_grad,
+        unit_sums,
+    ) = back(
+        nz,
+        grad_normed_mid,
+        ffn_part,
+        fc1_part,
+        fc2_part,
+        unit_sums,
+        projected,
+        attended,
+        lse,
+        branch,
+        middle,
+        scaled,
+        normed_in,
+        qkv_full,
+        out_full,
+        vec,
+        out_grad,
+        tokens,
+        doc_lengths,
+    )
     return (
         mixed_out,
         token_grad,
         weight_grad[:, : w_qkv.shape[1]],
         weight_grad[:, w_qkv.shape[1] :],
-        ours[:, :3],
-        ours[:, 3:],
-        small[10, :HEADS],
+        gains_grad,
+        biases_grad,
+        jnp.sum(scale_sums[2].reshape(HEADS, head_dim), axis=1),
         fc1_grad,
         fc2_grad,
-        mid_gain_grad,
-        ffn_bias_grad,
+        unit_sums[0],
+        unit_sums[1:3],
     )
 
 

time: 390 us -> 301 us (0.77)
  the two profiles are of different devices: /device:TPU:9 before, /device:TPU:0 now
where the time goes in v3:
time: 301 us; the launch traced here: 300 us
  Pallas kernels  257 us (85%)
  local copies, waits for them, and re-layouts  24.6 us (8%)
  other arithmetic  8.91 us (3%)
  matrix products  8.69 us (3%)
    pallas_call x1, Pallas kernels, back(): pl.pallas_call(functools.partial(back_kernel, nz), name='back', out_shape...  105 us
    pallas_call x1, Pallas kernels, gather(): pl.pallas_call(functools.partial(gather_kernel, nz), name='gather', out_s...  87.6 us
    pallas_call x1, Pallas kernels, ffn(): pl.pallas_call(ffn_kernel, name='ffn', out_shape=(sds((rows, width), jnp....  64.3 us
    unnamed x35, local copies, waits for them, and re-layouts  13.8 us

profile of v3, /device:TPU:0, one launch (start us, length us, event | category | flops | bytes accessed | tf_op | source)
XLA Modules:
  0.0 299.9 jit_solution(260188046214673026)
XLA Ops:
  2.9 87.6 %gather.1 = (bf16[4,2,2,2,32,3072]{5,4,3,2,1,0:T(8,128)(2,1)}, bf16[4,2,2,2,32,1024]{5,4,3,2,1,0:T(8,128)(2,1)}, f32[4,2,2,2,32,128]{5,4,3,2,1,0:T(8,128)}, bf16...) custom-call(bf16[32,3072]{1,0:T(8,128)(2,1)} %qkv_ref.1, ...), custom_call_target="tpu_custom_call" | custom-call | tf_op jit(solution)/shard_map/gather/pallas_call | solution.py:465
  90.6 1.2 copy.87
  91.8 1.3 convert_reduce_fusion
  93.1 1.3 fusion.7.nin_ref
  94.5 4.8 %fusion.proj_ref = bf16[256,3072]{1,0:T(8,128)(2,1)S(1)} fusion(bf16[256,1024]{1,0:T(8,128)(2,1)S(1)} %fusion.7.nin_ref, bf16[1024,3072]{1,0:T(8,128)(2,1)} %bitcast.39, f32[3072]{0:T(1024)S(1)} %pad_maximum_fusion), kind=kOutput, calls=%fused_computation.4 | convolution fusion | flops 1612185600 | bytes 8400896 | tf_op jit(solution)/shard_map/dot_general | solution.py:1334
  99.3 1.1 copy-done.5
  101.9 0.8 fusion.1
  102.7 0.9 fusion.2
  103.6 2.2 fusion.10
  105.8 0.9 fusion.15
  106.8 1.9 copy.83.att_ref
  108.9 1.3 fusion.14
  110.2 1.0 copy-done.2
  111.2 1.0 add_convert_fusion.mid_ref
  113.0 64.3 %ffn.1 = (f32[256,1024]{1,0:T(8,128)}, bf16[2,2,2,256,1024]{4,3,2,1,0:T(8,128)(2,1)}, bf16[1024,512]{1,0:T(8,128)(2,1)}, bf16[512,1024]{1,0:T(8,128)(2,1)}, f32[8,512]{1,0:T(8,128)}) custom-call(bf16[256,1024]{1,0:T(8,128)(2,1)} %add_convert_fusion.mid_ref, bf16[2,2,2,256,1024]{4,3,2,1,0:T(8,128)(2,1)} %get-tuple-element.34.og_ref, ...), custom_call_target="tpu_custom_call" | custom-call | tf_op jit(solution)/shard_map/ffn/pallas_call | solution.py:752
  179.0 104.8 %back.1 = (bf16[256,1024]{1,0:T(8,128)(2,1)}, f32[256,1024]{1,0:T(8,128)}, f32[32,4096]{1,0:T(8,128)}, f32[32,3]{1,0:T(8,128)}, f32[32,7]{1,0:T(8,128)}, /*index...) custom-call(f32[256,1024]{1,0:T(8,128)} %get-tuple-element.37.gnm_ref, ...), custom_call_target="tpu_custom_call" | custom-call | tf_op jit(solution)/shard_map/back/pallas_call | solution.py:1241
  283.8 1.9 slice.91
  285.7 1.6 slice.92
  287.2 1.4 copy.84
  288.6 1.4 copy.85
  291.5 1.3 slice.94
  292.8 1.3 slice.95
  294.1 1.9 copy.92
  296.0 2.3 copy.93
  (60 shorter events, 9.4 us)
Async XLA Ops:
  94.4 4.8 %copy-start.6 = (bf16[256,1024]{1,0:T(8,128)(2,1)}, bf16[256,1024]{1,0:T(8,128)(2,1)S(1)}, u32[]{:S(2)}) copy-start(bf16[256,1024]{1,0:T(8,128)(2,1)S(1)} %fusion.7.nin_ref) | copy-start | bytes 1572868
  99.3 1.2 copy-start.5
  100.4 0.7 copy-start.11
  101.9 1.7 copy-start.12
  103.6 2.2 copy-start.4
  105.8 3.0 %copy-start.3 = (bf16[256,1024]{1,0:T(8,128)(2,1)S(1)}, bf16[256,1024]{1,0:T(8,128)(2,1)}, u32[]{:S(2)}) copy-start(bf16[256,1024]{1,0:T(8,128)(2,1)} %tok_ref.1) | copy-start | bytes 1572868
  106.7 2.1 copy-start
  106.7 5.5 %copy-start.9 = (f32[2,512]{1,0:T(2,128)S(1)}, f32[2,512]{1,0:T(2,128)}, u32[]{:S(2)}) copy-start(f32[2,512]{1,0:T(2,128)} %param.23) | copy-start | bytes 12292
  106.7 5.6 %copy-start.10 = (f32[512]{0:T(512)S(1)}, f32[512]{0:T(512)}, u32[]{:S(2)}) copy-start(f32[512]{0:T(512)} %param.22) | copy-start | bytes 6148
  108.7 1.5 copy-start.1
  110.2 1.0 copy-start.2
  283.8 14.5 %copy-start.8 = (f32[256,512]{1,0:T(8,128)S(1)}, f32[256,512]{1,0:T(8,128)}, u32[]{:S(2)}) copy-start(f32[256,512]{1,0:T(8,128)} %get-tuple-element.157) | copy-start | bytes 1572868
  283.8 15.2 %copy-start.7 = (f32[512,256]{1,0:T(8,128)S(1)}, f32[512,256]{1,0:T(8,128)}, u32[]{:S(2)}) copy-start(f32[512,256]{1,0:T(8,128)} %get-tuple-element.158) | copy-start | bytes 1572868

commit v4 on v3

--- a/solution.py
+++ b/solution.py
@@ -320,170 +320,6 @@
             copy.wait_send()
 
 
-def gather_kernel(
-    nz,
-    qkv_ref,
-    out_ref,
-    vec_ref,
-    fc1_ref,
-    fc2_ref,
-    grad_ref,
-    qkv_all,
-    out_all,
-    vec_all,
-    fc1_all,
-    fc2_all,
-    grad_all,
-    local_sems,
-    send_sems,
-    recv_sems,
-):
-    z, y, x, c = place()
-    to_x, to_y, to_c = at(z, y, 1 - x, c), at(z, 1 - y, x, c), at(z, y, x, 1 - c)
-    others = [lax.rem(z + k, nz) for k in range(1, nz)]
-    slots = [z] + [lax.rem(z + nz - k, nz) for k in range(1, nz)]
-    peers = [at(other, y, x, c) for other in others]
-    greet([to_x, to_y, to_c] + peers)
-    sends = Sends(send_sems, recv_sems)
-    shards = ((qkv_ref, qkv_all), (out_ref, out_all))
-    mine = []
-    width1, width2 = fc1_ref.shape[0], fc2_ref.shape[1]
-    own = [
-        (qkv_ref, qkv_all.at[z, y, x, c]),
-        (out_ref, out_all.at[z, y, x, c]),
-        (vec_ref, vec_all.at[z, y, x, c]),
-        (fc1_ref, fc1_all.at[pl.ds(pl.multiple_of(z * width1, width1), width1)]),
-        (fc2_ref, fc2_all.at[:, pl.ds(pl.multiple_of(z * width2, width2), width2)]),
-        (grad_ref, grad_all.at[y, x, c]),
-    ]
-    for index, (src, dst) in enumerate(own):
-        copy = pltpu.make_async_copy(src, dst, local_sems.at[index])
-        copy.start()
-        mine.append(copy)
-
-    def halves(ref):
-        half = ref.shape[-1] // 2
-        return pl.ds(0, half), pl.ds(half, half)
-
-    vec_z = [sends.start(vec_ref, vec_all.at[z, y, x, c], peer) for peer in peers]
-    vec_x = [sends.start(vec_ref, vec_all.at[z, y, x, c], to_x)]
-    qkv_z = [sends.start(qkv_ref, qkv_all.at[z, y, x, c], peer) for peer in peers]
-
-    def first(src, whole, slot, from_input):
-        lo, hi = halves(src)
-        one = src if from_input else whole.at[slot, y, x, c]
-        return (
-            sends.start(one.at[:, lo], whole.at[slot, y, x, c, :, lo], to_x),
-            sends.start(one.at[:, hi], whole.at[slot, y, x, c, :, hi], to_y),
-        )
-
-    def second(whole, slot):
-        lo, hi = halves(whole)
-        return (
-            sends.start(whole.at[slot, y, :, c, :, lo], whole.at[slot, y, :, c, :, lo], to_y),
-            sends.start(whole.at[slot, :, x, c, :, hi], whole.at[slot, :, x, c, :, hi], to_x),
-        )
-
-    def third(whole, slot):
-        return sends.start(whole.at[slot, :, :, c], whole.at[slot, :, :, c], to_c)
-
-    def wait_all(copies):
-        for copy in copies:
-            copy.wait_recv()
-
-    def spread(src, whole, arrivals, between):
-        stage_a = [first(src, whole, z, True)]
-        stage_b = []
-        for k in range(1, nz):
-            arrivals[k - 1].wait_recv()
-            stage_a.append(first(src, whole, slots[k], False))
-            if k == 1:
-                between()
-            if k >= 2:
-                wait_all(stage_a[k - 2])
-                stage_b.append(second(whole, slots[k - 2]))
-        for k in range(len(stage_b), nz):
-            wait_all(stage_a[k])
-            stage_b.append(second(whole, slots[k]))
-        return stage_b
-
-    rest = {}
-
-    def after_qkv_z():
-        rest["out_z"] = [sends.start(out_ref, out_all.at[z, y, x, c], peer) for peer in peers]
-        rest["fc"] = []
-        for peer in peers:
-            rest["fc"].append(sends.start(fc1_ref, own[3][1], peer))
-            rest["fc"].append(sends.start(fc2_ref, own[4][1], peer))
-
-    for copy in mine[:3]:
-        copy.wait()
-    qkv_b = spread(qkv_ref, qkv_all, qkv_z, after_qkv_z)
-    wait_all(vec_z)
-    for k in range(1, nz):
-        vec_x.append(
-            sends.start(vec_all.at[slots[k], y, x, c], vec_all.at[slots[k], y, x, c], to_x)
-        )
-    out_b = spread(out_ref, out_all, rest.get("out_z", []), lambda: None)
-    wait_all(vec_x)
-    vec_y = sends.start(vec_all.at[:, y, :, c], vec_all.at[:, y, :, c], to_y)
-    lo, hi = halves(grad_ref)
-    grad_a = (
-        sends.start(grad_ref.at[:, lo], grad_all.at[y, x, c, :, lo], to_x),
-        sends.start(grad_ref.at[:, hi], grad_all.at[y, x, c, :, hi], to_y),
-    )
-    qkv_c = []
-    for k in range(nz):
-        wait_all(qkv_b[k])
-        qkv_c.append(third(qkv_all, slots[k]))
-    vec_y.wait_recv()
-    vec_c = sends.start(vec_all.at[:, :, :, c], vec_all.at[:, :, :, c], to_c)
-    mine[5].wait()
-    wait_all(grad_a)
-    grad_b = (
-        sends.start(grad_all.at[y, :, c, :, lo], grad_all.at[y, :, c, :, lo], to_y),
-        sends.start(grad_all.at[:, x, c, :, hi], grad_all.at[:, x, c, :, hi], to_x),
-    )
-    out_c = []
-    for k in range(nz):
-        wait_all(out_b[k])
-        out_c.append(third(out_all, slots[k]))
-    wait_all(grad_b)
-    grad_c = sends.start(grad_all.at[:, :, c], grad_all.at[:, :, c], to_c)
-    wait_all(qkv_c + out_c + [vec_c, grad_c] + rest.get("fc", []))
-    mine[3].wait()
-    mine[4].wait()
-    sends.finish()
-
-
-def gather(nz, w_qkv, w_out, vectors, w_fc1, w_fc2, out_grad):
-    def whole(shard, lead):
-        return jax.ShapeDtypeStruct(lead + shard.shape, shard.dtype)
-
-    every, plane = (nz, 2, 2, 2), (2, 2, 2)
-    count = 4 * (nz - 1) + 5 * 2 * nz + 64
-    return pl.pallas_call(
-        functools.partial(gather_kernel, nz),
-        name="gather",
-        out_shape=(
-            whole(w_qkv, every),
-            whole(w_out, every),
-            whole(vectors, every),
-            jax.ShapeDtypeStruct((w_fc1.shape[0] * nz, w_fc1.shape[1]), w_fc1.dtype),
-            jax.ShapeDtypeStruct((w_fc2.shape[0], w_fc2.shape[1] * nz), w_fc2.dtype),
-            whole(out_grad, plane),
-        ),
-        in_specs=[ANY] * 6,
-        out_specs=[ANY] * 6,
-        scratch_shapes=[
-            pltpu.SemaphoreType.DMA((6,)),
-            pltpu.SemaphoreType.DMA((count,)),
-            pltpu.SemaphoreType.DMA((count,)),
-        ],
-        compiler_params=pltpu.CompilerParams(collective_id=1, has_side_effects=True),
-    )(w_qkv, w_out, vectors, w_fc1, w_fc2, out_grad)
-
-
 def add_low(left, right):
     return (left.astype(jnp.float32) + right.astype(jnp.float32)).astype(jnp.bfloat16)
 
@@ -497,296 +333,6 @@
     if dims is None:
         return jnp.dot(left, right, preferred_element_type=jnp.float32)
     return lax.dot_general(left, right, dims, preferred_element_type=jnp.float32)
-
-
-def ffn_kernel(
-    mid_ref,
-    og_ref,
-    fc1_ref,
-    fc2_ref,
-    unit_ref,
-    gnm_out,
-    ffn_part,
-    fc1_part,
-    fc2_part,
-    unit_out,
-    mid_all,
-    act,
-    slope,
-    grad,
-    hidden,
-    grad_pre,
-    mid_part,
-    pre,
-    columns,
-    stats,
-    pair,
-    got,
-    totals,
-    from_core,
-    sums,
-    from_one,
-    from_two,
-    local_sem,
-    send_sems,
-    recv_sems,
-):
-    z, y, x, c = place()
-    to_x, to_y, to_c = at(z, y, 1 - x, c), at(z, 1 - y, x, c), at(z, y, x, 1 - c)
-    to_xy = at(z, 1 - y, 1 - x, c)
-    greet([to_x, to_y, to_c, to_xy])
-    sends = Sends(send_sems, recv_sems)
-    rows = mid_ref.shape[0]
-    width = mid_ref.shape[1]
-    units = fc1_ref.shape[1]
-    half = rows // 2
-    lo, hi = pl.ds(0, half), pl.ds(half, half)
-    one_x = sends.start(mid_ref.at[lo], mid_all.at[y, x, c, lo], to_x)
-    one_y = sends.start(mid_ref.at[hi], mid_all.at[y, x, c, hi], to_y)
-    own_c = sends.start(mid_ref, mid_all.at[y, x, c], to_c)
-    two_y = sends.start(mid_ref.at[lo], mid_all.at[y, x, c, lo], to_y)
-    two_x = sends.start(mid_ref.at[hi], mid_all.at[y, x, c, hi], to_x)
-    mine = pltpu.make_async_copy(mid_ref, mid_all.at[y, x, c], local_sem)
-    mine.start()
-    step = 32
-    lane = lax.broadcasted_iota(jnp.int32, (step, 128), 1)
-
-    def grads(yy, xx, cc):
-        grad[yy, xx, cc] = dot(og_ref[yy, xx, cc], fc2_ref[...], NT)
-
-    def forward(yy, xx, cc):
-        pre[...] = dot(mid_all[yy, xx, cc], fc1_ref[...])
-
-        def block(k, carry):
-            part = pl.ds(pl.multiple_of(k * step, step), step)
-            u = pre[part] + unit_ref[0:1]
-            square = u * u
-            th = jnp.tanh(SQRT_2_PI * u * (1.0 + 0.044715 * square))
-            lift = 0.5 + 0.5 * th
-            a = u * lift
-            act[yy, xx, cc, part] = a
-            slope[yy, xx, cc, part] = lift + (0.5 * SQRT_2_PI) * u * (1.0 - th * th) * (
-                1.0 + (3 * 0.044715) * square
-            )
-            gm = grad[yy, xx, cc, part] * unit_ref[1:2]
-            four = [
-                jnp.sum(a, axis=1, keepdims=True),
-                jnp.sum(a * a, axis=1, keepdims=True),
-                jnp.sum(gm, axis=1, keepdims=True),
-                jnp.sum(gm * a, axis=1, keepdims=True),
-            ]
-            tile = jnp.where(lane == 0, four[0], 0.0)
-            for j in range(1, 4):
-                tile = jnp.where(lane == j, four[j], tile)
-            columns[part] = tile
-            return carry
-
-        lax.fori_loop(0, rows // step, block, 0)
-        stats[yy, xx, cc] = columns[...].T[:8]
-
-    grads(y, x, c)
-    mine.wait()
-    forward(y, x, c)
-    grads(y, x, 1 - c)
-    grads(y, 1 - x, c)
-    one_x.wait_recv()
-    one_y.wait_recv()
-    ref_x, ref_y = mid_all.at[y, 1 - x, c, lo], mid_all.at[1 - y, x, c, hi]
-    three_y = sends.start(ref_x, ref_x, to_y)
-    three_x = sends.start(ref_y, ref_y, to_x)
-    c_one = [sends.start(ref_x, ref_x, to_c), sends.start(ref_y, ref_y, to_c)]
-    grads(1 - y, x, c)
-    own_c.wait_recv()
-    forward(y, x, 1 - c)
-    grads(y, 1 - x, 1 - c)
-    grads(1 - y, x, 1 - c)
-    two_x.wait_recv()
-    two_y.wait_recv()
-    ref_x, ref_y = mid_all.at[y, 1 - x, c, hi], mid_all.at[1 - y, x, c, lo]
-    c_two = [sends.start(ref_x, ref_x, to_c), sends.start(ref_y, ref_y, to_c)]
-    forward(y, 1 - x, c)
-    forward(1 - y, x, c)
-    grads(1 - y, 1 - x, c)
-    grads(1 - y, 1 - x, 1 - c)
-    for copy in c_one + c_two:
-        copy.wait_recv()
-    forward(y, 1 - x, 1 - c)
-    three_x.wait_recv()
-    three_y.wait_recv()
-    ref_xy = mid_all.at[1 - y, 1 - x, c]
-    c_three = sends.start(ref_xy, ref_xy, to_c)
-    forward(1 - y, x, 1 - c)
-    forward(1 - y, 1 - x, c)
-    c_three.wait_recv()
-    forward(1 - y, 1 - x, 1 - c)
-
-    sends.start(stats, got.at[3], to_c).wait_recv()
-    pair[...] = stats[...] + got[3]
-    arrivals = [
-        sends.start(pair, got.at[k], plane) for k, plane in enumerate((to_x, to_y, to_xy))
-    ]
-    for copy in arrivals:
-        copy.wait_recv()
-    total = (pair[...] + got[0]) + (got[1] + got[2])
-    total = total * (1.0 / (units * 8))
-    center, second = total[:, :, :, 0:1], total[:, :, :, 1:2]
-    first, cross = total[:, :, :, 2:3], total[:, :, :, 3:4]
-    inverse = lax.rsqrt(second - center * center + EPS)
-    totals[:, :, :, 0:1] = center
-    totals[:, :, :, 1:2] = inverse
-    totals[:, :, :, 2:3] = first
-    totals[:, :, :, 3:4] = inverse * (cross - center * first)
-    totals[:, :, :, 4:8] = jnp.zeros_like(total[:, :, :, 4:8])
-    unit_out[...] = jnp.zeros_like(unit_out)
-
-    def backward(yy, xx, cc):
-        columns[...] = jnp.concatenate(
-            [totals[yy, xx, cc], jnp.zeros((120, rows), jnp.float32)], axis=0
-        ).T
-
-        def block(k, carry):
-            part = pl.ds(pl.multiple_of(k * step, step), step)
-            center, inverse = columns[part, 0:1], columns[part, 1:2]
-            first, second = columns[part, 2:3], columns[part, 3:4]
-            gain = unit_ref[1:2]
-            g = grad[yy, xx, cc, part]
-            normed = (act[yy, xx, cc, part] - center) * inverse
-            hidden[yy, xx, cc, part] = (normed * gain + unit_ref[2:3]).astype(jnp.bfloat16)
-            back = inverse * (g * gain - first - normed * second)
-            low = (back * slope[yy, xx, cc, part]).astype(jnp.bfloat16)
-            grad_pre[yy, xx, cc, part] = low
-            eight = (step // 8, 8, units)
-            return (
-                carry[0] + jnp.sum((g * normed).reshape(eight), axis=0),
-                carry[1] + jnp.sum(low.astype(jnp.float32).reshape(eight), axis=0),
-                carry[2] + jnp.sum(g.reshape(eight), axis=0),
-            )
-
-        zero = jnp.zeros((8, units), jnp.float32)
-        parts = lax.fori_loop(0, rows // step, block, (zero, zero, zero))
-        for j, part in enumerate(parts):
-            unit_out[j : j + 1] += jnp.sum(part, axis=0, keepdims=True)
-        mid_part[yy, xx, cc] = dot(grad_pre[yy, xx, cc], fc1_ref[...], NT).astype(jnp.bfloat16)
-
-    left, right = pl.ds(0, width // 2), pl.ds(width // 2, width // 2)
-    order = [(1 - y, 1 - x), (y, 1 - x), (1 - y, x), (y, x)]
-    cores = []
-    for yy, xx in order:
-        backward(yy, xx, 1 - c)
-        cores.append(sends.start(mid_part.at[yy, xx, 1 - c], from_core.at[yy, xx], to_c))
-    stage_x, stage_y = [], []
-    for k, (yy, xx) in enumerate(order):
-        backward(yy, xx, c)
-        cores[k].wait_recv()
-        sums[yy, xx] = add_low(mid_part[yy, xx, c], from_core[yy, xx])
-        if k in (0, 1):
-            stage_x.append(
-                sends.start(sums.at[yy, xx, :, left], from_one.at[0, yy, :, left], to_x)
-            )
-        if k in (0, 2):
-            stage_y.append(
-                sends.start(sums.at[yy, xx, :, right], from_one.at[1, xx, :, right], to_y)
-            )
-
-    def ffn_of(yy, xx, cc):
-        ffn_part[yy, xx, cc] = dot(hidden[yy, xx, cc], fc2_ref[...]).astype(jnp.bfloat16)
-
-    for yy, xx in order[:2]:
-        ffn_of(yy, xx, 1 - c)
-        ffn_of(yy, xx, c)
-    for copy in (stage_x[0], stage_y[0]):
-        copy.wait_recv()
-    sums[1 - y, x, :, left] = add_low(sums[1 - y, x, :, left], from_one[0, 1 - y, :, left])
-    sums[y, 1 - x, :, right] = add_low(sums[y, 1 - x, :, right], from_one[1, 1 - x, :, right])
-    last_y = sends.start(sums.at[1 - y, x, :, left], from_two.at[:, left], to_y)
-    last_x = sends.start(sums.at[y, 1 - x, :, right], from_two.at[:, right], to_x)
-    for yy, xx in order[2:]:
-        ffn_of(yy, xx, 1 - c)
-        ffn_of(yy, xx, c)
-    blocks = 4
-
-    def fc1_block(k, carry):
-        part = pl.ds(pl.multiple_of(k * (width // blocks), 128), width // blocks)
-        block = jnp.zeros((width // blocks, units), jnp.float32)
-        for j in range(8):
-            yxc = (j // 4, (j // 2) % 2, j % 2)
-            block = block + dot(mid_all[(*yxc, slice(None), part)], grad_pre[yxc], TN)
-        fc1_part[part] = block.astype(jnp.bfloat16)
-        return carry
-
-    def fc2_block(k, carry):
-        part = pl.ds(pl.multiple_of(k * (width // blocks), 128), width // blocks)
-        block = jnp.zeros((units, width // blocks), jnp.float32)
-        for j in range(8):
-            yxc = (j // 4, (j // 2) % 2, j % 2)
-            block = block + dot(hidden[yxc], og_ref[(*yxc, slice(None), part)], TN)
-        fc2_part[:, part] = block.astype(jnp.bfloat16)
-        return carry
-
-    lax.fori_loop(0, blocks, fc1_block, 0)
-    for copy in (stage_x[1], stage_y[1]):
-        copy.wait_recv()
-    lax.fori_loop(0, blocks, fc2_block, 0)
-    last_x.wait_recv()
-    last_y.wait_recv()
-    own = sums[y, x].astype(jnp.float32)
-    gnm_out[:, left] = (
-        own[:, : width // 2]
-        + from_one[0, y, :, left].astype(jnp.float32)
-        + from_two[:, left].astype(jnp.float32)
-    )
-    gnm_out[:, right] = (
-        own[:, width // 2 :]
-        + from_one[1, x, :, right].astype(jnp.float32)
-        + from_two[:, right].astype(jnp.float32)
-    )
-    sends.finish()
-
-
-def ffn(mid, og_all, fc1, fc2, unit_rows):
-    rows, width = mid.shape
-    units = fc1.shape[1]
-    low, plane = jnp.bfloat16, (2, 2, 2)
-    sds = jax.ShapeDtypeStruct
-    count = 32
-    return pl.pallas_call(
-        ffn_kernel,
-        name="ffn",
-        out_shape=(
-            sds((rows, width), jnp.float32),
-            sds(plane + (rows, width), low),
-            sds(fc1.shape, low),
-            sds(fc2.shape, low),
-            sds((8, units), jnp.float32),
-        ),
-        in_specs=[IN_VMEM] * 5,
-        out_specs=[IN_VMEM] * 5,
-        scratch_shapes=[
-            pltpu.VMEM(plane + (rows, width), low),
-            pltpu.VMEM(plane + (rows, units), jnp.float32),
-            pltpu.VMEM(plane + (rows, units), jnp.float32),
-            pltpu.VMEM(plane + (rows, units), jnp.float32),
-            pltpu.VMEM(plane + (rows, units), low),
-            pltpu.VMEM(plane + (rows, units), low),
-            pltpu.VMEM(plane + (rows, width), low),
-            pltpu.VMEM((rows, units), jnp.float32),
-            pltpu.VMEM((rows, 128), jnp.float32),
-            pltpu.VMEM(plane + (8, rows), jnp.float32),
-            pltpu.VMEM(plane + (8, rows), jnp.float32),
-            pltpu.VMEM((4,) + plane + (8, rows), jnp.float32),
-            pltpu.VMEM(plane + (8, rows), jnp.float32),
-            pltpu.VMEM((2, 2, rows, width), low),
-            pltpu.VMEM((2, 2, rows, width), low),
-            pltpu.VMEM((2, 2, rows, width), low),
-            pltpu.VMEM((rows, width), low),
-            pltpu.SemaphoreType.DMA,
-            pltpu.SemaphoreType.DMA((count,)),
-            pltpu.SemaphoreType.DMA((count,)),
-        ],
-        compiler_params=pltpu.CompilerParams(
-            collective_id=2, has_side_effects=True, vmem_limit_bytes=62 * 2**20
-        ),
-    )(mid, og_all, fc1, fc2, unit_rows)
 
 
 def centered(values):
@@ -817,6 +363,574 @@
         key_doc = key_doc + (key >= end).astype(jnp.int32)
     allowed = jnp.logical_and(query_doc == key_doc, key <= query)
     return allowed.astype(jnp.float32)
+
+
+class Plane:
+    def __init__(self, sends, whole, here, targets):
+        self.sends, self.whole, self.here, self.targets = sends, whole, here, targets
+        half = whole.shape[3] // 2
+        self.lo, self.hi = pl.ds(0, half), pl.ds(half, half)
+
+    def part(self, y, x, c, rows):
+        return self.whole.at[y, x, c, rows]
+
+    def start(self, src):
+        (y, x, c), (to_x, to_y, to_c), lo, hi = self.here, self.targets, self.lo, self.hi
+        go = self.sends.start
+        self.first = [
+            go(src.at[lo], self.part(y, x, c, lo), to_x),
+            go(src.at[hi], self.part(y, x, c, hi), to_y),
+        ]
+        self.core = [go(src, self.whole.at[y, x, c], to_c)]
+        self.second = [
+            go(src.at[lo], self.part(y, x, c, lo), to_y),
+            go(src.at[hi], self.part(y, x, c, hi), to_x),
+        ]
+
+    def after_first(self):
+        (y, x, c), (to_x, to_y, to_c), lo, hi = self.here, self.targets, self.lo, self.hi
+        for copy in self.first:
+            copy.wait_recv()
+        by_x, by_y = self.part(y, 1 - x, c, lo), self.part(1 - y, x, c, hi)
+        go = self.sends.start
+        self.third = [go(by_x, by_x, to_y), go(by_y, by_y, to_x)]
+        self.side = [go(by_x, by_x, to_c), go(by_y, by_y, to_c)]
+
+    def after_second(self):
+        (y, x, c), (to_x, to_y, to_c), lo, hi = self.here, self.targets, self.lo, self.hi
+        for copy in self.second:
+            copy.wait_recv()
+        by_x, by_y = self.part(y, 1 - x, c, hi), self.part(1 - y, x, c, lo)
+        go = self.sends.start
+        self.side += [go(by_x, by_x, to_c), go(by_y, by_y, to_c)]
+
+    def after_third(self):
+        y, x, c = self.here
+        for copy in self.third:
+            copy.wait_recv()
+        ref = self.whole.at[1 - y, 1 - x, c]
+        self.last = self.sends.start(ref, ref, self.targets[2])
+
+
+def fore_kernel(
+    nz,
+    tok_ref,
+    og_ref,
+    qkv_ref,
+    out_ref,
+    gains_ref,
+    biases_ref,
+    fc1_ref,
+    fc2_ref,
+    unit_ref,
+    doc_ref,
+    scale_ref,
+    qkv_out,
+    out_out,
+    vec_out,
+    proj_out,
+    att_out,
+    lse_out,
+    branch_out,
+    middle_out,
+    nin_out,
+    scaled_out,
+    ffn_out,
+    fc1_out,
+    fc2_out,
+    gnm_out,
+    unit_out,
+    qkv_all,
+    out_all,
+    vec_all,
+    vec_mine,
+    fc1_all,
+    fc2_all,
+    og_all,
+    tok,
+    branch,
+    nin,
+    proj,
+    att,
+    lse,
+    scaled,
+    middle,
+    mask,
+    vec,
+    mid_all,
+    act,
+    slope,
+    grad,
+    hidden,
+    grad_pre,
+    mid_part,
+    pre,
+    stats,
+    pair,
+    got,
+    totals,
+    from_core,
+    sums,
+    from_one,
+    from_two,
+    ffn_part,
+    fc1_part,
+    fc2_part,
+    local_sems,
+    send_sems,
+    recv_sems,
+):
+    z, y, x, c = place()
+    to_x, to_y, to_c = at(z, y, 1 - x, c), at(z, 1 - y, x, c), at(z, y, x, 1 - c)
+    to_xy = at(z, 1 - y, 1 - x, c)
+    others = [lax.rem(z + k, nz) for k in range(1, nz)]
+    slots = [z] + [lax.rem(z + nz - k, nz) for k in range(1, nz)]
+    peers = [at(other, y, x, c) for other in others]
+    greet([to_x, to_y, to_c, to_xy] + peers)
+    sends = Sends(send_sems, recv_sems)
+    low, f32 = jnp.bfloat16, jnp.float32
+    rows, width = tok.shape
+    units = fc1_all.shape[1]
+    width1, width2 = fc1_ref.shape[0], fc2_ref.shape[1]
+    own1 = fc1_all.at[pl.ds(pl.multiple_of(z * width1, width1), width1)]
+    own2 = fc2_all.at[:, pl.ds(pl.multiple_of(z * width2, width2), width2)]
+    locals_ = []
+
+    def fetch(src, dst):
+        copy = pltpu.make_async_copy(src, dst, local_sems.at[len(locals_)])
+        copy.start()
+        locals_.append(copy)
+        return copy
+
+    def wait_all(copies):
+        for copy in copies:
+            copy.wait_recv()
+
+    vec_mine[...] = jnp.zeros_like(vec_mine)
+    vec_mine[:, 0:3] = gains_ref[...]
+    vec_mine[:, 3:10] = biases_ref[...]
+    vec_z = [sends.start(vec_mine, vec_all.at[z, y, x, c], peer) for peer in peers]
+    qkv_z = [sends.start(qkv_ref, qkv_all.at[z, y, x, c], peer) for peer in peers]
+
+    def halves(ref):
+        half = ref.shape[-1] // 2
+        return pl.ds(0, half), pl.ds(half, half)
+
+    def first(src, whole, slot):
+        lo, hi = halves(whole)
+        one = src if src is not None else whole.at[slot, y, x, c]
+        return (
+            sends.start(one.at[:, lo], whole.at[slot, y, x, c, :, lo], to_x),
+            sends.start(one.at[:, hi], whole.at[slot, y, x, c, :, hi], to_y),
+        )
+
+    def second(whole, slot):
+        lo, hi = halves(whole)
+        by_x, by_y = whole.at[slot, y, :, c, :, lo], whole.at[slot, :, x, c, :, hi]
+        return (sends.start(by_x, by_x, to_y), sends.start(by_y, by_y, to_x))
+
+    def third(whole, slot):
+        ref = whole.at[slot, :, :, c]
+        return sends.start(ref, ref, to_c)
+
+    qkv_a = [first(qkv_ref, qkv_all, z)]
+    tok_in = fetch(tok_ref, tok)
+    qkv_in = fetch(qkv_ref, qkv_all.at[z, y, x, c])
+    out_in = fetch(out_ref, out_all.at[z, y, x, c])
+    fc1_in = fetch(fc1_ref, own1)
+    fc2_in = fetch(fc2_ref, own2)
+    og_in = fetch(og_ref, og_all.at[y, x, c])
+    vec_all[z, y, x, c] = vec_mine[...]
+    mask[...] = doc_mask(doc_ref, rows)
+    step = 32
+    tok_in.wait()
+
+    def normed(k, carry):
+        part = pl.ds(pl.multiple_of(k * step, step), step)
+        branch[part] = centered(tok[part].astype(f32))[0]
+        return carry
+
+    lax.fori_loop(0, rows // step, normed, 0)
+    wait_all(vec_z)
+    by_x = vec_all.at[:, y, x, c]
+    vec_x = sends.start(by_x, by_x, to_x)
+    qkv_z[0].wait_recv()
+    qkv_a.append(first(None, qkv_all, slots[1]))
+    vec_x.wait_recv()
+    by_y = vec_all.at[:, y, :, c]
+    vec_y = sends.start(by_y, by_y, to_y)
+    qkv_in.wait()
+    wait_all(qkv_a[0])
+    qkv_b = [second(qkv_all, slots[0])]
+    vec_y.wait_recv()
+    by_c = vec_all.at[:, :, :, c]
+    vec_c = sends.start(by_c, by_c, to_c)
+    for k in range(2, nz):
+        qkv_z[k - 1].wait_recv()
+        qkv_a.append(first(None, qkv_all, slots[k]))
+    out_z = [sends.start(out_ref, out_all.at[z, y, x, c], peer) for peer in peers]
+    pair_peer = at(z + 1 - 2 * lax.rem(z, 2), y, x, c)
+    far_peer = peers[1]
+    fc2_far = sends.start(fc2_ref, own2, far_peer)
+    fc2_near = sends.start(fc2_ref, own2, pair_peer)
+    fc1_z = [sends.start(fc1_ref, own1, peer) for peer in peers]
+    vec_c.wait_recv()
+    rows16 = vec_all[...].reshape(width, 128).T[:16]
+    vec[...] = rows16
+    spot = lax.broadcasted_iota(jnp.int32, (1, width), 1)
+    head = 64
+    wide = jnp.zeros((1, width), f32)
+    for h in range(HEADS):
+        inside = jnp.logical_and(spot >= h * head, spot < (h + 1) * head)
+        wide = jnp.where(inside, scale_ref[h], wide)
+    vec[10:11] = wide
+
+    def scaled_in(k, carry):
+        part = pl.ds(pl.multiple_of(k * step, step), step)
+        nin[part] = (branch[part] * vec[0:1] + vec[3:4]).astype(low)
+        return carry
+
+    lax.fori_loop(0, rows // step, scaled_in, 0)
+    for k in range(1, nz):
+        wait_all(qkv_a[k])
+        qkv_b.append(second(qkv_all, slots[k]))
+    out_a = [first(out_ref, out_all, z)]
+    for k in range(1, nz):
+        out_z[k - 1].wait_recv()
+        out_a.append(first(None, out_all, slots[k]))
+    og = Plane(sends, og_all, (y, x, c), (to_x, to_y, to_c))
+    og.start(og_ref)
+    qkv_c = []
+    for k in range(nz):
+        wait_all(qkv_b[k])
+        qkv_c.append(third(qkv_all, slots[k]))
+    wait_all(qkv_c)
+    saves = [fetch(qkv_all, qkv_out), fetch(vec, vec_out), fetch(nin, nin_out)]
+
+    tile = width // 2
+    for k in range(6):
+        cols = pl.ds(k * tile, tile)
+        block = dot(nin[...], qkv_all[:, :, :, :, :, cols].reshape(width, tile))
+        if k < 2:
+            block = block + vec[4:5, cols]
+        if k >= 4:
+            block = block + vec[5:6, pl.ds((k - 4) * tile, tile)]
+        proj[:, cols] = block.astype(low)
+    saves.append(fetch(proj, proj_out))
+    out_in.wait()
+    out_b = []
+    for k in range(nz):
+        wait_all(out_a[k])
+        out_b.append(second(out_all, slots[k]))
+    lane = lax.broadcasted_iota(jnp.int32, (1, 128), 1)
+    is_low = lane < head
+    keep = (is_low.astype(low), (lane >= head).astype(low))
+    factor = 1.0 / math.sqrt(head)
+    lane_wide = lax.broadcasted_iota(jnp.int32, (rows, 128), 1)
+    lse[...] = jnp.zeros_like(lse)
+
+    def attend(p, carry):
+        q_at = pl.ds(pl.multiple_of(p * 128, 128), 128)
+        k_at = pl.ds(pl.multiple_of(width + p * 128, 128), 128)
+        v_at = pl.ds(pl.multiple_of(2 * width + p * 128, 128), 128)
+        q2, k2, v2 = proj[:, q_at], proj[:, k_at], proj[:, v_at]
+        found = []
+        for i in range(2):
+            scores = dot(q2 * keep[i], k2, NT) * factor
+            scores = jnp.where(mask[...] > 0, scores, NEGATIVE)
+            peak = jnp.max(scores, axis=1, keepdims=True)
+            exponent = jnp.exp(scores - peak)
+            total = jnp.sum(exponent, axis=1, keepdims=True)
+            prob = (exponent * (1.0 / total)).astype(low)
+            found.append(dot(prob, v2))
+            lse[...] = jnp.where(lane_wide == 2 * p + i, peak + jnp.log(total), lse[...])
+        both = jnp.where(is_low, *found)
+        att[:, q_at] = both
+        scaled[:, q_at] = (both * vec[10:11, q_at]).astype(low)
+        return carry
+
+    lax.fori_loop(0, 4, attend, 0)
+    og.after_first()
+    out_c = []
+    for k in range(nz):
+        wait_all(out_b[k])
+        out_c.append(third(out_all, slots[k]))
+    lax.fori_loop(4, 8, attend, 0)
+    saves += [fetch(att, att_out), fetch(lse, lse_out), fetch(scaled, scaled_out)]
+    wait_all(out_c)
+    saves.append(fetch(out_all, out_out))
+    quarter = width // 4
+    for k in range(4):
+        cols = pl.ds(k * quarter, quarter)
+        block = dot(scaled[...], out_all[:, :, :, :, :, cols].reshape(width, quarter))
+        branch[:, cols] = block + vec[6:7, cols]
+
+    def middles(k, carry):
+        part = pl.ds(pl.multiple_of(k * step, step), step)
+        post = centered(branch[part])[0]
+        value = tok[part].astype(f32) + post * vec[1:2] + vec[7:8]
+        middle[part] = value
+        mid_all[y, x, c, part] = (centered(value)[0] * vec[2:3] + vec[8:9]).astype(low)
+        return carry
+
+    lax.fori_loop(0, rows // step, middles, 0)
+    mid = Plane(sends, mid_all, (y, x, c), (to_x, to_y, to_c))
+    mid.start(mid_all.at[y, x, c])
+    saves += [fetch(branch, branch_out), fetch(middle, middle_out)]
+
+    def grads(yy, xx, cc):
+        grad[yy, xx, cc] = dot(og_all[yy, xx, cc], fc2_all[...], NT)
+
+    def fold(v):
+        quarters = [v[:, k * (units // 4) : (k + 1) * (units // 4)] for k in range(4)]
+        return (quarters[0] + quarters[1]) + (quarters[2] + quarters[3])
+
+    def forward(yy, xx, cc):
+        pre[...] = dot(mid_all[yy, xx, cc], fc1_all[...])
+
+        def block(k, carry):
+            part = pl.ds(pl.multiple_of(k * step, step), step)
+            u = pre[part] + unit_ref[0:1]
+            square = u * u
+            th = jnp.tanh(u * (SQRT_2_PI + (SQRT_2_PI * 0.044715) * square))
+            lift = 0.5 + 0.5 * th
+            a = u * lift
+            act[yy, xx, cc, part] = a
+            bend = u * (2.0 * SQRT_2_PI + (6.0 * 0.044715 * SQRT_2_PI) * square)
+            slope[yy, xx, cc, part] = lift + bend * (lift - lift * lift)
+            gm = grad[yy, xx, cc, part] * unit_ref[1:2]
+            for j, value in enumerate((a, a * a, gm, gm * a)):
+                pre[part, j * (units // 4) : (j + 1) * (units // 4)] = fold(value)
+            return carry
+
+        lax.fori_loop(0, rows // step, block, 0)
+        for j in range(4):
+            folded = pre[:, j * (units // 4) : (j + 1) * (units // 4)]
+            stats[yy, xx, cc, j : j + 1] = jnp.sum(folded.T, axis=0, keepdims=True)
+
+    stats[...] = jnp.zeros_like(stats)
+    og.after_second()
+    fc2_in.wait()
+    fc2_far.wait_recv()
+    near = fc2_all.at[:, pl.ds(pl.multiple_of(others[1] * width2, width2), width2)]
+    fc2_last = sends.start(near, near, pair_peer)
+    fc2_near.wait_recv()
+    og.after_third()
+    fc1_in.wait()
+    mid.after_first()
+    fc2_last.wait_recv()
+    og_in.wait()
+    grads(y, x, c)
+    wait_all(og.core)
+    grads(y, x, 1 - c)
+    grads(y, 1 - x, c)
+    grads(1 - y, x, c)
+    mid.after_second()
+    wait_all(og.side)
+    grads(y, 1 - x, 1 - c)
+    grads(1 - y, x, 1 - c)
+    grads(1 - y, 1 - x, c)
+    og.last.wait_recv()
+    grads(1 - y, 1 - x, 1 - c)
+    wait_all(fc1_z)
+    forward(y, x, c)
+    wait_all(mid.core)
+    forward(y, x, 1 - c)
+    mid.after_third()
+    forward(y, 1 - x, c)
+    forward(1 - y, x, c)
+    wait_all(mid.side)
+    forward(y, 1 - x, 1 - c)
+    forward(1 - y, x, 1 - c)
+    forward(1 - y, 1 - x, c)
+    mid.last.wait_recv()
+    forward(1 - y, 1 - x, 1 - c)
+
+    sends.start(stats, got.at[3], to_c).wait_recv()
+    pair[...] = stats[...] + got[3]
+    wait_all([sends.start(pair, got.at[k], to) for k, to in enumerate((to_x, to_y, to_xy))])
+    total = (pair[...] + got[0]) + (got[1] + got[2])
+    total = total * (1.0 / (units * 8))
+    center, square = total[:, :, :, 0:1], total[:, :, :, 1:2]
+    mean, cross = total[:, :, :, 2:3], total[:, :, :, 3:4]
+    inverse = lax.rsqrt(square - center * center + EPS)
+    totals[:, :, :, 0:1] = inverse
+    totals[:, :, :, 1:2] = -center * inverse
+    totals[:, :, :, 2:3] = inverse * mean
+    totals[:, :, :, 3:4] = inverse * (inverse * (cross - center * mean))
+    unit_out[...] = jnp.zeros_like(unit_out)
+
+    def backward(yy, xx, cc):
+        for j in range(4):
+            spread = jnp.broadcast_to(totals[yy, xx, cc, j : j + 1], (128, rows))
+            pre[:, j * 128 : (j + 1) * 128] = spread.T
+
+        def block(k, carry):
+            part = pl.ds(pl.multiple_of(k * step, step), step)
+
+            def across(j):
+                return jnp.concatenate([pre[part, j * 128 : (j + 1) * 128]] * (units // 128), axis=1)
+
+            g = grad[yy, xx, cc, part]
+            inverse = across(0)
+            normed = act[yy, xx, cc, part] * inverse + across(1)
+            gain = unit_ref[1:2]
+            hidden[yy, xx, cc, part] = (normed * gain + unit_ref[2:3]).astype(low)
+            back = g * gain * inverse - across(2) - normed * across(3)
+            value = (back * slope[yy, xx, cc, part]).astype(low)
+            grad_pre[yy, xx, cc, part] = value
+            return (
+                carry[0] + eights(g * normed),
+                carry[1] + eights(value.astype(f32)),
+                carry[2] + eights(g),
+            )
+
+        zero = jnp.zeros((8, units), f32)
+        parts = lax.fori_loop(0, rows // step, block, (zero, zero, zero))
+        for j, part in enumerate(parts):
+            unit_out[j : j + 1] += jnp.sum(part, axis=0, keepdims=True)
+        return dot(grad_pre[yy, xx, cc], fc1_all[...], NT)
+
+    left, right = pl.ds(0, width // 2), pl.ds(width // 2, width // 2)
+    order = [(1 - y, 1 - x), (y, 1 - x), (1 - y, x), (y, x)]
+    stage_x, stage_y = [], []
+    for k, (yy, xx) in enumerate(order):
+        mid_part[yy, xx] = backward(yy, xx, 1 - c).astype(low)
+        core = sends.start(mid_part.at[yy, xx], from_core.at[yy, xx], to_c)
+        block = backward(yy, xx, c)
+        core.wait_recv()
+        sums[yy, xx] = (block + from_core[yy, xx].astype(f32)).astype(low)
+        if k in (0, 1):
+            stage_x.append(sends.start(sums.at[yy, xx, :, left], from_one.at[yy, :, left], to_x))
+        if k in (0, 2):
+            stage_y.append(sends.start(sums.at[yy, xx, :, right], from_one.at[xx, :, right], to_y))
+
+    def ffn_of(yy, xx, cc):
+        ffn_part[yy, xx, cc] = dot(hidden[yy, xx, cc], fc2_all[...]).astype(low)
+
+    for yy, xx in order[:2]:
+        ffn_of(yy, xx, 1 - c)
+        ffn_of(yy, xx, c)
+    wait_all((stage_x[0], stage_y[0]))
+    sums[1 - y, x, :, left] = add_low(sums[1 - y, x, :, left], from_one[1 - y, :, left])
+    sums[y, 1 - x, :, right] = add_low(sums[y, 1 - x, :, right], from_one[1 - x, :, right])
+    last_y = sends.start(sums.at[1 - y, x, :, left], from_two.at[:, left], to_y)
+    last_x = sends.start(sums.at[y, 1 - x, :, right], from_two.at[:, right], to_x)
+    for yy, xx in order[2:]:
+        ffn_of(yy, xx, 1 - c)
+        ffn_of(yy, xx, c)
+    saves.append(fetch(ffn_part, ffn_out))
+    blocks = 4
+
+    def fc1_block(k, carry):
+        part = pl.ds(pl.multiple_of(k * (width // blocks), 128), width // blocks)
+        block = jnp.zeros((width // blocks, units), f32)
+        for j in range(8):
+            yxc = (j // 4, (j // 2) % 2, j % 2)
+            block = block + dot(mid_all[(*yxc, slice(None), part)], grad_pre[yxc], TN)
+        fc1_part[part] = block.astype(low)
+        return carry
+
+    def fc2_block(k, carry):
+        part = pl.ds(pl.multiple_of(k * (width // blocks), 128), width // blocks)
+        block = jnp.zeros((units, width // blocks), f32)
+        for j in range(8):
+            yxc = (j // 4, (j // 2) % 2, j % 2)
+            block = block + dot(hidden[yxc], og_all[(*yxc, slice(None), part)], TN)
+        fc2_part[:, part] = block.astype(low)
+        return carry
+
+    lax.fori_loop(0, blocks, fc1_block, 0)
+    saves.append(fetch(fc1_part, fc1_out))
+    lax.fori_loop(0, blocks, fc2_block, 0)
+    saves.append(fetch(fc2_part, fc2_out))
+    wait_all((stage_x[1], stage_y[1], last_x, last_y))
+    for cols, k in ((left, y), (right, x)):
+        gnm_out[:, cols] = (
+            sums[y, x, :, cols].astype(f32)
+            + from_one[k, :, cols].astype(f32)
+            + from_two[:, cols].astype(f32)
+        )
+    for copy in saves:
+        copy.wait()
+    sends.finish()
+
+
+def fore(nz, tokens, og, doc_lengths, w_qkv, w_out, gains, biases, scale, fc1, fc2, unit_rows):
+    rows, width = tokens.shape
+    share, units = w_qkv.shape[0], fc1.shape[1]
+    low, f32, plane, every = jnp.bfloat16, jnp.float32, (2, 2, 2), (nz, 2, 2, 2)
+    sds, vm = jax.ShapeDtypeStruct, pltpu.VMEM
+    count = 160
+    smem = pl.BlockSpec(memory_space=pltpu.SMEM)
+    shapes = (
+        (every + w_qkv.shape, low),
+        (every + w_out.shape, low),
+        ((16, width), f32),
+        ((rows, w_qkv.shape[1]), low),
+        ((rows, width), f32),
+        ((rows, 128), f32),
+        ((rows, width), f32),
+        ((rows, width), f32),
+        ((rows, width), low),
+        ((rows, width), low),
+        (plane + (rows, width), low),
+        ((width, units), low),
+        ((units, width), low),
+        ((rows, width), f32),
+        ((8, units), f32),
+    )
+    return pl.pallas_call(
+        functools.partial(fore_kernel, nz),
+        name="fore",
+        out_shape=tuple(sds(shape, kind) for shape, kind in shapes),
+        in_specs=[ANY] * 4 + [IN_VMEM] * 2 + [ANY] * 2 + [IN_VMEM, smem, smem],
+        out_specs=[ANY] * 13 + [IN_VMEM] * 2,
+        scratch_shapes=[
+            vm(every + w_qkv.shape, low),
+            vm(every + w_out.shape, low),
+            vm(every + (share, 128), f32),
+            vm((share, 128), f32),
+            vm((width, units), low),
+            vm((units, width), low),
+            vm(plane + (rows, width), low),
+            vm((rows, width), low),
+            vm((rows, width), f32),
+            vm((rows, width), low),
+            vm((rows, w_qkv.shape[1]), low),
+            vm((rows, width), f32),
+            vm((rows, 128), f32),
+            vm((rows, width), low),
+            vm((rows, width), f32),
+            vm((rows, rows), f32),
+            vm((16, width), f32),
+            vm(plane + (rows, width), low),
+            vm(plane + (rows, units), f32),
+            vm(plane + (rows, units), f32),
+            vm(plane + (rows, units), f32),
+            vm(plane + (rows, units), low),
+            vm(plane + (rows, units), low),
+            vm((2, 2, rows, width), low),
+            vm((rows, units), f32),
+            vm(plane + (8, rows), f32),
+            vm(plane + (8, rows), f32),
+            vm((4,) + plane + (8, rows), f32),
+            vm(plane + (8, rows), f32),
+            vm((2, 2, rows, width), low),
+            vm((2, 2, rows, width), low),
+            vm((2, rows, width), low),
+            vm((rows, width), low),
+            vm(plane + (rows, width), low),
+            vm((width, units), low),
+            vm((units, width), low),
+            pltpu.SemaphoreType.DMA((24,)),
+            pltpu.SemaphoreType.DMA((count,)),
+            pltpu.SemaphoreType.DMA((count,)),
+        ],
+        compiler_params=pltpu.CompilerParams(
+            collective_id=1, has_side_effects=True, vmem_limit_bytes=63 * 2**20
+        ),
+    )(tokens, og, w_qkv, w_out, gains, biases, fc1, fc2, unit_rows, doc_lengths, scale)
 
 
 def back_kernel(
@@ -1304,56 +1418,41 @@
     mid_gain,
     ffn_biases,
 ):
-    model_width = tokens.shape[1]
-    local_rows = tokens.shape[0]
-    head_dim = model_width // HEADS
-    factor = 1.0 / math.sqrt(head_dim)
-    share = gains.shape[0]
-    vectors = jnp.concatenate(
-        [gains, biases, jnp.zeros((share, 128 - gains.shape[1] - biases.shape[1]), jnp.float32)],
-        axis=1,
-    )
-    qkv_full, out_full, vec_full, fc1_rows, fc2_cols, shard_rows = gather(
-        nz, w_qkv, w_out, vectors, w_fc1, w_fc2, out_grad
-    )
-    qkv_full = qkv_full.reshape(model_width, -1)
-    out_full = out_full.reshape(model_width, -1)
-    vec_full = vec_full.reshape(model_width, 128)
-    vec_rows = vec_full[:, :10].T
-    gain_full = vec_rows[:3]
-    bias_full = vec_rows[3:]
-    doc_ends = jnp.cumsum(doc_lengths[0])[:-1]
-    places = jnp.arange(local_rows)
-    doc_ids = jnp.sum((places[:, None] >= doc_ends[None, :]).astype(jnp.int32), axis=1)
-    inputs = tokens.astype(jnp.float32)
-    normed_one, inverse_one = normalize(inputs)
-    normed_in = (normed_one * gain_full[0] + bias_full[0]).astype(jnp.bfloat16)
-    zero_bias = jnp.zeros((model_width,), jnp.float32)
-    qkv_bias = jnp.concatenate([bias_full[1], zero_bias, bias_full[2]])
-    projected = (
-        jnp.dot(normed_in, qkv_full, preferred_element_type=jnp.float32) + qkv_bias
-    ).astype(jnp.bfloat16)
-    query_rows = projected[:, :model_width].reshape(local_rows, HEADS, head_dim)
-    key_rows = projected[:, model_width : 2 * model_width].reshape(local_rows, HEADS, head_dim)
-    value_rows = projected[:, 2 * model_width :].reshape(local_rows, HEADS, head_dim)
-    attended, sums_log = attend_forward(query_rows, key_rows, value_rows, doc_ids, factor)
-    attended = attended.reshape(local_rows, model_width)
-    scale_wide = jnp.repeat(head_scale, head_dim)
-    scaled = (attended * scale_wide).astype(jnp.bfloat16)
-    branch = jnp.dot(scaled, out_full, preferred_element_type=jnp.float32) + bias_full[3]
-    normed_post, inverse_post = normalize(branch)
-    middle = inputs + normed_post * gain_full[1] + bias_full[4]
-    normed_two, inverse_two = normalize(middle)
-    normed_mid = (normed_two * gain_full[2] + bias_full[5]).astype(jnp.bfloat16)
     units = w_fc1.shape[1]
     unit_rows = jnp.concatenate(
         [ffn_biases[:1], mid_gain[None], ffn_biases[1:], jnp.zeros((5, units), jnp.float32)]
     )
-    grad_normed_mid, ffn_part, fc1_part, fc2_part, unit_sums = ffn(
-        normed_mid, shard_rows, fc1_rows, fc2_cols, unit_rows
-    )
-    lse = jnp.pad(sums_log[0][:, :, 0].T, ((0, 0), (0, 128 - HEADS)))
-    vec = jnp.concatenate([vec_rows, scale_wide[None], jnp.zeros((5, model_width), jnp.float32)])
+    (
+        qkv_full,
+        out_full,
+        vec,
+        proj,
+        att,
+        lse,
+        branch,
+        middle,
+        nin,
+        scaled,
+        ffn_part,
+        fc1_part,
+        fc2_part,
+        gnm,
+        unit_sums,
+    ) = fore(
+        nz,
+        tokens,
+        out_grad,
+        doc_lengths,
+        w_qkv,
+        w_out,
+        gains,
+        biases,
+        head_scale,
+        w_fc1,
+        w_fc2,
+        unit_rows,
+    )
+    model_width = tokens.shape[1]
     (
         mixed_out,
         token_grad,
@@ -1366,20 +1465,20 @@
         unit_sums,
     ) = back(
         nz,
-        grad_normed_mid,
+        gnm,
         ffn_part,
         fc1_part,
         fc2_part,
         unit_sums,
-        projected,
-        attended,
+        proj,
+        att,
         lse,
         branch,
         middle,
         scaled,
-        normed_in,
-        qkv_full,
-        out_full,
+        nin,
+        qkv_full.reshape(model_width, -1),
+        out_full.reshape(model_width, -1),
         vec,
         out_grad,
         tokens,
@@ -1392,7 +1491,7 @@
         weight_grad[:, w_qkv.shape[1] :],
         gains_grad,
         biases_grad,
-        jnp.sum(scale_sums[2].reshape(HEADS, head_dim), axis=1),
+        jnp.sum(scale_sums[2].reshape(HEADS, -1), axis=1),
         fc1_grad,
         fc2_grad,
         unit_sums[0],
@@ -1401,7 +1500,7 @@
 
 
 def layer(nz, nt, tokens, out_grad, doc_lengths, w_qkv, *rest):
-    if nt == 8 and nz > 1 and w_qkv.shape[0] % 16 == 0:
+    if nz == 4 and nt == 8 and w_qkv.shape[0] % 16 == 0:
         return fused(nz, tokens, out_grad, doc_lengths, w_qkv, *rest)
     return plain(tokens, out_grad, doc_lengths, w_qkv, *rest)
 

time: 301 us -> 246 us (0.82)
  Pallas kernels: 257 us -> 224 us
  matrix products: 8.69 us -> 0 us
  other arithmetic: 8.91 us -> 1.98 us
  local copies, waits for them, and re-layouts: 24.6 us -> 19 us
    pallas_call x2 -> x1, Pallas kernels: 152 us -> 126 us  [fore(): pl.pallas_call(functools.partial(fore_kernel, nz), name='fore', out_shape...]
    dot_general x4 -> x0, matrix products: 8.69 us -> none  [the longest x1 4.77 us: fused(): jnp.dot(normed_in, qkv_full, preferred_element_type=jnp.float32) + qkv_bias]
    pallas_call x1, Pallas kernels: 105 us -> 98.1 us  [back(): pl.pallas_call(functools.partial(back_kernel, nz), name='back', out_shape...]
    reduce_sum x5 -> x1, other arithmetic: 4.17 us -> 0.63 us  [fused(): jnp.sum(scale_sums[2].reshape(HEADS, -1), axis=1)]
    unnamed x35 -> x12, local copies, waits for them, and re-layouts: 13.8 us -> 11.3 us
where the time goes in v4:
time: 246 us
  Pallas kernels  224 us (91%)
  local copies, waits for them, and re-layouts  19 us (8%)
    pallas_call x1, Pallas kernels, fore(): pl.pallas_call(functools.partial(fore_kernel, nz), name='fore', out_shape...  126 us
    pallas_call x1, Pallas kernels, back(): pl.pallas_call(functools.partial(back_kernel, nz), name='back', out_shape...  98.1 us
    unnamed x12, local copies, waits for them, and re-layouts  11.3 us

profile of v4, /device:TPU:0, one launch (start us, length us, event | category | flops | bytes accessed | tf_op | source)
XLA Modules:
  0.0 245.7 jit_solution(7407276261402146171)
XLA Ops:
  0.7 0.1 pad.3.clone
  0.7 0.8 fusion
  1.5 1.4 maximum_maximum_fusion.unit_ref
  2.9 1.4 copy.23.gains_ref
  4.2 1.4 copy.24.biases_ref
  5.6 125.9 %fore.1 = (bf16[4,2,2,2,32,3072]{5,4,3,2,1,0:T(8,128)(2,1)}, bf16[4,2,2,2,32,1024]{5,4,3,2,1,0:T(8,128)(2,1)}, f32[16,1024]{1,0:T(8,128)}, bf16[256,3072]{1,0:T(...) custom-call(bf16[256,1024]{1,0:T(8,128)(2,1)} %tok_ref.3, ...), custom_call_target="tpu_custom_call" | custom-call | tf_op jit(solution)/shard_map/fore/pallas_call | solution.py:883
  131.5 98.1 %back.1 = (bf16[256,1024]{1,0:T(8,128)(2,1)}, f32[256,1024]{1,0:T(8,128)}, f32[32,4096]{1,0:T(8,128)}, f32[32,3]{1,0:T(8,128)}, f32[32,7]{1,0:T(8,128)}, /*index...) custom-call(f32[256,1024]{1,0:T(8,128)} %get-tuple-element.35.gnm_ref, ...), custom_call_target="tpu_custom_call" | custom-call | tf_op jit(solution)/shard_map/back/pallas_call | solution.py:1355
  229.6 0.0 copy-start.1
  229.6 0.0 copy-start
  229.6 1.5 copy.25
  231.1 1.3 slice.26
  232.4 1.3 slice.27
  233.7 1.4 copy.26
  235.1 0.8 slice_reduce_fusion
  235.9 0.1 reshape_squeeze.3
  235.9 0.6 reduce_sum.9
  236.6 1.6 slice.24
  238.1 1.8 slice.23
  239.9 1.9 copy.31
  241.8 2.3 copy.32
  244.1 0.0 copy-done.1
  244.1 0.8 copy.33
  244.9 0.0 copy-done
  244.9 0.8 copy.34
  (1 shorter events, 0.0 us)
Async XLA Ops:
  229.6 14.5 %copy-start.1 = (f32[256,512]{1,0:T(8,128)S(1)}, f32[256,512]{1,0:T(8,128)}, u32[]{:S(2)}) copy-start(f32[256,512]{1,0:T(8,128)} %get-tuple-element.90) | copy-start | bytes 1572868
  229.6 15.2 %copy-start = (f32[512,256]{1,0:T(8,128)S(1)}, f32[512,256]{1,0:T(8,128)}, u32[]{:S(2)}) copy-start(f32[512,256]{1,0:T(8,128)} %get-tuple-element.91) | copy-start | bytes 1572868

commit v5 on v4

--- a/solution.py
+++ b/solution.py
@@ -422,7 +422,8 @@
     biases_ref,
     fc1_ref,
     fc2_ref,
-    unit_ref,
+    gain_ref,
+    shift_ref,
     doc_ref,
     scale_ref,
     qkv_out,
@@ -436,14 +437,17 @@
     nin_out,
     scaled_out,
     ffn_out,
+    fc2_out,
+    late_out,
     fc1_out,
-    fc2_out,
     gnm_out,
     unit_out,
     qkv_all,
     out_all,
     vec_all,
     vec_mine,
+    vec_turn,
+    unit_ref,
     fc1_all,
     fc2_all,
     og_all,
@@ -475,7 +479,9 @@
     from_two,
     ffn_part,
     fc1_part,
+    late_part,
     fc2_part,
+    fc1_got,
     local_sems,
     send_sems,
     recv_sems,
@@ -486,14 +492,6 @@
     others = [lax.rem(z + k, nz) for k in range(1, nz)]
     slots = [z] + [lax.rem(z + nz - k, nz) for k in range(1, nz)]
     peers = [at(other, y, x, c) for other in others]
-    greet([to_x, to_y, to_c, to_xy] + peers)
-    sends = Sends(send_sems, recv_sems)
-    low, f32 = jnp.bfloat16, jnp.float32
-    rows, width = tok.shape
-    units = fc1_all.shape[1]
-    width1, width2 = fc1_ref.shape[0], fc2_ref.shape[1]
-    own1 = fc1_all.at[pl.ds(pl.multiple_of(z * width1, width1), width1)]
-    own2 = fc2_all.at[:, pl.ds(pl.multiple_of(z * width2, width2), width2)]
     locals_ = []
 
     def fetch(src, dst):
@@ -502,47 +500,93 @@
         locals_.append(copy)
         return copy
 
+    rows, width = tok.shape
+    fourth = width // 4
+    qkv_in = [
+        fetch(
+            qkv_ref.at[:, pl.ds(i * width + g * fourth, fourth)],
+            qkv_all.at[z, y, x, c, :, pl.ds((3 * g + i) * fourth, fourth)],
+        )
+        for g in range(4)
+        for i in range(3)
+    ]
+    vec_turn[...] = jnp.zeros_like(vec_turn)
+    share = vec_mine.shape[0]
+    vec_turn[0:3, 0:share] = gains_ref[...]
+    vec_turn[3:10, 0:share] = biases_ref[...]
+    vec_mine[...] = vec_turn[...].T[:share]
+    greet([to_x, to_y, to_c, to_xy] + peers)
+    sends = Sends(send_sems, recv_sems)
+    low, f32 = jnp.bfloat16, jnp.float32
+    units = fc1_all.shape[1]
+    width1, width2 = fc1_ref.shape[0], fc2_ref.shape[1]
+    own1 = fc1_all.at[pl.ds(pl.multiple_of(z * width1, width1), width1)]
+    own2 = fc2_all.at[:, pl.ds(pl.multiple_of(z * width2, width2), width2)]
     def wait_all(copies):
         for copy in copies:
             copy.wait_recv()
 
-    vec_mine[...] = jnp.zeros_like(vec_mine)
-    vec_mine[:, 0:3] = gains_ref[...]
-    vec_mine[:, 3:10] = biases_ref[...]
     vec_z = [sends.start(vec_mine, vec_all.at[z, y, x, c], peer) for peer in peers]
-    qkv_z = [sends.start(qkv_ref, qkv_all.at[z, y, x, c], peer) for peer in peers]
-
-    def halves(ref):
-        half = ref.shape[-1] // 2
-        return pl.ds(0, half), pl.ds(half, half)
-
-    def first(src, whole, slot):
-        lo, hi = halves(whole)
-        one = src if src is not None else whole.at[slot, y, x, c]
-        return (
-            sends.start(one.at[:, lo], whole.at[slot, y, x, c, :, lo], to_x),
-            sends.start(one.at[:, hi], whole.at[slot, y, x, c, :, hi], to_y),
-        )
-
-    def second(whole, slot):
-        lo, hi = halves(whole)
+    phase = 6 * fourth
+    spans = (pl.ds(0, phase), pl.ds(phase, phase))
+    for copy in qkv_in:
+        copy.wait()
+    own_qkv = qkv_all.at[z, y, x, c]
+    qkv_z = [
+        [sends.start(own_qkv.at[:, span], own_qkv.at[:, span], peer) for peer in peers]
+        for span in spans
+    ]
+
+    def sides(whole, p):
+        size = phase // 2 if whole is qkv_all else whole.shape[-1] // 2
+        return pl.ds(2 * p * size, size), pl.ds((2 * p + 1) * size, size)
+
+    def first(whole, slot, p=0):
+        lo, hi = sides(whole, p)
+        by_x, by_y = whole.at[slot, y, x, c, :, lo], whole.at[slot, y, x, c, :, hi]
+        return (sends.start(by_x, by_x, to_x), sends.start(by_y, by_y, to_y))
+
+    def second(whole, slot, p=0):
+        lo, hi = sides(whole, p)
         by_x, by_y = whole.at[slot, y, :, c, :, lo], whole.at[slot, :, x, c, :, hi]
         return (sends.start(by_x, by_x, to_y), sends.start(by_y, by_y, to_x))
 
-    def third(whole, slot):
-        ref = whole.at[slot, :, :, c]
+    def third(whole, slot, p=None):
+        ref = whole.at[slot, :, :, c] if p is None else whole.at[slot, :, :, c, :, spans[p]]
         return sends.start(ref, ref, to_c)
 
-    qkv_a = [first(qkv_ref, qkv_all, z)]
+    a0, a1 = [first(qkv_all, z, 0)], [first(qkv_all, z, 1)]
     tok_in = fetch(tok_ref, tok)
-    qkv_in = fetch(qkv_ref, qkv_all.at[z, y, x, c])
     out_in = fetch(out_ref, out_all.at[z, y, x, c])
     fc1_in = fetch(fc1_ref, own1)
     fc2_in = fetch(fc2_ref, own2)
     og_in = fetch(og_ref, og_all.at[y, x, c])
     vec_all[z, y, x, c] = vec_mine[...]
+    unit_ref[...] = jnp.zeros_like(unit_ref)
+    unit_ref[0:1] = shift_ref[0:1]
+    unit_ref[1:2] = gain_ref[...]
+    unit_ref[2:3] = shift_ref[1:2]
+    step = 32
+    wait_all(vec_z)
+    by_x = vec_all.at[:, y, x, c]
+    vec_x = sends.start(by_x, by_x, to_x)
+    qkv_z[0][0].wait_recv()
+    a0.append(first(qkv_all, slots[1], 0))
+    vec_x.wait_recv()
+    by_y = vec_all.at[:, y, :, c]
+    vec_y = sends.start(by_y, by_y, to_y)
+    for k in range(2, nz):
+        qkv_z[0][k - 1].wait_recv()
+        a0.append(first(qkv_all, slots[k], 0))
+    b0 = []
+    for k in range(nz):
+        wait_all(a0[k])
+        b0.append(second(qkv_all, slots[k], 0))
+        if k == 0:
+            vec_y.wait_recv()
+            by_c = vec_all.at[:, :, :, c]
+            vec_c = sends.start(by_c, by_c, to_c)
     mask[...] = doc_mask(doc_ref, rows)
-    step = 32
     tok_in.wait()
 
     def normed(k, carry):
@@ -551,32 +595,8 @@
         return carry
 
     lax.fori_loop(0, rows // step, normed, 0)
-    wait_all(vec_z)
-    by_x = vec_all.at[:, y, x, c]
-    vec_x = sends.start(by_x, by_x, to_x)
-    qkv_z[0].wait_recv()
-    qkv_a.append(first(None, qkv_all, slots[1]))
-    vec_x.wait_recv()
-    by_y = vec_all.at[:, y, :, c]
-    vec_y = sends.start(by_y, by_y, to_y)
-    qkv_in.wait()
-    wait_all(qkv_a[0])
-    qkv_b = [second(qkv_all, slots[0])]
-    vec_y.wait_recv()
-    by_c = vec_all.at[:, :, :, c]
-    vec_c = sends.start(by_c, by_c, to_c)
-    for k in range(2, nz):
-        qkv_z[k - 1].wait_recv()
-        qkv_a.append(first(None, qkv_all, slots[k]))
-    out_z = [sends.start(out_ref, out_all.at[z, y, x, c], peer) for peer in peers]
-    pair_peer = at(z + 1 - 2 * lax.rem(z, 2), y, x, c)
-    far_peer = peers[1]
-    fc2_far = sends.start(fc2_ref, own2, far_peer)
-    fc2_near = sends.start(fc2_ref, own2, pair_peer)
-    fc1_z = [sends.start(fc1_ref, own1, peer) for peer in peers]
     vec_c.wait_recv()
-    rows16 = vec_all[...].reshape(width, 128).T[:16]
-    vec[...] = rows16
+    vec[...] = vec_all[...].reshape(width, 128).T[:16]
     spot = lax.broadcasted_iota(jnp.int32, (1, width), 1)
     head = 64
     wide = jnp.zeros((1, width), f32)
@@ -591,37 +611,39 @@
         return carry
 
     lax.fori_loop(0, rows // step, scaled_in, 0)
+    c0 = []
     for k in range(1, nz):
-        wait_all(qkv_a[k])
-        qkv_b.append(second(qkv_all, slots[k]))
-    out_a = [first(out_ref, out_all, z)]
-    for k in range(1, nz):
-        out_z[k - 1].wait_recv()
-        out_a.append(first(None, out_all, slots[k]))
-    og = Plane(sends, og_all, (y, x, c), (to_x, to_y, to_c))
-    og.start(og_ref)
-    qkv_c = []
-    for k in range(nz):
-        wait_all(qkv_b[k])
-        qkv_c.append(third(qkv_all, slots[k]))
-    wait_all(qkv_c)
-    saves = [fetch(qkv_all, qkv_out), fetch(vec, vec_out), fetch(nin, nin_out)]
-
-    tile = width // 2
-    for k in range(6):
-        cols = pl.ds(k * tile, tile)
-        block = dot(nin[...], qkv_all[:, :, :, :, :, cols].reshape(width, tile))
-        if k < 2:
-            block = block + vec[4:5, cols]
-        if k >= 4:
-            block = block + vec[5:6, pl.ds((k - 4) * tile, tile)]
-        proj[:, cols] = block.astype(low)
-    saves.append(fetch(proj, proj_out))
+        qkv_z[1][k - 1].wait_recv()
+        a1.append(first(qkv_all, slots[k], 1))
+        wait_all(b0[k - 1])
+        c0.append(third(qkv_all, slots[k - 1], 0))
     out_in.wait()
-    out_b = []
-    for k in range(nz):
-        wait_all(out_a[k])
-        out_b.append(second(out_all, slots[k]))
+    own_out = out_all.at[z, y, x, c]
+    out_z = [sends.start(own_out, own_out, peer) for peer in peers]
+    pair_peer = at(z + 1 - 2 * lax.rem(z, 2), y, x, c)
+    far_peer = peers[1]
+    fc2_far = sends.start(fc2_ref, own2, far_peer)
+    fc2_near = sends.start(fc2_ref, own2, pair_peer)
+    fc1_z = [sends.start(fc1_ref, own1, peer) for peer in peers]
+    wait_all(b0[nz - 1])
+    c0.append(third(qkv_all, slots[nz - 1], 0))
+    b1 = []
+    for k in range(2):
+        wait_all(a1[k])
+        b1.append(second(qkv_all, slots[k], 1))
+    wait_all(c0)
+
+    def project(p):
+        for g in (2 * p, 2 * p + 1):
+            cols = pl.ds(3 * g * fourth, 3 * fourth)
+            here = pl.ds(g * fourth, fourth)
+            bias = jnp.concatenate(
+                [vec[4:5, here], jnp.zeros((1, fourth), f32), vec[5:6, here]], axis=1
+            )
+            block = dot(nin[...], qkv_all[:, :, :, :, :, cols].reshape(width, 3 * fourth))
+            proj[:, cols] = (block + bias).astype(low)
+
+    project(0)
     lane = lax.broadcasted_iota(jnp.int32, (1, 128), 1)
     is_low = lane < head
     keep = (is_low.astype(low), (lane >= head).astype(low))
@@ -630,9 +652,11 @@
     lse[...] = jnp.zeros_like(lse)
 
     def attend(p, carry):
-        q_at = pl.ds(pl.multiple_of(p * 128, 128), 128)
-        k_at = pl.ds(pl.multiple_of(width + p * 128, 128), 128)
-        v_at = pl.ds(pl.multiple_of(2 * width + p * 128, 128), 128)
+        base = lax.div(p, 2) * (3 * fourth) + lax.rem(p, 2) * 128
+        q_at = pl.ds(pl.multiple_of(base, 128), 128)
+        k_at = pl.ds(pl.multiple_of(base + fourth, 128), 128)
+        v_at = pl.ds(pl.multiple_of(base + 2 * fourth, 128), 128)
+        here = pl.ds(pl.multiple_of(p * 128, 128), 128)
         q2, k2, v2 = proj[:, q_at], proj[:, k_at], proj[:, v_at]
         found = []
         for i in range(2):
@@ -645,17 +669,44 @@
             found.append(dot(prob, v2))
             lse[...] = jnp.where(lane_wide == 2 * p + i, peak + jnp.log(total), lse[...])
         both = jnp.where(is_low, *found)
-        att[:, q_at] = both
-        scaled[:, q_at] = (both * vec[10:11, q_at]).astype(low)
+        att[:, here] = both
+        scaled[:, here] = (both * vec[10:11, here]).astype(low)
         return carry
 
-    lax.fori_loop(0, 4, attend, 0)
+    lax.fori_loop(0, 1, attend, 0)
+    for k in range(2, nz):
+        wait_all(a1[k])
+        b1.append(second(qkv_all, slots[k], 1))
+    out_a = [first(out_all, z)]
+    for k in range(1, nz):
+        out_z[k - 1].wait_recv()
+        out_a.append(first(out_all, slots[k]))
+    og = Plane(sends, og_all, (y, x, c), (to_x, to_y, to_c))
+    og.start(og_ref)
+    lax.fori_loop(1, 2, attend, 0)
+    c1 = []
+    for k in range(2):
+        wait_all(b1[k])
+        c1.append(third(qkv_all, slots[k], 1))
+    lax.fori_loop(2, 4, attend, 0)
+    for k in range(2, nz):
+        wait_all(b1[k])
+        c1.append(third(qkv_all, slots[k], 1))
+    wait_all(c1)
+    saves = [fetch(qkv_all, qkv_out), fetch(vec, vec_out), fetch(nin, nin_out)]
+    project(1)
+    saves.append(fetch(proj, proj_out))
+    out_b = []
+    for k in range(nz):
+        wait_all(out_a[k])
+        out_b.append(second(out_all, slots[k]))
+    lax.fori_loop(4, 6, attend, 0)
     og.after_first()
+    lax.fori_loop(6, 8, attend, 0)
     out_c = []
     for k in range(nz):
         wait_all(out_b[k])
         out_c.append(third(out_all, slots[k]))
-    lax.fori_loop(4, 8, attend, 0)
     saves += [fetch(att, att_out), fetch(lse, lse_out), fetch(scaled, scaled_out)]
     wait_all(out_c)
     saves.append(fetch(out_all, out_out))
@@ -808,40 +859,53 @@
     def ffn_of(yy, xx, cc):
         ffn_part[yy, xx, cc] = dot(hidden[yy, xx, cc], fc2_all[...]).astype(low)
 
-    for yy, xx in order[:2]:
-        ffn_of(yy, xx, 1 - c)
-        ffn_of(yy, xx, c)
+    blocks = nz
+    size = width // blocks
+
+    early = fc1_part.shape[-1]
+    soon, late = slice(0, early), slice(early, units)
+
+    def fc1_block(which, cols):
+        part = pl.ds(pl.multiple_of(which * size, 128), size)
+        block = jnp.zeros((size, cols.stop - cols.start), f32)
+        for j in range(8):
+            yxc = (j // 4, (j // 2) % 2, j % 2)
+            block = block + dot(mid_all[(*yxc, slice(None), part)], grad_pre[(*yxc, slice(None), cols)], TN)
+        return block
+
+    fc1_far = {}
+    for k in (1, 0, 2):
+        fc1_part[k] = fc1_block(others[k], soon).astype(low)
+        fc1_far[k] = sends.start(fc1_part.at[k], fc1_got.at[k], peers[k])
     wait_all((stage_x[0], stage_y[0]))
     sums[1 - y, x, :, left] = add_low(sums[1 - y, x, :, left], from_one[1 - y, :, left])
     sums[y, 1 - x, :, right] = add_low(sums[y, 1 - x, :, right], from_one[1 - x, :, right])
     last_y = sends.start(sums.at[1 - y, x, :, left], from_two.at[:, left], to_y)
     last_x = sends.start(sums.at[y, 1 - x, :, right], from_two.at[:, right], to_x)
-    for yy, xx in order[2:]:
+    fc1_out[:, soon] = fc1_block(z, soon)
+    fc1_out[:, late] = fc1_block(z, late)
+
+    def late_block(k, carry):
+        part = pl.ds(pl.multiple_of(k * size, 128), size)
+        late_part[part] = fc1_block(k, late).astype(low)
+        return carry
+
+    lax.fori_loop(0, blocks, late_block, 0)
+    saves.append(fetch(late_part, late_out))
+    for yy, xx in order:
         ffn_of(yy, xx, 1 - c)
         ffn_of(yy, xx, c)
     saves.append(fetch(ffn_part, ffn_out))
-    blocks = 4
-
-    def fc1_block(k, carry):
-        part = pl.ds(pl.multiple_of(k * (width // blocks), 128), width // blocks)
-        block = jnp.zeros((width // blocks, units), f32)
-        for j in range(8):
-            yxc = (j // 4, (j // 2) % 2, j % 2)
-            block = block + dot(mid_all[(*yxc, slice(None), part)], grad_pre[yxc], TN)
-        fc1_part[part] = block.astype(low)
-        return carry
 
     def fc2_block(k, carry):
-        part = pl.ds(pl.multiple_of(k * (width // blocks), 128), width // blocks)
-        block = jnp.zeros((units, width // blocks), f32)
+        part = pl.ds(pl.multiple_of(k * size, 128), size)
+        block = jnp.zeros((units, size), f32)
         for j in range(8):
             yxc = (j // 4, (j // 2) % 2, j % 2)
             block = block + dot(hidden[yxc], og_all[(*yxc, slice(None), part)], TN)
         fc2_part[:, part] = block.astype(low)
         return carry
 
-    lax.fori_loop(0, blocks, fc1_block, 0)
-    saves.append(fetch(fc1_part, fc1_out))
     lax.fori_loop(0, blocks, fc2_block, 0)
     saves.append(fetch(fc2_part, fc2_out))
     wait_all((stage_x[1], stage_y[1], last_x, last_y))
@@ -851,12 +915,15 @@
             + from_one[k, :, cols].astype(f32)
             + from_two[:, cols].astype(f32)
         )
+    for k in range(nz - 1):
+        fc1_far[k].wait_recv()
+        fc1_out[:, soon] += fc1_got[k].astype(f32)
     for copy in saves:
         copy.wait()
     sends.finish()
 
 
-def fore(nz, tokens, og, doc_lengths, w_qkv, w_out, gains, biases, scale, fc1, fc2, unit_rows):
+def fore(nz, tokens, og, doc_lengths, w_qkv, w_out, gains, biases, scale, fc1, fc2, gain, shift):
     rows, width = tokens.shape
     share, units = w_qkv.shape[0], fc1.shape[1]
     low, f32, plane, every = jnp.bfloat16, jnp.float32, (2, 2, 2), (nz, 2, 2, 2)
@@ -875,8 +942,9 @@
         ((rows, width), low),
         ((rows, width), low),
         (plane + (rows, width), low),
-        ((width, units), low),
         ((units, width), low),
+        ((width, units // 2), low),
+        (fc1.shape, f32),
         ((rows, width), f32),
         ((8, units), f32),
     )
@@ -884,13 +952,15 @@
         functools.partial(fore_kernel, nz),
         name="fore",
         out_shape=tuple(sds(shape, kind) for shape, kind in shapes),
-        in_specs=[ANY] * 4 + [IN_VMEM] * 2 + [ANY] * 2 + [IN_VMEM, smem, smem],
-        out_specs=[ANY] * 13 + [IN_VMEM] * 2,
+        in_specs=[ANY] * 4 + [IN_VMEM] * 2 + [ANY] * 2 + [IN_VMEM] * 2 + [smem] * 2,
+        out_specs=[ANY] * 13 + [IN_VMEM] * 3,
         scratch_shapes=[
             vm(every + w_qkv.shape, low),
             vm(every + w_out.shape, low),
             vm(every + (share, 128), f32),
             vm((share, 128), f32),
+            vm((128, 128), f32),
+            vm((8, units), f32),
             vm((width, units), low),
             vm((units, width), low),
             vm(plane + (rows, width), low),
@@ -921,37 +991,40 @@
             vm((2, rows, width), low),
             vm((rows, width), low),
             vm(plane + (rows, width), low),
-            vm((width, units), low),
+            vm((nz - 1, fc1.shape[0], units // 2), low),
+            vm((width, units // 2), low),
             vm((units, width), low),
-            pltpu.SemaphoreType.DMA((24,)),
+            vm((nz - 1, fc1.shape[0], units // 2), low),
+            pltpu.SemaphoreType.DMA((36,)),
             pltpu.SemaphoreType.DMA((count,)),
             pltpu.SemaphoreType.DMA((count,)),
         ],
         compiler_params=pltpu.CompilerParams(
             collective_id=1, has_side_effects=True, vmem_limit_bytes=63 * 2**20
         ),
-    )(tokens, og, w_qkv, w_out, gains, biases, fc1, fc2, unit_rows, doc_lengths, scale)
+    )(tokens, og, w_qkv, w_out, gains.T, biases.T, fc1, fc2, gain, shift, doc_lengths, scale)
 
 
 def back_kernel(
     nz,
-    gnm_ref,
+    gnm_in,
     ffn_ref,
-    fc1_ref,
+    late_ref,
+    own1_in,
     fc2_ref,
     unit_ref,
-    proj_ref,
-    att_ref,
-    lse_ref,
-    branch_ref,
-    middle_ref,
-    scaled_ref,
-    nin_ref,
-    qkv_ref,
-    out_ref,
+    proj_in,
+    att_in,
+    lse_in,
+    branch_in,
+    middle_in,
+    scaled_in,
+    nin_in,
+    qkv_in,
+    out_in,
     vec_ref,
-    og_ref,
-    tok_ref,
+    og_in,
+    tok_in,
     doc_ref,
     mixed_out,
     token_out,
@@ -984,8 +1057,23 @@
     mask,
     accs,
     small,
+    small_far,
+    small_y,
+    small_half,
     small_got,
     turned,
+    gnm_ref,
+    proj_ref,
+    att_ref,
+    lse_ref,
+    branch_ref,
+    middle_ref,
+    scaled_ref,
+    nin_ref,
+    qkv_ref,
+    out_ref,
+    og_ref,
+    tok_ref,
     local_sems,
     send_sems,
     recv_sems,
@@ -1009,20 +1097,36 @@
     f_c = [
         sends.start(ffn_ref.at[:, :, 1 - c, part], f_core.at[:, :, part], to_c) for part in parts
     ]
-    locals_ = [
-        pltpu.make_async_copy(ffn_ref.at[:, :, c], f_sums, local_sems.at[0]),
-    ]
+    locals_ = []
+
+    def fetch(src, dst):
+        copy = pltpu.make_async_copy(src, dst, local_sems.at[len(locals_)])
+        copy.start()
+        locals_.append(copy)
+        return copy
+
+    middle_got = fetch(middle_in, middle_ref)
+    gnm_got = fetch(gnm_in, gnm_ref)
+    og_got = fetch(og_in, og_ref)
+    branch_got = fetch(branch_in, branch_ref)
+    ffn_got = fetch(ffn_ref.at[:, :, c], f_sums)
+    out_got = fetch(out_in, out_ref)
+    att_got = fetch(att_in, att_ref)
+    scaled_got = fetch(scaled_in, scaled_ref)
+    nin_got = fetch(nin_in, nin_ref)
+    proj_got = fetch(proj_in, proj_ref)
+    lse_got = fetch(lse_in, lse_ref)
+    qkv_got = fetch(qkv_in, qkv_ref)
+    tok_got = fetch(tok_in, tok_ref)
 
     def block1(which):
-        return fc1_ref.at[pl.ds(pl.multiple_of(which * width1, width1), width1)]
+        return late_ref.at[pl.ds(pl.multiple_of(which * width1, width1), width1)]
 
     def block2(which):
         return fc2_ref.at[:, pl.ds(pl.multiple_of(which * width2, width2), width2)]
 
-    locals_.append(pltpu.make_async_copy(block1(z), got1.at[nz - 1], local_sems.at[1]))
-    locals_.append(pltpu.make_async_copy(block2(z), got2.at[nz - 1], local_sems.at[2]))
-    for copy in locals_:
-        copy.start()
+    own1_got = fetch(own1_in, fc1_out)
+    own2_got = fetch(block2(z), got2.at[nz - 1])
     far = []
     for k, peer in enumerate(peers):
         far.append(sends.start(unit_ref, got_unit.at[k], peer))
@@ -1035,7 +1139,7 @@
         part = parts[k]
         f_c[k].wait_recv()
         if k == 0:
-            locals_[0].wait()
+            ffn_got.wait()
         for yy in range(2):
             for xx in range(2):
                 f_sums[yy, xx, part] = add_low(f_sums[yy, xx, part], f_core[yy, xx, part])
@@ -1176,10 +1280,11 @@
         gmid[part] = grad_middle
         return carry
 
+    for copy in (middle_got, gnm_got, og_got, branch_got):
+        copy.wait()
     lax.fori_loop(0, rows // step, norms, 0)
     mask[...] = doc_mask(doc_ref, rows)
     ffn_one(0)
-    ffn_one(1)
     quarter = width // 4
 
     def scaled_block(k, carry):
@@ -1189,6 +1294,8 @@
         gatt[:, part] = (block * vec_ref[10:11, part]).astype(low)
         return carry
 
+    out_got.wait()
+    att_got.wait()
     lax.fori_loop(0, 4, scaled_block, 0)
 
     def out_block(k, carry):
@@ -1197,9 +1304,13 @@
         w_part[k, :, :, :, :, pl.ds(0, width)] = block.reshape(2, 2, 2, share, width)
         return carry
 
+    scaled_got.wait()
     lax.fori_loop(0, nz, out_block, 0)
     w_zero(0)
+    nin_got.wait()
     nin_t[...] = nin_ref[...].T
+    proj_got.wait()
+    lse_got.wait()
     head = 64
     lane = lax.broadcasted_iota(jnp.int32, (1, 128), 1)
     is_low = lane < head
@@ -1208,10 +1319,12 @@
     keep = (is_low.astype(low), (lane >= head).astype(low))
 
     def pair(p, carry):
-        q_at = pl.ds(pl.multiple_of(p * 128, 128), 128)
-        k_at = pl.ds(pl.multiple_of(width + p * 128, 128), 128)
-        v_at = pl.ds(pl.multiple_of(2 * width + p * 128, 128), 128)
-        q2, k2, v2, do2 = proj_ref[:, q_at], proj_ref[:, k_at], proj_ref[:, v_at], gatt[:, q_at]
+        base = lax.div(p, 2) * (3 * quarter) + lax.rem(p, 2) * 128
+        q_at = pl.ds(pl.multiple_of(base, 128), 128)
+        k_at = pl.ds(pl.multiple_of(base + quarter, 128), 128)
+        v_at = pl.ds(pl.multiple_of(base + 2 * quarter, 128), 128)
+        here = pl.ds(pl.multiple_of(p * 128, 128), 128)
+        q2, k2, v2, do2 = proj_ref[:, q_at], proj_ref[:, k_at], proj_ref[:, v_at], gatt[:, here]
         lses = lse_ref[...]
         found = []
         for i in range(2):
@@ -1227,48 +1340,50 @@
             )
         for where, a, b in zip((q_at, k_at, v_at), *found):
             dproj[:, where] = jnp.where(is_low, a, b).astype(low)
-        accs[4, :, q_at] = eights(dproj[:, q_at].astype(f32))
-        accs[5, :, q_at] = eights(dproj[:, v_at].astype(f32))
+        accs[4, :, here] = eights(dproj[:, q_at].astype(f32))
+        accs[5, :, here] = eights(dproj[:, v_at].astype(f32))
         return carry
 
     def wgrad(j):
         start, size = spans[j]
-        third = size // 3
+        cols = pl.ds((j - 1) * size, size)
 
         def one(k, carry):
             part = pl.ds(pl.multiple_of(k * (width // nz), width // nz), width // nz)
-            for i in range(3):
-                first = i * width + (j - 1) * third
-                block = dot(nin_t[part], dproj[:, first : first + third]).astype(low)
-                w_part[k, :, :, :, :, pl.ds(start + i * third, third)] = block.reshape(
-                    2, 2, 2, share, third
-                )
+            block = dot(nin_t[part], dproj[:, cols]).astype(low)
+            w_part[k, :, :, :, :, pl.ds(start, size)] = block.reshape(2, 2, 2, share, size)
             return carry
 
         lax.fori_loop(0, nz, one, 0)
         w_zero(j)
 
-    lax.fori_loop(0, 2, pair, 0)
+    lax.fori_loop(0, 1, pair, 0)
+    w_step1(0)
+    lax.fori_loop(1, 2, pair, 0)
     wgrad(1)
-    w_step1(0)
     ffn_two(0)
-    lax.fori_loop(2, 4, pair, 0)
+    lax.fori_loop(2, 3, pair, 0)
+    w_step1(1)
+    lax.fori_loop(3, 4, pair, 0)
     wgrad(2)
-    w_step1(1)
-    ffn_two(1)
-    lax.fori_loop(4, 6, pair, 0)
+    w_step2(0)
+    lax.fori_loop(4, 5, pair, 0)
+    w_step1(2)
+    lax.fori_loop(5, 6, pair, 0)
     wgrad(3)
-    w_step1(2)
-    lax.fori_loop(6, 8, pair, 0)
+    w_step2(1)
+    w_step3(0)
+    lax.fori_loop(6, 7, pair, 0)
+    w_step1(3)
+    lax.fori_loop(7, 8, pair, 0)
     wgrad(4)
-    w_step1(3)
-    w_step1(4)
 
     def gni_block(k, carry):
         part = pl.ds(pl.multiple_of(k * quarter, quarter), quarter)
         gni[:, part] = dot(dproj[...], qkv_ref[part], NT)
         return carry
 
+    qkv_got.wait()
     lax.fori_loop(0, 4, gni_block, 0)
 
     def tokens_back(k, carry):
@@ -1280,78 +1395,92 @@
         accs[3] += eights(grad)
         return carry
 
+    tok_got.wait()
     lax.fori_loop(0, rows // step, tokens_back, 0)
     for j in range(16):
-        small[0, j : j + 1] = jnp.sum(accs[j], axis=0, keepdims=True)
-    small_c = sends.start(small.at[0], small_got.at[0], to_c)
-    w_step2(0)
-    small_c.wait_recv()
-    small[1] = small[0] + small_got[0]
-    small_p = [
-        sends.start(small.at[1], small_got.at[1 + k], to)
-        for k, to in enumerate((to_x, to_y, to_xy))
+        small[j : j + 1] = jnp.sum(accs[j], axis=0, keepdims=True)
+    spot = lax.broadcasted_iota(jnp.int32, (1, width), 1)
+    tile = jnp.zeros((1, 128), f32)
+    for h in range(HEADS):
+        inside = jnp.logical_and(spot >= h * head, spot < (h + 1) * head)
+        found = jnp.sum(jnp.where(inside, small[10:11], 0.0), axis=1, keepdims=True)
+        tile = jnp.where(lane == h, found, tile)
+    small[11:12] = jnp.concatenate([tile] * (width // 128), axis=1)
+    part_z = width // nz
+
+    def lanes(which):
+        return pl.ds(pl.multiple_of(which * part_z, 128), part_z)
+
+    small_z = [
+        sends.start(small.at[:, lanes(others[k])], small_far.at[k], peer)
+        for k, peer in enumerate(peers)
     ]
-    ffn_three(0)
-    ffn_three(1)
-    w_step2(1)
-    for copy in small_p:
-        copy.wait_recv()
-    small[2] = (small[1] + small_got[1]) + (small_got[2] + small_got[3])
-    small_z = [
-        sends.start(small.at[2], small_got.at[4 + k], peer) for k, peer in enumerate(peers)
-    ]
-    w_step3(0)
     w_step2(2)
     w_step3(1)
+    w_step1(4)
+    total = small[:, lanes(z)]
+    for k in range(nz - 1):
+        small_z[k].wait_recv()
+        total = total + small_far[k]
+    small_y[...] = total
+    mine = small_y.at[:, pl.ds(pl.multiple_of(y * 128, 128), 128)]
+    other = small_y.at[:, pl.ds(pl.multiple_of((1 - y) * 128, 128), 128)]
+    by_y = sends.start(other, small_got.at[0], to_y)
     w_step2(3)
+    by_y.wait_recv()
+    small_half[0] = mine[...] + small_got[0]
+    by_x = sends.start(small_half.at[0], small_got.at[1], to_x)
     w_step3(2)
+    ffn_three(0)
+    ffn_one(1)
+    by_x.wait_recv()
+    small_half[1] = small_half[0] + small_got[1]
+    by_c = sends.start(small_half.at[1], small_got.at[2], to_c)
     w_step2(4)
     w_step3(3)
+    by_c.wait_recv()
+    total = small_half[1] + small_got[2]
+    scale_out[...] = jnp.broadcast_to(total[11:12], (8, 128))
+    ours = pl.ds(pl.multiple_of(x * 64 + c * 32, 32), 32)
+    turned[...] = jnp.concatenate([total, jnp.zeros((112, 128), f32)], axis=0).T
+    ours = jnp.concatenate([turned[ours], jnp.zeros((96, 128), f32)], axis=0).T
+    gains_out[...] = ours[0:3, :share]
+    biases_out[...] = ours[3:10, :share]
+    ffn_two(1)
     w_step4(0)
-    total = small[2]
-    for k in range(nz - 1):
-        small_z[k].wait_recv()
-        total = total + small_got[4 + k]
-    scale_out[...] = total[8:16]
-    index = (lax.axis_index("dp") * 8 + lax.axis_index("tensor")) * share
-    mine = pl.ds(pl.multiple_of(index, share), share)
-    pad = jnp.zeros((112, width), f32)
-    turned[...] = jnp.concatenate([total, pad], axis=0).T
-    gains_out[...] = turned[mine, 0:3]
-    turned[...] = jnp.concatenate([total[3:10], pad, total[:9]], axis=0).T
-    biases_out[...] = turned[mine, 0:7]
     w_step4(1)
+    w_step3(4)
     w_step4(2)
-    w_step3(4)
     for copy in far:
         copy.wait_recv()
-    for copy in locals_[1:]:
-        copy.wait()
-    own1, own2, unit = got1[nz - 1].astype(f32), got2[nz - 1].astype(f32), unit_ref[...]
+    own1_got.wait()
+    own2_got.wait()
+    late = pl.ds(fc1_out.shape[1] - got1.shape[2], got1.shape[2])
+    own2, unit = got2[nz - 1].astype(f32), unit_ref[...]
     for k in range(nz - 1):
-        own1 = own1 + got1[k].astype(f32)
+        fc1_out[:, late] += got1[k].astype(f32)
         own2 = own2 + got2[k].astype(f32)
         unit = unit + got_unit[k]
-    fc1_out[...] = own1
     fc2_out[...] = own2
     unit_out[...] = unit
     w_step4(3)
+    ffn_three(1)
     w_step4(4)
     sends.finish()
 
 
 def back(nz, *operands):
-    (gnm, ffn_part, fc1, fc2, unit, proj, att, lse, branch, middle, scaled, nin, qkv, out, vec) = (
-        operands[:15]
-    )
+    gnm, ffn_part, late, fc1, fc2, unit, proj, att, lse, branch, middle = operands[:11]
+    scaled, nin, qkv, out, vec = operands[11:16]
     rows, width = middle.shape
     share = width // (nz * 8)
     columns = proj.shape[1] + width
     low, f32 = jnp.bfloat16, jnp.float32
     sds = jax.ShapeDtypeStruct
-    fc1_own, fc2_own = (fc1.shape[0] // nz, fc1.shape[1]), (fc2.shape[0], fc2.shape[1] // nz)
+    fc2_own = (fc2.shape[0], fc2.shape[1] // nz)
     count = 64 + 8 * nz
-    specs = [IN_VMEM] + [ANY] * 3 + [IN_VMEM] * 13 + [pl.BlockSpec(memory_space=pltpu.SMEM)]
+    specs = [ANY] * 5 + [IN_VMEM] + [ANY] * 9 + [IN_VMEM] + [ANY] * 2
+    specs.append(pl.BlockSpec(memory_space=pltpu.SMEM))
     return pl.pallas_call(
         functools.partial(back_kernel, nz),
         name="back",
@@ -1359,10 +1488,10 @@
             sds((rows, width), low),
             sds((rows, width), f32),
             sds((share, columns), f32),
-            sds((share, 3), f32),
-            sds((share, 7), f32),
-            sds((8, width), f32),
-            sds(fc1_own, f32),
+            sds((3, share), f32),
+            sds((7, share), f32),
+            sds((8, 128), f32),
+            sds(fc1.shape, f32),
             sds(fc2_own, f32),
             sds(unit.shape, f32),
         ),
@@ -1373,7 +1502,7 @@
             pltpu.VMEM((2, 2, rows, width), low),
             pltpu.VMEM((2, 2, rows, width), low),
             pltpu.VMEM((rows, width), low),
-            pltpu.VMEM((nz,) + fc1_own, low),
+            pltpu.VMEM((nz - 1, fc1.shape[0], late.shape[1]), low),
             pltpu.VMEM((nz,) + fc2_own, low),
             pltpu.VMEM((nz - 1,) + unit.shape, f32),
             pltpu.VMEM((nz, 2, 2, 2, share, columns), low),
@@ -1390,10 +1519,25 @@
             pltpu.VMEM((width, rows), low),
             pltpu.VMEM((rows, rows), f32),
             pltpu.VMEM((16, 8, width), f32),
-            pltpu.VMEM((3, 16, width), f32),
-            pltpu.VMEM((nz + 3, 16, width), f32),
-            pltpu.VMEM((width, 128), f32),
-            pltpu.SemaphoreType.DMA((3,)),
+            pltpu.VMEM((16, width), f32),
+            pltpu.VMEM((nz - 1, 16, width // nz), f32),
+            pltpu.VMEM((16, width // nz), f32),
+            pltpu.VMEM((3, 16, 128), f32),
+            pltpu.VMEM((3, 16, 128), f32),
+            pltpu.VMEM((128, 128), f32),
+            pltpu.VMEM((rows, width), f32),
+            pltpu.VMEM(proj.shape, low),
+            pltpu.VMEM((rows, width), f32),
+            pltpu.VMEM(lse.shape, f32),
+            pltpu.VMEM((rows, width), f32),
+            pltpu.VMEM((rows, width), f32),
+            pltpu.VMEM((rows, width), low),
+            pltpu.VMEM((rows, width), low),
+            pltpu.VMEM(qkv.shape, low),
+            pltpu.VMEM(out.shape, low),
+            pltpu.VMEM((rows, width), low),
+            pltpu.VMEM((rows, width), low),
+            pltpu.SemaphoreType.DMA((20,)),
             pltpu.SemaphoreType.DMA((count,)),
             pltpu.SemaphoreType.DMA((count,)),
         ],
@@ -1401,6 +1545,105 @@
             collective_id=3, has_side_effects=True, vmem_limit_bytes=63 * 2**20
         ),
     )(*operands)
+
+
+def finish_kernel(
+    mixed,
+    token,
+    weight,
+    fc1,
+    fc2,
+    gains,
+    biases,
+    scale,
+    unit,
+    mixed_out,
+    token_out,
+    qkv_out,
+    out_out,
+    fc1_out,
+    fc2_out,
+    gains_out,
+    biases_out,
+    scale_out,
+    gain_out,
+    shift_out,
+    mixed_at,
+    token_at,
+    weight_at,
+    fc1_at,
+    fc2_at,
+    in_sems,
+    out_sems,
+):
+    columns = qkv_out.shape[1]
+    moves = (
+        (token, token_at, ((token_at, token_out),)),
+        (
+            weight,
+            weight_at,
+            (
+                (weight_at.at[:, pl.ds(0, columns)], qkv_out),
+                (weight_at.at[:, pl.ds(columns, out_out.shape[1])], out_out),
+            ),
+        ),
+        (mixed, mixed_at, ((mixed_at, mixed_out),)),
+        (fc1, fc1_at, ((fc1_at, fc1_out),)),
+        (fc2, fc2_at, ((fc2_at, fc2_out),)),
+    )
+    reads, writes = [], []
+    for k, (src, here, _) in enumerate(moves):
+        reads.append(pltpu.make_async_copy(src, here, in_sems.at[k]))
+        reads[-1].start()
+    gains_out[...] = gains[...]
+    biases_out[...] = biases[...]
+    scale_out[...] = scale[0:1, : scale_out.shape[1]]
+    gain_out[...] = unit[0:1]
+    shift_out[0:1] = unit[1:2]
+    shift_out[1:2] = unit[2:3]
+    for read, (_, _, outs) in zip(reads, moves):
+        read.wait()
+        for src, dst in outs:
+            writes.append(pltpu.make_async_copy(src, dst, out_sems.at[len(writes)]))
+            writes[-1].start()
+    for write in writes:
+        write.wait()
+
+
+def finish(mixed, token, weight, gains, biases, scale, fc1, fc2, unit):
+    share, columns = weight.shape
+    width, units = token.shape[1], unit.shape[1]
+    f32 = jnp.float32
+    shapes = (
+        (mixed.shape, mixed.dtype),
+        (token.shape, f32),
+        ((share, columns - width), f32),
+        ((share, width), f32),
+        (fc1.shape, f32),
+        (fc2.shape, f32),
+        (gains.shape, f32),
+        (biases.shape, f32),
+        ((1, HEADS), f32),
+        ((1, units), f32),
+        ((2, units), f32),
+    )
+    return pl.pallas_call(
+        finish_kernel,
+        name="finish",
+        out_shape=tuple(jax.ShapeDtypeStruct(shape, kind) for shape, kind in shapes),
+        in_specs=[ANY] * 5 + [IN_VMEM] * 4,
+        out_specs=[ANY] * 6 + [IN_VMEM] * 5,
+        scratch_shapes=[
+            pltpu.VMEM(mixed.shape, mixed.dtype),
+            pltpu.VMEM(token.shape, f32),
+            pltpu.VMEM(weight.shape, f32),
+            pltpu.VMEM(fc1.shape, f32),
+            pltpu.VMEM(fc2.shape, f32),
+            pltpu.SemaphoreType.DMA((5,)),
+            pltpu.SemaphoreType.DMA((6,)),
+        ],
+        compiler_params=pltpu.CompilerParams(vmem_limit_bytes=63 * 2**20),
+    )(mixed, token, weight, fc1, fc2, gains, biases, scale, unit)
 
 
 def fused(
@@ -1418,10 +1661,6 @@
     mid_gain,
     ffn_biases,
 ):
-    units = w_fc1.shape[1]
-    unit_rows = jnp.concatenate(
-        [ffn_biases[:1], mid_gain[None], ffn_biases[1:], jnp.zeros((5, units), jnp.float32)]
-    )
     (
         qkv_full,
         out_full,
@@ -1434,8 +1673,9 @@
         nin,
         scaled,
         ffn_part,
-        fc1_part,
         fc2_part,
+        fc1_late,
+        fc1_own,
         gnm,
         unit_sums,
     ) = fore(
@@ -1450,16 +1690,17 @@
         head_scale,
         w_fc1,
         w_fc2,
-        unit_rows,
+        mid_gain[None],
+        ffn_biases,
     )
     model_width = tokens.shape[1]
     (
-        mixed_out,
+        mixed,
         token_grad,
         weight_grad,
         gains_grad,
         biases_grad,
-        scale_sums,
+        scale,
         fc1_grad,
         fc2_grad,
         unit_sums,
@@ -1467,7 +1708,8 @@
         nz,
         gnm,
         ffn_part,
-        fc1_part,
+        fc1_late,
+        fc1_own,
         fc2_part,
         unit_sums,
         proj,
@@ -1484,18 +1726,29 @@
         tokens,
         doc_lengths,
     )
-    return (
-        mixed_out,
+    mixed, token_grad, qkv, out, fc1, fc2, gains_grad, biases_grad, scale, gain, shift = finish(
+        mixed,
         token_grad,
-        weight_grad[:, : w_qkv.shape[1]],
-        weight_grad[:, w_qkv.shape[1] :],
+        weight_grad,
         gains_grad,
         biases_grad,
-        jnp.sum(scale_sums[2].reshape(HEADS, -1), axis=1),
+        scale,
         fc1_grad,
         fc2_grad,
-        unit_sums[0],
-        unit_sums[1:3],
+        unit_sums,
+    )
+    return (
+        mixed,
+        token_grad,
+        qkv,
+        out,
+        gains_grad.T,
+        biases_grad.T,
+        scale[0],
+        fc1,
+        fc2,
+        gain[0],
+        shift,
     )
 
 

time: 246 us -> 203 us (0.83)
  Pallas kernels: 224 us -> 202 us
  local copies, waits for them, and re-layouts: 19 us -> 0 us
    pallas_call x1, Pallas kernels: 98.1 us -> 71.8 us  [back(): pl.pallas_call(functools.partial(back_kernel, nz), name='back', out_shape...]
    unnamed x12 -> x0, local copies, waits for them, and re-layouts: 11.3 us -> none
    slice x6 -> x0, local copies, waits for them, and re-layouts: 7.48 us -> none  [the longest x1 1.77 us: fused(): weight_grad[:, :w_qkv.shape[1]]]
    pallas_call x0 -> x1, Pallas kernels: none -> 4.32 us  [finish(): pl.pallas_call(finish_kernel, name='finish', out_shape=tuple((jax.ShapeDt...]
where the time goes in v5:
time: 203 us
  Pallas kernels  202 us (100%)
    pallas_call x1, Pallas kernels, fore(): pl.pallas_call(functools.partial(fore_kernel, nz), name='fore', out_shape...  126 us
    pallas_call x1, Pallas kernels, back(): pl.pallas_call(functools.partial(back_kernel, nz), name='back', out_shape...  71.8 us
    pallas_call x1, Pallas kernels, finish(): pl.pallas_call(finish_kernel, name='finish', out_shape=tuple((jax.ShapeDt...  4.32 us

profile of v5, /device:TPU:0, one launch (start us, length us, event | category | flops | bytes accessed | tf_op | source)
XLA Modules:
  0.0 202.6 jit_solution(7214507703122249553)
XLA Ops:
  0.6 125.7 %fore.1 = (bf16[4,2,2,2,32,3072]{5,4,3,2,1,0:T(8,128)(2,1)}, bf16[4,2,2,2,32,1024]{5,4,3,2,1,0:T(8,128)(2,1)}, f32[16,1024]{1,0:T(8,128)}, bf16[256,3072]{1,0:T(...) custom-call(bf16[256,1024]{1,0:T(8,128)(2,1)} %tok_in.1, ...), custom_call_target="tpu_custom_call" | custom-call | tf_op jit(solution)/shard_map/fore/pallas_call | solution.py:951
  126.3 71.8 %back.1 = (bf16[256,1024]{1,0:T(8,128)(2,1)}, f32[256,1024]{1,0:T(8,128)}, f32[32,4096]{1,0:T(8,128)}, f32[3,32]{1,0:T(4,128)}, f32[7,32]{1,0:T(8,128)}, /*index...) custom-call(f32[256,1024]{1,0:T(8,128)} %get-tuple-element.47.gnm_in, ...), custom_call_target="tpu_custom_call" | custom-call | tf_op jit(solution)/shard_map/back/pallas_call | solution.py:1484
  198.1 4.3 %finish.1 = (bf16[256,1024]{1,0:T(8,128)(2,1)}, f32[256,1024]{1,0:T(8,128)}, f32[32,3072]{1,0:T(8,128)}, f32[32,1024]{1,0:T(8,128)}, f32[256,512]{1,0:T(8,128)},...) custom-call(bf16[256,1024]{1,0:T(8,128)(2,1)} %get-tuple-element.63., ...), custom_call_target="tpu_custom_call" | custom-call | tf_op jit(solution)/shard_map/finish/pallas_call | solution.py:1630

commit v6 on v5

--- a/solution.py
+++ b/solution.py
@@ -374,7 +374,7 @@
     def part(self, y, x, c, rows):
         return self.whole.at[y, x, c, rows]
 
-    def start(self, src):
+    def start_first(self, src):
         (y, x, c), (to_x, to_y, to_c), lo, hi = self.here, self.targets, self.lo, self.hi
         go = self.sends.start
         self.first = [
@@ -382,6 +382,10 @@
             go(src.at[hi], self.part(y, x, c, hi), to_y),
         ]
         self.core = [go(src, self.whole.at[y, x, c], to_c)]
+
+    def start_second(self, src):
+        (y, x, c), (to_x, to_y, _), lo, hi = self.here, self.targets, self.lo, self.hi
+        go = self.sends.start
         self.second = [
             go(src.at[lo], self.part(y, x, c, lo), to_y),
             go(src.at[hi], self.part(y, x, c, hi), to_x),
@@ -477,7 +481,9 @@
     sums,
     from_one,
     from_two,
-    ffn_part,
+    f_part,
+    f_core,
+    f_sums,
     fc1_part,
     late_part,
     fc2_part,
@@ -556,6 +562,8 @@
         return sends.start(ref, ref, to_c)
 
     a0, a1 = [first(qkv_all, z, 0)], [first(qkv_all, z, 1)]
+    og = Plane(sends, og_all, (y, x, c), (to_x, to_y, to_c))
+    og.start_first(og_ref)
     tok_in = fetch(tok_ref, tok)
     out_in = fetch(out_ref, out_all.at[z, y, x, c])
     fc1_in = fetch(fc1_ref, own1)
@@ -570,22 +578,22 @@
     wait_all(vec_z)
     by_x = vec_all.at[:, y, x, c]
     vec_x = sends.start(by_x, by_x, to_x)
-    qkv_z[0][0].wait_recv()
-    a0.append(first(qkv_all, slots[1], 0))
+    wait_all(a0[0])
+    b0 = [second(qkv_all, z, 0)]
+    wait_all(a1[0])
+    b1 = [second(qkv_all, z, 1)]
     vec_x.wait_recv()
     by_y = vec_all.at[:, y, :, c]
     vec_y = sends.start(by_y, by_y, to_y)
-    for k in range(2, nz):
+    for k in range(1, nz):
         qkv_z[0][k - 1].wait_recv()
         a0.append(first(qkv_all, slots[k], 0))
-    b0 = []
-    for k in range(nz):
+    vec_y.wait_recv()
+    by_c = vec_all.at[:, :, :, c]
+    vec_c = sends.start(by_c, by_c, to_c)
+    for k in range(1, nz):
         wait_all(a0[k])
         b0.append(second(qkv_all, slots[k], 0))
-        if k == 0:
-            vec_y.wait_recv()
-            by_c = vec_all.at[:, :, :, c]
-            vec_c = sends.start(by_c, by_c, to_c)
     mask[...] = doc_mask(doc_ref, rows)
     tok_in.wait()
 
@@ -627,10 +635,8 @@
     fc1_z = [sends.start(fc1_ref, own1, peer) for peer in peers]
     wait_all(b0[nz - 1])
     c0.append(third(qkv_all, slots[nz - 1], 0))
-    b1 = []
-    for k in range(2):
-        wait_all(a1[k])
-        b1.append(second(qkv_all, slots[k], 1))
+    wait_all(a1[1])
+    b1.append(second(qkv_all, slots[1], 1))
     wait_all(c0)
 
     def project(p):
@@ -681,8 +687,7 @@
     for k in range(1, nz):
         out_z[k - 1].wait_recv()
         out_a.append(first(out_all, slots[k]))
-    og = Plane(sends, og_all, (y, x, c), (to_x, to_y, to_c))
-    og.start(og_ref)
+    og.start_second(og_ref)
     lax.fori_loop(1, 2, attend, 0)
     c1 = []
     for k in range(2):
@@ -726,7 +731,8 @@
 
     lax.fori_loop(0, rows // step, middles, 0)
     mid = Plane(sends, mid_all, (y, x, c), (to_x, to_y, to_c))
-    mid.start(mid_all.at[y, x, c])
+    mid.start_first(mid_all.at[y, x, c])
+    mid.start_second(mid_all.at[y, x, c])
     saves += [fetch(branch, branch_out), fetch(middle, middle_out)]
 
     def grads(yy, xx, cc):
@@ -759,7 +765,6 @@
             folded = pre[:, j * (units // 4) : (j + 1) * (units // 4)]
             stats[yy, xx, cc, j : j + 1] = jnp.sum(folded.T, axis=0, keepdims=True)
 
-    stats[...] = jnp.zeros_like(stats)
     og.after_second()
     fc2_in.wait()
     fc2_far.wait_recv()
@@ -844,20 +849,34 @@
 
     left, right = pl.ds(0, width // 2), pl.ds(width // 2, width // 2)
     order = [(1 - y, 1 - x), (y, 1 - x), (1 - y, x), (y, x)]
-    stage_x, stage_y = [], []
-    for k, (yy, xx) in enumerate(order):
+    stage_x, stage_y, cores = [], [], []
+
+    def to_core(k):
+        yy, xx = order[k]
         mid_part[yy, xx] = backward(yy, xx, 1 - c).astype(low)
-        core = sends.start(mid_part.at[yy, xx], from_core.at[yy, xx], to_c)
+        cores.append(sends.start(mid_part.at[yy, xx], from_core.at[yy, xx], to_c))
+
+    def from_pair(k):
+        yy, xx = order[k]
         block = backward(yy, xx, c)
-        core.wait_recv()
+        cores[k].wait_recv()
         sums[yy, xx] = (block + from_core[yy, xx].astype(f32)).astype(low)
         if k in (0, 1):
             stage_x.append(sends.start(sums.at[yy, xx, :, left], from_one.at[yy, :, left], to_x))
         if k in (0, 2):
             stage_y.append(sends.start(sums.at[yy, xx, :, right], from_one.at[xx, :, right], to_y))
 
+    to_core(0)
+    to_core(1)
+    from_pair(0)
+    to_core(2)
+    from_pair(1)
+    to_core(3)
+    from_pair(2)
+    from_pair(3)
+
     def ffn_of(yy, xx, cc):
-        ffn_part[yy, xx, cc] = dot(hidden[yy, xx, cc], fc2_all[...]).astype(low)
+        return dot(hidden[yy, xx, cc], fc2_all[...])
 
     blocks = nz
     size = width // blocks
@@ -892,10 +911,15 @@
 
     lax.fori_loop(0, blocks, late_block, 0)
     saves.append(fetch(late_part, late_out))
+    cores = []
     for yy, xx in order:
-        ffn_of(yy, xx, 1 - c)
-        ffn_of(yy, xx, c)
-    saves.append(fetch(ffn_part, ffn_out))
+        f_part[yy, xx] = ffn_of(yy, xx, 1 - c).astype(low)
+        cores.append(sends.start(f_part.at[yy, xx], f_core.at[yy, xx], to_c))
+    for k, (yy, xx) in enumerate(order):
+        block = ffn_of(yy, xx, c)
+        cores[k].wait_recv()
+        f_sums[yy, xx] = (block + f_core[yy, xx].astype(f32)).astype(low)
+    saves.append(fetch(f_sums, ffn_out))
 
     def fc2_block(k, carry):
         part = pl.ds(pl.multiple_of(k * size, 128), size)
@@ -941,7 +965,7 @@
         ((rows, width), f32),
         ((rows, width), low),
         ((rows, width), low),
-        (plane + (rows, width), low),
+        ((2, 2, rows, width), low),
         ((units, width), low),
         ((width, units // 2), low),
         (fc1.shape, f32),
@@ -982,15 +1006,17 @@
             vm(plane + (rows, units), low),
             vm((2, 2, rows, width), low),
             vm((rows, units), f32),
-            vm(plane + (8, rows), f32),
-            vm(plane + (8, rows), f32),
-            vm((4,) + plane + (8, rows), f32),
-            vm(plane + (8, rows), f32),
+            vm(plane + (4, rows), f32),
+            vm(plane + (4, rows), f32),
+            vm((4,) + plane + (4, rows), f32),
+            vm(plane + (4, rows), f32),
             vm((2, 2, rows, width), low),
             vm((2, 2, rows, width), low),
             vm((2, rows, width), low),
             vm((rows, width), low),
-            vm(plane + (rows, width), low),
+            vm((2, 2, rows, width), low),
+            vm((2, 2, rows, width), low),
+            vm((2, 2, rows, width), low),
             vm((nz - 1, fc1.shape[0], units // 2), low),
             vm((width, units // 2), low),
             vm((units, width), low),
@@ -1035,7 +1061,6 @@
     fc1_out,
     fc2_out,
     unit_out,
-    f_core,
     f_sums,
     f_one,
     f_two,
@@ -1062,6 +1087,10 @@
     small_half,
     small_got,
     turned,
+    mixed_at,
+    weight_at,
+    fc1_at,
+    fc2_at,
     gnm_ref,
     proj_ref,
     att_ref,
@@ -1083,20 +1112,6 @@
     to_xy = at(z, 1 - y, 1 - x, c)
     others = [lax.rem(z + k, nz) for k in range(1, nz)]
     peers = [at(other, y, x, c) for other in others]
-    greet([to_x, to_y, to_c, to_xy] + peers)
-    sends = Sends(send_sems, recv_sems)
-    rows, width = middle_ref.shape
-    low = jnp.bfloat16
-    f32 = jnp.float32
-    share = weight_out.shape[0]
-    width1, width2 = fc1_out.shape[0], fc2_out.shape[1]
-
-    pieces = 2
-    parts = [pl.ds(k * (rows // pieces), rows // pieces) for k in range(pieces)]
-    left, right = pl.ds(0, width // 2), pl.ds(width // 2, width // 2)
-    f_c = [
-        sends.start(ffn_ref.at[:, :, 1 - c, part], f_core.at[:, :, part], to_c) for part in parts
-    ]
     locals_ = []
 
     def fetch(src, dst):
@@ -1109,7 +1124,7 @@
     gnm_got = fetch(gnm_in, gnm_ref)
     og_got = fetch(og_in, og_ref)
     branch_got = fetch(branch_in, branch_ref)
-    ffn_got = fetch(ffn_ref.at[:, :, c], f_sums)
+    ffn_got = fetch(ffn_ref, f_sums)
     out_got = fetch(out_in, out_ref)
     att_got = fetch(att_in, att_ref)
     scaled_got = fetch(scaled_in, scaled_ref)
@@ -1119,13 +1134,24 @@
     qkv_got = fetch(qkv_in, qkv_ref)
     tok_got = fetch(tok_in, tok_ref)
 
+    greet([to_x, to_y, to_c, to_xy] + peers)
+    sends = Sends(send_sems, recv_sems)
+    rows, width = middle_ref.shape
+    low = jnp.bfloat16
+    f32 = jnp.float32
+    share = weight_out.shape[0]
+    width1, width2 = fc1_out.shape[0], fc2_out.shape[1]
+
+    pieces = 2
+    parts = [pl.ds(k * (rows // pieces), rows // pieces) for k in range(pieces)]
+    left, right = pl.ds(0, width // 2), pl.ds(width // 2, width // 2)
     def block1(which):
         return late_ref.at[pl.ds(pl.multiple_of(which * width1, width1), width1)]
 
     def block2(which):
         return fc2_ref.at[:, pl.ds(pl.multiple_of(which * width2, width2), width2)]
 
-    own1_got = fetch(own1_in, fc1_out)
+    own1_got = fetch(own1_in, fc1_at)
     own2_got = fetch(block2(z), got2.at[nz - 1])
     far = []
     for k, peer in enumerate(peers):
@@ -1137,21 +1163,17 @@
 
     def ffn_one(k):
         part = parts[k]
-        f_c[k].wait_recv()
+        f_first.append(
+            (
+                sends.start(ffn_ref.at[:, 1 - x, part, left], f_one.at[0, :, part, left], to_x),
+                sends.start(ffn_ref.at[1 - y, :, part, right], f_one.at[1, :, part, right], to_y),
+            )
+        )
+
+    def ffn_two(k):
+        part = parts[k]
         if k == 0:
             ffn_got.wait()
-        for yy in range(2):
-            for xx in range(2):
-                f_sums[yy, xx, part] = add_low(f_sums[yy, xx, part], f_core[yy, xx, part])
-        f_first.append(
-            (
-                sends.start(f_sums.at[:, 1 - x, part, left], f_one.at[0, :, part, left], to_x),
-                sends.start(f_sums.at[1 - y, :, part, right], f_one.at[1, :, part, right], to_y),
-            )
-        )
-
-    def ffn_two(k):
-        part = parts[k]
         for copy in f_first[k]:
             copy.wait_recv()
         f_sums[1 - y, x, part, left] = add_low(
@@ -1177,9 +1199,10 @@
                 + f_one[i, at_, part, cols].astype(f32)
                 + f_two[part, cols].astype(f32)
             )
-            mixed_out[part, cols] = (
+            mixed_at[part, cols] = (
                 middle_ref[part, cols] + total + vec_ref[9:10, cols]
             ).astype(low)
+        puts.append(fetch(mixed_at.at[part], mixed_out.at[part]))
 
     spans = [(0, width)] + [(width + g * 3 * width // 4, 3 * width // 4) for g in range(4)]
     w_first, w_second, w_third, w_c = {}, {}, {}, {}
@@ -1252,13 +1275,17 @@
             w_third[j][k].wait_recv()
             total = total + w_far[k, :, every].astype(f32)
         if j == 0:
-            weight_out[:, 3 * width :] = total
+            weight_at[:, 3 * width :] = total
+            spots = [pl.ds(3 * width, width)]
         else:
             third = size // 3
-            for i in range(3):
-                first = i * width + (j - 1) * third
-                weight_out[:, first : first + third] = total[:, i * third : (i + 1) * third]
-
+            spots = [pl.ds(i * width + (j - 1) * third, third) for i in range(3)]
+            for i, spot in enumerate(spots):
+                weight_at[:, spot] = total[:, i * third : (i + 1) * third]
+        for spot in spots:
+            puts.append(fetch(weight_at.at[:, spot], weight_out.at[:, spot]))
+
+    ffn_one(0)
     accs[...] = jnp.zeros_like(accs)
     step = 32
 
@@ -1284,7 +1311,6 @@
         copy.wait()
     lax.fori_loop(0, rows // step, norms, 0)
     mask[...] = doc_mask(doc_ref, rows)
-    ffn_one(0)
     quarter = width // 4
 
     def scaled_block(k, carry):
@@ -1357,115 +1383,147 @@
         lax.fori_loop(0, nz, one, 0)
         w_zero(j)
 
-    lax.fori_loop(0, 1, pair, 0)
-    w_step1(0)
-    lax.fori_loop(1, 2, pair, 0)
-    wgrad(1)
-    ffn_two(0)
-    lax.fori_loop(2, 3, pair, 0)
-    w_step1(1)
-    lax.fori_loop(3, 4, pair, 0)
-    wgrad(2)
-    w_step2(0)
-    lax.fori_loop(4, 5, pair, 0)
-    w_step1(2)
-    lax.fori_loop(5, 6, pair, 0)
-    wgrad(3)
-    w_step2(1)
-    w_step3(0)
-    lax.fori_loop(6, 7, pair, 0)
-    w_step1(3)
-    lax.fori_loop(7, 8, pair, 0)
-    wgrad(4)
-
     def gni_block(k, carry):
         part = pl.ds(pl.multiple_of(k * quarter, quarter), quarter)
         gni[:, part] = dot(dproj[...], qkv_ref[part], NT)
         return carry
 
-    qkv_got.wait()
-    lax.fori_loop(0, 4, gni_block, 0)
-
     def tokens_back(k, carry):
         part = pl.ds(pl.multiple_of(k * step, step), step)
         normed, inverse = centered(tok_ref[part].astype(f32))
         grad = gni[part]
-        token_out[part] = gmid[part] + centered_back(grad * vec_ref[0:1], normed, inverse)
+        gmid[part] = gmid[part] + centered_back(grad * vec_ref[0:1], normed, inverse)
         accs[0] += eights(grad * normed)
         accs[3] += eights(grad)
         return carry
 
-    tok_got.wait()
-    lax.fori_loop(0, rows // step, tokens_back, 0)
-    for j in range(16):
-        small[j : j + 1] = jnp.sum(accs[j], axis=0, keepdims=True)
-    spot = lax.broadcasted_iota(jnp.int32, (1, width), 1)
-    tile = jnp.zeros((1, 128), f32)
-    for h in range(HEADS):
-        inside = jnp.logical_and(spot >= h * head, spot < (h + 1) * head)
-        found = jnp.sum(jnp.where(inside, small[10:11], 0.0), axis=1, keepdims=True)
-        tile = jnp.where(lane == h, found, tile)
-    small[11:12] = jnp.concatenate([tile] * (width // 128), axis=1)
     part_z = width // nz
+    chain = {}
 
     def lanes(which):
         return pl.ds(pl.multiple_of(which * part_z, 128), part_z)
 
-    small_z = [
-        sends.start(small.at[:, lanes(others[k])], small_far.at[k], peer)
-        for k, peer in enumerate(peers)
-    ]
+    def small_start():
+        for j in range(16):
+            small[j : j + 1] = jnp.sum(accs[j], axis=0, keepdims=True)
+        spot = lax.broadcasted_iota(jnp.int32, (1, width), 1)
+        tile = jnp.zeros((1, 128), f32)
+        for h in range(HEADS):
+            inside = jnp.logical_and(spot >= h * head, spot < (h + 1) * head)
+            found = jnp.sum(jnp.where(inside, small[10:11], 0.0), axis=1, keepdims=True)
+            tile = jnp.where(lane == h, found, tile)
+        small[11:12] = jnp.concatenate([tile] * (width // 128), axis=1)
+        chain["z"] = [
+            sends.start(small.at[:, lanes(others[k])], small_far.at[k], peer)
+            for k, peer in enumerate(peers)
+        ]
+
+    def small_second():
+        total = small[:, lanes(z)]
+        for k in range(nz - 1):
+            chain["z"][k].wait_recv()
+            total = total + small_far[k]
+        small_y[...] = total
+        other = small_y.at[:, pl.ds(pl.multiple_of((1 - y) * 128, 128), 128)]
+        chain["y"] = sends.start(other, small_got.at[0], to_y)
+
+    def small_third():
+        chain["y"].wait_recv()
+        small_half[0] = small_y[:, pl.ds(pl.multiple_of(y * 128, 128), 128)] + small_got[0]
+        chain["x"] = sends.start(small_half.at[0], small_got.at[1], to_x)
+
+    def small_fourth():
+        chain["x"].wait_recv()
+        small_half[1] = small_half[0] + small_got[1]
+        chain["c"] = sends.start(small_half.at[1], small_got.at[2], to_c)
+
+    def small_last():
+        chain["c"].wait_recv()
+        total = small_half[1] + small_got[2]
+        scale_out[...] = jnp.broadcast_to(total[11:12], (8, 128))
+        ours = pl.ds(pl.multiple_of((2 * x + c) * share, share), share)
+        turned[...] = jnp.concatenate([total, jnp.zeros((112, 128), f32)], axis=0).T
+        mine = jnp.concatenate([turned[ours], jnp.zeros((128 - share, 128), f32)], axis=0).T
+        gains_out[...] = mine[0:3, :share]
+        biases_out[...] = mine[3:10, :share]
+
+    puts = []
+
+    def far_last():
+        for copy in far:
+            copy.wait_recv()
+        own1_got.wait()
+        own2_got.wait()
+        late = pl.ds(fc1_at.shape[1] - got1.shape[2], got1.shape[2])
+        own2, unit = got2[nz - 1].astype(f32), unit_ref[...]
+        for k in range(nz - 1):
+            fc1_at[:, late] += got1[k].astype(f32)
+            own2 = own2 + got2[k].astype(f32)
+            unit = unit + got_unit[k]
+        fc2_at[...] = own2
+        unit_out[...] = unit
+        puts.append(fetch(fc1_at, fc1_out))
+        puts.append(fetch(fc2_at, fc2_out))
+
+    def pairs(first, last):
+        lax.fori_loop(first, last, pair, 0)
+
+    def gni_all():
+        qkv_got.wait()
+        lax.fori_loop(0, 4, gni_block, 0)
+
+    def tokens_all():
+        tok_got.wait()
+        lax.fori_loop(0, rows // step, tokens_back, 0)
+        puts.append(fetch(gmid, token_out))
+
+    pairs(0, 1)
+    w_step1(0)
+    pairs(1, 2)
+    wgrad(1)
+    ffn_two(0)
+    pairs(2, 3)
+    w_step1(1)
+    pairs(3, 4)
+    wgrad(2)
+    w_step2(0)
+    pairs(4, 5)
+    w_step1(2)
+    pairs(5, 6)
+    wgrad(3)
+    w_step2(1)
+    w_step3(0)
+    pairs(6, 7)
+    w_step1(3)
+    pairs(7, 8)
+    wgrad(4)
     w_step2(2)
+    gni_all()
     w_step3(1)
     w_step1(4)
-    total = small[:, lanes(z)]
-    for k in range(nz - 1):
-        small_z[k].wait_recv()
-        total = total + small_far[k]
-    small_y[...] = total
-    mine = small_y.at[:, pl.ds(pl.multiple_of(y * 128, 128), 128)]
-    other = small_y.at[:, pl.ds(pl.multiple_of((1 - y) * 128, 128), 128)]
-    by_y = sends.start(other, small_got.at[0], to_y)
+    tokens_all()
+    small_start()
     w_step2(3)
-    by_y.wait_recv()
-    small_half[0] = mine[...] + small_got[0]
-    by_x = sends.start(small_half.at[0], small_got.at[1], to_x)
     w_step3(2)
-    ffn_three(0)
     ffn_one(1)
-    by_x.wait_recv()
-    small_half[1] = small_half[0] + small_got[1]
-    by_c = sends.start(small_half.at[1], small_got.at[2], to_c)
+    small_second()
     w_step2(4)
     w_step3(3)
-    by_c.wait_recv()
-    total = small_half[1] + small_got[2]
-    scale_out[...] = jnp.broadcast_to(total[11:12], (8, 128))
-    ours = pl.ds(pl.multiple_of(x * 64 + c * 32, 32), 32)
-    turned[...] = jnp.concatenate([total, jnp.zeros((112, 128), f32)], axis=0).T
-    ours = jnp.concatenate([turned[ours], jnp.zeros((96, 128), f32)], axis=0).T
-    gains_out[...] = ours[0:3, :share]
-    biases_out[...] = ours[3:10, :share]
-    ffn_two(1)
+    ffn_three(0)
+    small_third()
     w_step4(0)
     w_step4(1)
+    small_fourth()
+    ffn_two(1)
     w_step3(4)
     w_step4(2)
-    for copy in far:
-        copy.wait_recv()
-    own1_got.wait()
-    own2_got.wait()
-    late = pl.ds(fc1_out.shape[1] - got1.shape[2], got1.shape[2])
-    own2, unit = got2[nz - 1].astype(f32), unit_ref[...]
-    for k in range(nz - 1):
-        fc1_out[:, late] += got1[k].astype(f32)
-        own2 = own2 + got2[k].astype(f32)
-        unit = unit + got_unit[k]
-    fc2_out[...] = own2
-    unit_out[...] = unit
+    small_last()
+    far_last()
     w_step4(3)
     ffn_three(1)
     w_step4(4)
+    for put in puts:
+        put.wait()
     sends.finish()
 
 
@@ -1496,9 +1554,8 @@
             sds(unit.shape, f32),
         ),
         in_specs=specs,
-        out_specs=[IN_VMEM] * 9,
+        out_specs=[ANY] * 3 + [IN_VMEM] * 3 + [ANY] * 2 + [IN_VMEM],
         scratch_shapes=[
-            pltpu.VMEM((2, 2, rows, width), low),
             pltpu.VMEM((2, 2, rows, width), low),
             pltpu.VMEM((2, 2, rows, width), low),
             pltpu.VMEM((rows, width), low),
@@ -1525,6 +1582,10 @@
             pltpu.VMEM((3, 16, 128), f32),
             pltpu.VMEM((3, 16, 128), f32),
             pltpu.VMEM((128, 128), f32),
+            pltpu.VMEM((rows, width), low),
+            pltpu.VMEM((share, columns), f32),
+            pltpu.VMEM(fc1.shape, f32),
+            pltpu.VMEM(fc2_own, f32),
             pltpu.VMEM((rows, width), f32),
             pltpu.VMEM(proj.shape, low),
             pltpu.VMEM((rows, width), f32),
@@ -1537,7 +1598,7 @@
             pltpu.VMEM(out.shape, low),
             pltpu.VMEM((rows, width), low),
             pltpu.VMEM((rows, width), low),
-            pltpu.SemaphoreType.DMA((20,)),
+            pltpu.SemaphoreType.DMA((48,)),
             pltpu.SemaphoreType.DMA((count,)),
             pltpu.SemaphoreType.DMA((count,)),
         ],

time: 203 us -> 191 us (0.941)
  Pallas kernels: 202 us -> 190 us
    pallas_call x1, Pallas kernels: 126 us -> 118 us  [fore(): pl.pallas_call(functools.partial(fore_kernel, nz), name='fore', out_shape...]
    pallas_call x1, Pallas kernels: 71.8 us -> 67.3 us  [back(): pl.pallas_call(functools.partial(back_kernel, nz), name='back', out_shape...]
where the time goes in v6:
time: 191 us; the launch traced here: 190 us
  Pallas kernels  190 us (99%)
    pallas_call x1, Pallas kernels, fore(): pl.pallas_call(functools.partial(fore_kernel, nz), name='fore', out_shape...  118 us
    pallas_call x1, Pallas kernels, back(): pl.pallas_call(functools.partial(back_kernel, nz), name='back', out_shape...  67.3 us
    pallas_call x1, Pallas kernels, finish(): pl.pallas_call(finish_kernel, name='finish', out_shape=tuple((jax.ShapeDt...  4.32 us

profile of v6, /device:TPU:0, one launch (start us, length us, event | category | flops | bytes accessed | tf_op | source)
XLA Modules:
  0.0 190.4 jit_solution(2366830690490708602)
XLA Ops:
  0.6 117.9 %fore.1 = (bf16[4,2,2,2,32,3072]{5,4,3,2,1,0:T(8,128)(2,1)}, bf16[4,2,2,2,32,1024]{5,4,3,2,1,0:T(8,128)(2,1)}, f32[16,1024]{1,0:T(8,128)}, bf16[256,3072]{1,0:T(...) custom-call(bf16[256,1024]{1,0:T(8,128)(2,1)} %tok_in.1, ...), custom_call_target="tpu_custom_call" | custom-call | tf_op jit(solution)/shard_map/fore/pallas_call | solution.py:975
  118.6 67.3 %back.1 = (bf16[256,1024]{1,0:T(8,128)(2,1)}, f32[256,1024]{1,0:T(8,128)}, f32[32,4096]{1,0:T(8,128)}, f32[3,32]{1,0:T(4,128)}, f32[7,32]{1,0:T(8,128)}, /*index...) custom-call(f32[256,1024]{1,0:T(8,128)} %get-tuple-element.47.gnm_in, ...), custom_call_target="tpu_custom_call" | custom-call | tf_op jit(solution)/shard_map/back/pallas_call | solution.py:1542
  185.9 4.3 %finish.1 = (bf16[256,1024]{1,0:T(8,128)(2,1)}, f32[256,1024]{1,0:T(8,128)}, f32[32,3072]{1,0:T(8,128)}, f32[32,1024]{1,0:T(8,128)}, f32[256,512]{1,0:T(8,128)},...) custom-call(bf16[256,1024]{1,0:T(8,128)(2,1)} %get-tuple-element.63., ...), custom_call_target="tpu_custom_call" | custom-call | tf_op jit(solution)/shard_map/finish/pallas_call | solution.py:1691

commit v7 on v6

--- a/solution.py
+++ b/solution.py
@@ -410,10 +410,11 @@
 
     def after_third(self):
         y, x, c = self.here
-        for copy in self.third:
+        self.last = []
+        for copy, part in zip(self.third, (self.lo, self.hi)):
             copy.wait_recv()
-        ref = self.whole.at[1 - y, 1 - x, c]
-        self.last = self.sends.start(ref, ref, self.targets[2])
+            ref = self.part(1 - y, 1 - x, c, part)
+            self.last.append(self.sends.start(ref, ref, self.targets[2]))
 
 
 def fore_kernel(
@@ -441,10 +442,11 @@
     nin_out,
     scaled_out,
     ffn_out,
+    first_out,
     fc2_out,
     late_out,
+    gnm_out,
     fc1_out,
-    gnm_out,
     unit_out,
     qkv_all,
     out_all,
@@ -543,6 +545,13 @@
         for span in spans
     ]
 
+    z_pair = z + 1 - 2 * lax.rem(z, 2)
+    pair_peer, far_peer = at(z_pair, y, x, c), peers[1]
+    qkv_slots = slots
+
+    def go_on(p):
+        qkv_z[p][0].wait_recv()
+
     def sides(whole, p):
         size = phase // 2 if whole is qkv_all else whole.shape[-1] // 2
         return pl.ds(2 * p * size, size), pl.ds((2 * p + 1) * size, size)
@@ -575,6 +584,15 @@
     unit_ref[1:2] = gain_ref[...]
     unit_ref[2:3] = shift_ref[1:2]
     step = 32
+    mask[...] = doc_mask(doc_ref, rows)
+    tok_in.wait()
+
+    def normed(k, carry):
+        part = pl.ds(pl.multiple_of(k * step, step), step)
+        branch[part] = centered(tok[part].astype(f32))[0]
+        return carry
+
+    lax.fori_loop(0, rows // step, normed, 0)
     wait_all(vec_z)
     by_x = vec_all.at[:, y, x, c]
     vec_x = sends.start(by_x, by_x, to_x)
@@ -582,27 +600,22 @@
     b0 = [second(qkv_all, z, 0)]
     wait_all(a1[0])
     b1 = [second(qkv_all, z, 1)]
+    go_on(0)
+    a0.append(first(qkv_all, qkv_slots[1], 0))
     vec_x.wait_recv()
     by_y = vec_all.at[:, y, :, c]
     vec_y = sends.start(by_y, by_y, to_y)
-    for k in range(1, nz):
+    for k in range(2, nz):
         qkv_z[0][k - 1].wait_recv()
-        a0.append(first(qkv_all, slots[k], 0))
+        a0.append(first(qkv_all, qkv_slots[k], 0))
     vec_y.wait_recv()
     by_c = vec_all.at[:, :, :, c]
     vec_c = sends.start(by_c, by_c, to_c)
     for k in range(1, nz):
         wait_all(a0[k])
-        b0.append(second(qkv_all, slots[k], 0))
-    mask[...] = doc_mask(doc_ref, rows)
-    tok_in.wait()
-
-    def normed(k, carry):
-        part = pl.ds(pl.multiple_of(k * step, step), step)
-        branch[part] = centered(tok[part].astype(f32))[0]
-        return carry
-
-    lax.fori_loop(0, rows // step, normed, 0)
+        b0.append(second(qkv_all, qkv_slots[k], 0))
+    go_on(1)
+    a1.append(first(qkv_all, qkv_slots[1], 1))
     vec_c.wait_recv()
     vec[...] = vec_all[...].reshape(width, 128).T[:16]
     spot = lax.broadcasted_iota(jnp.int32, (1, width), 1)
@@ -619,24 +632,23 @@
         return carry
 
     lax.fori_loop(0, rows // step, scaled_in, 0)
-    c0 = []
-    for k in range(1, nz):
+    wait_all(b0[0])
+    c0 = [third(qkv_all, z, 0)]
+    for k in range(2, nz):
         qkv_z[1][k - 1].wait_recv()
-        a1.append(first(qkv_all, slots[k], 1))
+        a1.append(first(qkv_all, qkv_slots[k], 1))
         wait_all(b0[k - 1])
-        c0.append(third(qkv_all, slots[k - 1], 0))
+        c0.append(third(qkv_all, qkv_slots[k - 1], 0))
     out_in.wait()
     own_out = out_all.at[z, y, x, c]
     out_z = [sends.start(own_out, own_out, peer) for peer in peers]
-    pair_peer = at(z + 1 - 2 * lax.rem(z, 2), y, x, c)
-    far_peer = peers[1]
     fc2_far = sends.start(fc2_ref, own2, far_peer)
     fc2_near = sends.start(fc2_ref, own2, pair_peer)
     fc1_z = [sends.start(fc1_ref, own1, peer) for peer in peers]
     wait_all(b0[nz - 1])
-    c0.append(third(qkv_all, slots[nz - 1], 0))
+    c0.append(third(qkv_all, qkv_slots[nz - 1], 0))
     wait_all(a1[1])
-    b1.append(second(qkv_all, slots[1], 1))
+    b1.append(second(qkv_all, qkv_slots[1], 1))
     wait_all(c0)
 
     def project(p):
@@ -664,7 +676,7 @@
         v_at = pl.ds(pl.multiple_of(base + 2 * fourth, 128), 128)
         here = pl.ds(pl.multiple_of(p * 128, 128), 128)
         q2, k2, v2 = proj[:, q_at], proj[:, k_at], proj[:, v_at]
-        found = []
+        found, logs = [], []
         for i in range(2):
             scores = dot(q2 * keep[i], k2, NT) * factor
             scores = jnp.where(mask[...] > 0, scores, NEGATIVE)
@@ -673,7 +685,10 @@
             total = jnp.sum(exponent, axis=1, keepdims=True)
             prob = (exponent * (1.0 / total)).astype(low)
             found.append(dot(prob, v2))
-            lse[...] = jnp.where(lane_wide == 2 * p + i, peak + jnp.log(total), lse[...])
+            logs.append(peak + jnp.log(total))
+        spread_logs = jnp.where(lane_wide == 2 * p, logs[0], logs[1])
+        at_pair = lax.div(lane_wide, 2) == p
+        lse[...] = jnp.where(at_pair, spread_logs, lse[...])
         both = jnp.where(is_low, *found)
         att[:, here] = both
         scaled[:, here] = (both * vec[10:11, here]).astype(low)
@@ -682,7 +697,7 @@
     lax.fori_loop(0, 1, attend, 0)
     for k in range(2, nz):
         wait_all(a1[k])
-        b1.append(second(qkv_all, slots[k], 1))
+        b1.append(second(qkv_all, qkv_slots[k], 1))
     out_a = [first(out_all, z)]
     for k in range(1, nz):
         out_z[k - 1].wait_recv()
@@ -692,11 +707,11 @@
     c1 = []
     for k in range(2):
         wait_all(b1[k])
-        c1.append(third(qkv_all, slots[k], 1))
+        c1.append(third(qkv_all, qkv_slots[k], 1))
     lax.fori_loop(2, 4, attend, 0)
     for k in range(2, nz):
         wait_all(b1[k])
-        c1.append(third(qkv_all, slots[k], 1))
+        c1.append(third(qkv_all, qkv_slots[k], 1))
     wait_all(c1)
     saves = [fetch(qkv_all, qkv_out), fetch(vec, vec_out), fetch(nin, nin_out)]
     project(1)
@@ -705,9 +720,9 @@
     for k in range(nz):
         wait_all(out_a[k])
         out_b.append(second(out_all, slots[k]))
-    lax.fori_loop(4, 6, attend, 0)
+    lax.fori_loop(4, 6, attend, 0, unroll=True)
     og.after_first()
-    lax.fori_loop(6, 8, attend, 0)
+    lax.fori_loop(6, 8, attend, 0, unroll=True)
     out_c = []
     for k in range(nz):
         wait_all(out_b[k])
@@ -729,11 +744,12 @@
         mid_all[y, x, c, part] = (centered(value)[0] * vec[2:3] + vec[8:9]).astype(low)
         return carry
 
-    lax.fori_loop(0, rows // step, middles, 0)
+    lax.fori_loop(0, rows // step, middles, 0, unroll=2)
     mid = Plane(sends, mid_all, (y, x, c), (to_x, to_y, to_c))
     mid.start_first(mid_all.at[y, x, c])
     mid.start_second(mid_all.at[y, x, c])
-    saves += [fetch(branch, branch_out), fetch(middle, middle_out)]
+    branch_put = fetch(branch, branch_out)
+    saves.append(fetch(middle, middle_out))
 
     def grads(yy, xx, cc):
         grad[yy, xx, cc] = dot(og_all[yy, xx, cc], fc2_all[...], NT)
@@ -786,20 +802,20 @@
     grads(y, 1 - x, 1 - c)
     grads(1 - y, x, 1 - c)
     grads(1 - y, 1 - x, c)
-    og.last.wait_recv()
+    wait_all(og.last)
     grads(1 - y, 1 - x, 1 - c)
     wait_all(fc1_z)
     forward(y, x, c)
     wait_all(mid.core)
     forward(y, x, 1 - c)
-    mid.after_third()
     forward(y, 1 - x, c)
     forward(1 - y, x, c)
     wait_all(mid.side)
     forward(y, 1 - x, 1 - c)
     forward(1 - y, x, 1 - c)
+    mid.after_third()
     forward(1 - y, 1 - x, c)
-    mid.last.wait_recv()
+    wait_all(mid.last)
     forward(1 - y, 1 - x, 1 - c)
 
     sends.start(stats, got.at[3], to_c).wait_recv()
@@ -920,6 +936,9 @@
         cores[k].wait_recv()
         f_sums[yy, xx] = (block + f_core[yy, xx].astype(f32)).astype(low)
     saves.append(fetch(f_sums, ffn_out))
+    top = pl.ds(0, first_out.shape[1])
+    out_x = sends.start(f_sums.at[:, 1 - x, top, left], first_out.at[:, :, left], to_x)
+    out_y = sends.start(f_sums.at[1 - y, :, top, right], first_out.at[:, :, right], to_y)
 
     def fc2_block(k, carry):
         part = pl.ds(pl.multiple_of(k * size, 128), size)
@@ -932,16 +951,19 @@
 
     lax.fori_loop(0, blocks, fc2_block, 0)
     saves.append(fetch(fc2_part, fc2_out))
+    branch_put.wait()
     wait_all((stage_x[1], stage_y[1], last_x, last_y))
     for cols, k in ((left, y), (right, x)):
-        gnm_out[:, cols] = (
+        branch[:, cols] = (
             sums[y, x, :, cols].astype(f32)
             + from_one[k, :, cols].astype(f32)
             + from_two[:, cols].astype(f32)
         )
+        saves.append(fetch(branch.at[:, cols], gnm_out.at[:, cols]))
     for k in range(nz - 1):
         fc1_far[k].wait_recv()
         fc1_out[:, soon] += fc1_got[k].astype(f32)
+    wait_all((out_x, out_y))
     for copy in saves:
         copy.wait()
     sends.finish()
@@ -966,10 +988,11 @@
         ((rows, width), low),
         ((rows, width), low),
         ((2, 2, rows, width), low),
+        ((2, rows // 4, width), low),
         ((units, width), low),
-        ((width, units // 2), low),
+        ((width, units - 3 * units // 4), low),
+        ((rows, width), f32),
         (fc1.shape, f32),
-        ((rows, width), f32),
         ((8, units), f32),
     )
     return pl.pallas_call(
@@ -977,7 +1000,7 @@
         name="fore",
         out_shape=tuple(sds(shape, kind) for shape, kind in shapes),
         in_specs=[ANY] * 4 + [IN_VMEM] * 2 + [ANY] * 2 + [IN_VMEM] * 2 + [smem] * 2,
-        out_specs=[ANY] * 13 + [IN_VMEM] * 3,
+        out_specs=[ANY] * 15 + [IN_VMEM] * 2,
         scratch_shapes=[
             vm(every + w_qkv.shape, low),
             vm(every + w_out.shape, low),
@@ -1017,11 +1040,11 @@
             vm((2, 2, rows, width), low),
             vm((2, 2, rows, width), low),
             vm((2, 2, rows, width), low),
-            vm((nz - 1, fc1.shape[0], units // 2), low),
-            vm((width, units // 2), low),
+            vm((nz - 1, fc1.shape[0], 3 * units // 4), low),
+            vm((width, units - 3 * units // 4), low),
             vm((units, width), low),
-            vm((nz - 1, fc1.shape[0], units // 2), low),
-            pltpu.SemaphoreType.DMA((36,)),
+            vm((nz - 1, fc1.shape[0], 3 * units // 4), low),
+            pltpu.SemaphoreType.DMA((40,)),
             pltpu.SemaphoreType.DMA((count,)),
             pltpu.SemaphoreType.DMA((count,)),
         ],
@@ -1035,6 +1058,7 @@
     nz,
     gnm_in,
     ffn_ref,
+    first_in,
     late_ref,
     own1_in,
     fc2_ref,
@@ -1124,6 +1148,11 @@
     gnm_got = fetch(gnm_in, gnm_ref)
     og_got = fetch(og_in, og_ref)
     branch_got = fetch(branch_in, branch_ref)
+    top, half = pl.ds(0, first_in.shape[1]), first_in.shape[2] // 2
+    first_got = [
+        fetch(first_in.at[:, :, pl.ds(i * half, half)], f_one.at[i, :, top, pl.ds(i * half, half)])
+        for i in range(2)
+    ]
     ffn_got = fetch(ffn_ref, f_sums)
     out_got = fetch(out_in, out_ref)
     att_got = fetch(att_in, att_ref)
@@ -1142,7 +1171,7 @@
     share = weight_out.shape[0]
     width1, width2 = fc1_out.shape[0], fc2_out.shape[1]
 
-    pieces = 2
+    pieces = 4
     parts = [pl.ds(k * (rows // pieces), rows // pieces) for k in range(pieces)]
     left, right = pl.ds(0, width // 2), pl.ds(width // 2, width // 2)
     def block1(which):
@@ -1174,8 +1203,11 @@
         part = parts[k]
         if k == 0:
             ffn_got.wait()
-        for copy in f_first[k]:
-            copy.wait_recv()
+            for copy in first_got:
+                copy.wait()
+        else:
+            for copy in f_first[k - 1]:
+                copy.wait_recv()
         f_sums[1 - y, x, part, left] = add_low(
             f_sums[1 - y, x, part, left], f_one[0, 1 - y, part, left]
         )
@@ -1285,7 +1317,8 @@
         for spot in spots:
             puts.append(fetch(weight_at.at[:, spot], weight_out.at[:, spot]))
 
-    ffn_one(0)
+    ffn_one(1)
+    ffn_two(0)
     accs[...] = jnp.zeros_like(accs)
     step = 32
 
@@ -1477,13 +1510,15 @@
         lax.fori_loop(0, rows // step, tokens_back, 0)
         puts.append(fetch(gmid, token_out))
 
+    ffn_one(2)
     pairs(0, 1)
     w_step1(0)
     pairs(1, 2)
     wgrad(1)
-    ffn_two(0)
+    ffn_two(1)
     pairs(2, 3)
     w_step1(1)
+    ffn_two(2)
     pairs(3, 4)
     wgrad(2)
     w_step2(0)
@@ -1505,22 +1540,24 @@
     small_start()
     w_step2(3)
     w_step3(2)
-    ffn_one(1)
     small_second()
     w_step2(4)
+    ffn_one(3)
     w_step3(3)
+    small_third()
     ffn_three(0)
-    small_third()
+    ffn_three(1)
+    ffn_three(2)
     w_step4(0)
+    w_step3(4)
+    ffn_two(3)
+    small_fourth()
+    small_last()
     w_step4(1)
-    small_fourth()
-    ffn_two(1)
-    w_step3(4)
     w_step4(2)
-    small_last()
+    w_step4(3)
     far_last()
-    w_step4(3)
-    ffn_three(1)
+    ffn_three(3)
     w_step4(4)
     for put in puts:
         put.wait()
@@ -1528,16 +1565,16 @@
 
 
 def back(nz, *operands):
-    gnm, ffn_part, late, fc1, fc2, unit, proj, att, lse, branch, middle = operands[:11]
-    scaled, nin, qkv, out, vec = operands[11:16]
+    gnm, ffn_part, ffn_first, late, fc1, fc2, unit, proj, att, lse, branch = operands[:11]
+    middle, scaled, nin, qkv, out, vec = operands[11:17]
     rows, width = middle.shape
     share = width // (nz * 8)
     columns = proj.shape[1] + width
     low, f32 = jnp.bfloat16, jnp.float32
     sds = jax.ShapeDtypeStruct
     fc2_own = (fc2.shape[0], fc2.shape[1] // nz)
-    count = 64 + 8 * nz
-    specs = [ANY] * 5 + [IN_VMEM] + [ANY] * 9 + [IN_VMEM] + [ANY] * 2
+    count = 96 + 8 * nz
+    specs = [ANY] * 6 + [IN_VMEM] + [ANY] * 9 + [IN_VMEM] + [ANY] * 2
     specs.append(pl.BlockSpec(memory_space=pltpu.SMEM))
     return pl.pallas_call(
         functools.partial(back_kernel, nz),
@@ -1598,7 +1635,7 @@
             pltpu.VMEM(out.shape, low),
             pltpu.VMEM((rows, width), low),
             pltpu.VMEM((rows, width), low),
-            pltpu.SemaphoreType.DMA((48,)),
+            pltpu.SemaphoreType.DMA((64,)),
             pltpu.SemaphoreType.DMA((count,)),
             pltpu.SemaphoreType.DMA((count,)),
         ],
@@ -1734,10 +1771,11 @@
         nin,
         scaled,
         ffn_part,
+        ffn_first,
         fc2_part,
         fc1_late,
+        gnm,
         fc1_own,
-        gnm,
         unit_sums,
     ) = fore(
         nz,
@@ -1769,6 +1807,7 @@
         nz,
         gnm,
         ffn_part,
+        ffn_first,
         fc1_late,
         fc1_own,
         fc2_part,

time: 191 us -> 189 us (0.990)
  Pallas kernels: 190 us -> 188 us
where the time goes in v7:
time: 189 us
  Pallas kernels  188 us (99%)
    pallas_call x1, Pallas kernels, fore(): pl.pallas_call(functools.partial(fore_kernel, nz), name='fore', out_shape...  118 us
    pallas_call x1, Pallas kernels, back(): pl.pallas_call(functools.partial(back_kernel, nz), name='back', out_shape...  65.6 us
    pallas_call x1, Pallas kernels, finish(): pl.pallas_call(finish_kernel, name='finish', out_shape=tuple((jax.ShapeDt...  4.32 us

profile of v7, /device:TPU:0, one launch (start us, length us, event | category | flops | bytes accessed | tf_op | source)
XLA Modules:
  0.0 188.9 jit_solution(17310870686077704161)
XLA Ops:
  0.6 118.1 %fore.1 = (bf16[4,2,2,2,32,3072]{5,4,3,2,1,0:T(8,128)(2,1)}, bf16[4,2,2,2,32,1024]{5,4,3,2,1,0:T(8,128)(2,1)}, f32[16,1024]{1,0:T(8,128)}, bf16[256,3072]{1,0:T(...) custom-call(bf16[256,1024]{1,0:T(8,128)(2,1)} %tok_in.1, ...), custom_call_target="tpu_custom_call" | custom-call | tf_op jit(solution)/shard_map/fore/pallas_call | solution.py:998
  118.7 65.6 %back.1 = (bf16[256,1024]{1,0:T(8,128)(2,1)}, f32[256,1024]{1,0:T(8,128)}, f32[32,4096]{1,0:T(8,128)}, f32[3,32]{1,0:T(4,128)}, f32[7,32]{1,0:T(8,128)}, /*index...) custom-call(f32[256,1024]{1,0:T(8,128)} %get-tuple-element.48.gnm_in, ...), custom_call_target="tpu_custom_call" | custom-call | tf_op jit(solution)/shard_map/back/pallas_call | solution.py:1579
  184.4 4.3 %finish.1 = (bf16[256,1024]{1,0:T(8,128)(2,1)}, f32[256,1024]{1,0:T(8,128)}, f32[32,3072]{1,0:T(8,128)}, f32[32,1024]{1,0:T(8,128)}, f32[256,512]{1,0:T(8,128)},...) custom-call(bf16[256,1024]{1,0:T(8,128)(2,1)} %get-tuple-element.65., ...), custom_call_target="tpu_custom_call" | custom-call | tf_op jit(solution)/shard_map/finish/pallas_call | solution.py:1728

commit v8 on v7

--- a/solution.py
+++ b/solution.py
@@ -1343,8 +1343,18 @@
     for copy in (middle_got, gnm_got, og_got, branch_got):
         copy.wait()
     lax.fori_loop(0, rows // step, norms, 0)
+    quarter = width // 4
+
+    def out_block(k, carry):
+        part = pl.ds(pl.multiple_of(k * (width // nz), width // nz), width // nz)
+        block = dot(scaled_ref[:, part], gpost[...], TN).astype(low)
+        w_part[k, :, :, :, :, pl.ds(0, width)] = block.reshape(2, 2, 2, share, width)
+        return carry
+
+    scaled_got.wait()
+    lax.fori_loop(0, nz, out_block, 0)
+    w_zero(0)
     mask[...] = doc_mask(doc_ref, rows)
-    quarter = width // 4
 
     def scaled_block(k, carry):
         part = pl.ds(pl.multiple_of(k * quarter, quarter), quarter)
@@ -1357,15 +1367,6 @@
     att_got.wait()
     lax.fori_loop(0, 4, scaled_block, 0)
 
-    def out_block(k, carry):
-        part = pl.ds(pl.multiple_of(k * (width // nz), width // nz), width // nz)
-        block = dot(scaled_ref[:, part], gpost[...], TN).astype(low)
-        w_part[k, :, :, :, :, pl.ds(0, width)] = block.reshape(2, 2, 2, share, width)
-        return carry
-
-    scaled_got.wait()
-    lax.fori_loop(0, nz, out_block, 0)
-    w_zero(0)
     nin_got.wait()
     nin_t[...] = nin_ref[...].T
     proj_got.wait()
@@ -1511,8 +1512,8 @@
         puts.append(fetch(gmid, token_out))
 
     ffn_one(2)
+    w_step1(0)
     pairs(0, 1)
-    w_step1(0)
     pairs(1, 2)
     wgrad(1)
     ffn_two(1)

time: 189 us -> 188 us (level)
  no operation moved by 1% of the time
where the time goes in v8:
time: 188 us
  Pallas kernels  187 us (99%)
    pallas_call x1, Pallas kernels, fore(): pl.pallas_call(functools.partial(fore_kernel, nz), name='fore', out_shape...  118 us
    pallas_call x1, Pallas kernels, back(): pl.pallas_call(functools.partial(back_kernel, nz), name='back', out_shape...  64.8 us
    pallas_call x1, Pallas kernels, finish(): pl.pallas_call(finish_kernel, name='finish', out_shape=tuple((jax.ShapeDt...  4.32 us

profile of v8, /device:TPU:0, one launch (start us, length us, event | category | flops | bytes accessed | tf_op | source)
XLA Modules:
  0.0 188.1 jit_solution(1344369464181152747)
XLA Ops:
  0.6 118.1 %fore.1 = (bf16[4,2,2,2,32,3072]{5,4,3,2,1,0:T(8,128)(2,1)}, bf16[4,2,2,2,32,1024]{5,4,3,2,1,0:T(8,128)(2,1)}, f32[16,1024]{1,0:T(8,128)}, bf16[256,3072]{1,0:T(...) custom-call(bf16[256,1024]{1,0:T(8,128)(2,1)} %tok_in.1, ...), custom_call_target="tpu_custom_call" | custom-call | tf_op jit(solution)/shard_map/fore/pallas_call | solution.py:998
  118.7 64.8 %back.1 = (bf16[256,1024]{1,0:T(8,128)(2,1)}, f32[256,1024]{1,0:T(8,128)}, f32[32,4096]{1,0:T(8,128)}, f32[3,32]{1,0:T(4,128)}, f32[7,32]{1,0:T(8,128)}, /*index...) custom-call(f32[256,1024]{1,0:T(8,128)} %get-tuple-element.48.gnm_in, ...), custom_call_target="tpu_custom_call" | custom-call | tf_op jit(solution)/shard_map/back/pallas_call | solution.py:1580
  183.6 4.3 %finish.1 = (bf16[256,1024]{1,0:T(8,128)(2,1)}, f32[256,1024]{1,0:T(8,128)}, f32[32,3072]{1,0:T(8,128)}, f32[32,1024]{1,0:T(8,128)}, f32[256,512]{1,0:T(8,128)},...) custom-call(bf16[256,1024]{1,0:T(8,128)(2,1)} %get-tuple-element.65., ...), custom_call_target="tpu_custom_call" | custom-call | tf_op jit(solution)/shard_map/finish/pallas_call | solution.py:1729

commit v9 on v8

--- a/solution.py
+++ b/solution.py
@@ -451,6 +451,8 @@
     qkv_all,
     out_all,
     vec_all,
+    vec_plane,
+    vec_pair,
     vec_mine,
     vec_turn,
     unit_ref,
@@ -519,10 +521,13 @@
         for i in range(3)
     ]
     vec_turn[...] = jnp.zeros_like(vec_turn)
-    share = vec_mine.shape[0]
+    share = qkv_ref.shape[0]
     vec_turn[0:3, 0:share] = gains_ref[...]
     vec_turn[3:10, 0:share] = biases_ref[...]
-    vec_mine[...] = vec_turn[...].T[:share]
+    across = vec_turn[...].T[:share]
+    vec_turn[...] = jnp.zeros_like(vec_turn)
+    vec_turn[pl.ds(pl.multiple_of((2 * x + c) * share, share), share)] = across
+    vec_mine[...] = vec_turn[...].T[:16]
     greet([to_x, to_y, to_c, to_xy] + peers)
     sends = Sends(send_sems, recv_sems)
     low, f32 = jnp.bfloat16, jnp.float32
@@ -534,7 +539,7 @@
         for copy in copies:
             copy.wait_recv()
 
-    vec_z = [sends.start(vec_mine, vec_all.at[z, y, x, c], peer) for peer in peers]
+    vec_z = [sends.start(vec_mine, vec_all.at[0, z], peer) for peer in peers]
     phase = 6 * fourth
     spans = (pl.ds(0, phase), pl.ds(phase, phase))
     for copy in qkv_in:
@@ -578,7 +583,7 @@
     fc1_in = fetch(fc1_ref, own1)
     fc2_in = fetch(fc2_ref, own2)
     og_in = fetch(og_ref, og_all.at[y, x, c])
-    vec_all[z, y, x, c] = vec_mine[...]
+    vec_all[0, z] = vec_mine[...]
     unit_ref[...] = jnp.zeros_like(unit_ref)
     unit_ref[0:1] = shift_ref[0:1]
     unit_ref[1:2] = gain_ref[...]
@@ -594,8 +599,7 @@
 
     lax.fori_loop(0, rows // step, normed, 0)
     wait_all(vec_z)
-    by_x = vec_all.at[:, y, x, c]
-    vec_x = sends.start(by_x, by_x, to_x)
+    vec_x = sends.start(vec_all.at[0], vec_all.at[1], to_x)
     wait_all(a0[0])
     b0 = [second(qkv_all, z, 0)]
     wait_all(a1[0])
@@ -603,21 +607,21 @@
     go_on(0)
     a0.append(first(qkv_all, qkv_slots[1], 0))
     vec_x.wait_recv()
-    by_y = vec_all.at[:, y, :, c]
-    vec_y = sends.start(by_y, by_y, to_y)
+    vec_plane[y] = vec_all[0] + vec_all[1]
+    vec_y = sends.start(vec_plane.at[y], vec_plane.at[y], to_y)
     for k in range(2, nz):
         qkv_z[0][k - 1].wait_recv()
         a0.append(first(qkv_all, qkv_slots[k], 0))
     vec_y.wait_recv()
-    by_c = vec_all.at[:, :, :, c]
-    vec_c = sends.start(by_c, by_c, to_c)
+    vec_c = sends.start(vec_plane, vec_pair, to_c)
     for k in range(1, nz):
         wait_all(a0[k])
         b0.append(second(qkv_all, qkv_slots[k], 0))
     go_on(1)
     a1.append(first(qkv_all, qkv_slots[1], 1))
     vec_c.wait_recv()
-    vec[...] = vec_all[...].reshape(width, 128).T[:16]
+    for n in range(2 * nz):
+        vec[:, n * 128 : (n + 1) * 128] = vec_plane[n % 2, n // 2] + vec_pair[n % 2, n // 2]
     spot = lax.broadcasted_iota(jnp.int32, (1, width), 1)
     head = 64
     wide = jnp.zeros((1, width), f32)
@@ -1004,8 +1008,10 @@
         scratch_shapes=[
             vm(every + w_qkv.shape, low),
             vm(every + w_out.shape, low),
-            vm(every + (share, 128), f32),
-            vm((share, 128), f32),
+            vm((2, nz, 16, 128), f32),
+            vm((2, nz, 16, 128), f32),
+            vm((2, nz, 16, 128), f32),
+            vm((16, 128), f32),
             vm((128, 128), f32),
             vm((8, units), f32),
             vm((width, units), low),

time: 188 us -> 187 us (level)
  Pallas kernels: 187 us -> 185 us
    pallas_call x1, Pallas kernels: 118 us -> 116 us  [fore(): pl.pallas_call(functools.partial(fore_kernel, nz), name='fore', out_shape...]
where the time goes in v9:
time: 187 us; the launch traced here: 186 us
  Pallas kernels  185 us (99%)
    pallas_call x1, Pallas kernels, fore(): pl.pallas_call(functools.partial(fore_kernel, nz), name='fore', out_shape...  116 us
    pallas_call x1, Pallas kernels, back(): pl.pallas_call(functools.partial(back_kernel, nz), name='back', out_shape...  65.1 us
    pallas_call x1, Pallas kernels, finish(): pl.pallas_call(finish_kernel, name='finish', out_shape=tuple((jax.ShapeDt...  4.32 us

profile of v9, /device:TPU:0, one launch (start us, length us, event | category | flops | bytes accessed | tf_op | source)
XLA Modules:
  0.0 186.1 jit_solution(4561762964881582773)
XLA Ops:
  0.6 115.9 %fore.1 = (bf16[4,2,2,2,32,3072]{5,4,3,2,1,0:T(8,128)(2,1)}, bf16[4,2,2,2,32,1024]{5,4,3,2,1,0:T(8,128)(2,1)}, f32[16,1024]{1,0:T(8,128)}, bf16[256,3072]{1,0:T(...) custom-call(bf16[256,1024]{1,0:T(8,128)(2,1)} %tok_in.1, ...), custom_call_target="tpu_custom_call" | custom-call | tf_op jit(solution)/shard_map/fore/pallas_call | solution.py:1002
  116.5 65.1 %back.1 = (bf16[256,1024]{1,0:T(8,128)(2,1)}, f32[256,1024]{1,0:T(8,128)}, f32[32,4096]{1,0:T(8,128)}, f32[3,32]{1,0:T(4,128)}, f32[7,32]{1,0:T(8,128)}, /*index...) custom-call(f32[256,1024]{1,0:T(8,128)} %get-tuple-element.48.gnm_in, ...), custom_call_target="tpu_custom_call" | custom-call | tf_op jit(solution)/shard_map/back/pallas_call | solution.py:1586
  181.6 4.3 %finish.1 = (bf16[256,1024]{1,0:T(8,128)(2,1)}, f32[256,1024]{1,0:T(8,128)}, f32[32,3072]{1,0:T(8,128)}, f32[32,1024]{1,0:T(8,128)}, f32[256,512]{1,0:T(8,128)},...) custom-call(bf16[256,1024]{1,0:T(8,128)(2,1)} %get-tuple-element.65., ...), custom_call_target="tpu_custom_call" | custom-call | tf_op jit(solution)/shard_map/finish/pallas_call | solution.py:1735

commit v10 on v9

--- a/solution.py
+++ b/solution.py
@@ -1348,7 +1348,7 @@
 
     for copy in (middle_got, gnm_got, og_got, branch_got):
         copy.wait()
-    lax.fori_loop(0, rows // step, norms, 0)
+    lax.fori_loop(0, rows // step, norms, 0, unroll=2)
     quarter = width // 4
 
     def out_block(k, carry):

time: 187 us -> 186 us (level)
  no operation moved by 1% of the time
where the time goes in v10:
time: 186 us; the launch traced here: 185 us
  Pallas kernels  185 us (99%)
    pallas_call x1, Pallas kernels, fore(): pl.pallas_call(functools.partial(fore_kernel, nz), name='fore', out_shape...  116 us
    pallas_call x1, Pallas kernels, back(): pl.pallas_call(functools.partial(back_kernel, nz), name='back', out_shape...  64.3 us
    pallas_call x1, Pallas kernels, finish(): pl.pallas_call(finish_kernel, name='finish', out_shape=tuple((jax.ShapeDt...  4.32 us

profile of v10, /device:TPU:0, one launch (start us, length us, event | category | flops | bytes accessed | tf_op | source)
XLA Modules:
  0.0 185.4 jit_solution(14703181939623858452)
XLA Ops:
  0.6 115.9 %fore.1 = (bf16[4,2,2,2,32,3072]{5,4,3,2,1,0:T(8,128)(2,1)}, bf16[4,2,2,2,32,1024]{5,4,3,2,1,0:T(8,128)(2,1)}, f32[16,1024]{1,0:T(8,128)}, bf16[256,3072]{1,0:T(...) custom-call(bf16[256,1024]{1,0:T(8,128)(2,1)} %tok_in.1, ...), custom_call_target="tpu_custom_call" | custom-call | tf_op jit(solution)/shard_map/fore/pallas_call | solution.py:1002
  116.5 64.3 %back.1 = (bf16[256,1024]{1,0:T(8,128)(2,1)}, f32[256,1024]{1,0:T(8,128)}, f32[32,4096]{1,0:T(8,128)}, f32[3,32]{1,0:T(4,128)}, f32[7,32]{1,0:T(8,128)}, /*index...) custom-call(f32[256,1024]{1,0:T(8,128)} %get-tuple-element.48.gnm_in, ...), custom_call_target="tpu_custom_call" | custom-call | tf_op jit(solution)/shard_map/back/pallas_call | solution.py:1586
  180.9 4.3 %finish.1 = (bf16[256,1024]{1,0:T(8,128)(2,1)}, f32[256,1024]{1,0:T(8,128)}, f32[32,3072]{1,0:T(8,128)}, f32[32,1024]{1,0:T(8,128)}, f32[256,512]{1,0:T(8,128)},...) custom-call(bf16[256,1024]{1,0:T(8,128)(2,1)} %get-tuple-element.65., ...), custom_call_target="tpu_custom_call" | custom-call | tf_op jit(solution)/shard_map/finish/pallas_call | solution.py:1735
